TPU v7x, 512 devices: a whole 4x4x16 slice. The times are simulated.
512 devices in a mesh: lsec: 8 (over x, core), rsec: 8 (over z_lo), ops: 8 (over y, z_hi).
Axes of the slice: x: 4, y: 4, z: 16 (z_hi: 2, z_lo: 8; z = z_hi * 8 + z_lo), core: 2. Of those that a mesh axis runs over, the one named last changes fastest.
Arguments:
- psi: bfloat16 [64, 64, 128, 128], P(('lsec', 'rsec')), may hold values from -6 to 6
- left_ops: bfloat16 [16, 64, 128, 128], P('ops', ('lsec', 'rsec')), may hold values from -0.5 to 0.5
- right_ops: bfloat16 [16, 64, 128, 128], P('ops', ('lsec', 'rsec')), may hold values from -0.125 to 0.125
- left_order: int32 [64], replicated, may hold values from 0 to 63, each once
- right_order: int32 [64], replicated, may hold values from 0 to 63, each once
- left_qn: int32 [64], replicated, may hold values from 0 to 2
- right_qn: int32 [64], replicated, may hold values from 0 to 2
- left_dims: int32 [64], replicated, may hold values from 96 to 128
- right_dims: int32 [64], replicated, may hold values from 96 to 128
Outputs:
- first_sigma: bfloat16 [64, 64, 128, 128], P(('lsec', 'rsec'))
- second_sigma: bfloat16 [64, 64, 128, 128], P(('lsec', 'rsec'), 'ops')
Inputs may be any that keep to these rules, and one draw needn't show every extreme that they name: left_order holds each left sector once. right_order holds each right sector once.
All inputs are finite; a program needn't handle non-finite values.
Results may differ from a plain program's by a relative error of at most 0.025.
Values may be sent and summed in bfloat16 or wider, within the bound.
No kernel may reach another device: no remote copies, remote signals or barrier semaphores. Data moves between devices by JAX's collectives and lax.ppermute only.
A program may use at most 64 MiB of HBM per device.

v0:
```python
import jax
import jax.numpy as jnp
from jax import lax
from jax.sharding import PartitionSpec as P

SPREAD = 1


def relayout(blocks):
    return lax.all_to_all(blocks, ("lsec", "rsec"), split_axis=1, concat_axis=1, tiled=True)


def inverse(order):
    count = order.shape[0]
    return jnp.zeros((count,), jnp.int32).at[order].set(jnp.arange(count, dtype=jnp.int32))


def on_device(
    psi, left_ops, right_ops, left_order, right_order, left_qn, right_qn, left_dims, right_dims
):
    slot = lax.axis_index(("lsec", "rsec"))
    width = psi.shape[-1]
    line = jnp.arange(width, dtype=jnp.int32)
    left_sector = left_order[slot]
    right_sector = right_order[slot]
    inv_left = inverse(left_order)
    inv_right = inverse(right_order)
    left_here = left_ops[:, 0]
    right_here = right_ops[:, 0]
    allowed_row = jnp.abs(left_qn[left_sector] - right_qn) <= SPREAD
    row_used = line < left_dims[left_sector]
    col_used = line[None, :] < right_dims[:, None]
    mask_left = allowed_row[:, None, None] & row_used[None, :, None] & col_used[:, None, :]
    allowed_col = jnp.abs(left_qn - right_qn[right_sector]) <= SPREAD
    rows_used = line[None, :] < left_dims[:, None]
    cols_here = line < right_dims[right_sector]
    mask_right = allowed_col[:, None, None] & rows_used[:, :, None] & cols_here[None, None, :]
    start = jnp.where(mask_left, psi[0], jnp.zeros((), jnp.bfloat16))
    start_slots = start[right_order]
    lefted = jnp.einsum(
        "kxy,byz->kbxz", left_here, start_slots, preferred_element_type=jnp.float32
    ).astype(jnp.bfloat16)
    arrived = relayout(lefted)
    partial_value = jnp.einsum(
        "kixy,kzy->ixz", arrived, right_here, preferred_element_type=jnp.float32
    )
    partial_value = partial_value[inv_left]
    summed = lax.psum(partial_value.astype(jnp.bfloat16), "ops").astype(jnp.float32)
    first = jnp.where(mask_right, summed, 0.0).astype(jnp.bfloat16)
    first_slots = first[left_order]
    righted = jnp.einsum(
        "ixy,kzy->kixz", first_slots, right_here, preferred_element_type=jnp.float32
    ).astype(jnp.bfloat16)
    returned = relayout(righted)
    second_partial = jnp.einsum(
        "kxy,kjyz->jxz", left_here, returned, preferred_element_type=jnp.float32
    )
    second_partial = second_partial[inv_right]
    second_share = lax.psum_scatter(
        second_partial.astype(jnp.bfloat16), "ops", scatter_dimension=0, tiled=True
    ).astype(jnp.float32)
    count = second_share.shape[0]
    mask_second = lax.dynamic_slice_in_dim(mask_left, lax.axis_index("ops") * count, count, 0)
    second = jnp.where(mask_second, second_share, 0.0).astype(jnp.bfloat16)
    return (first[None], second[None])


def solution(mesh):
    placed = (
        P(("lsec", "rsec"), None, None, None),
        P("ops", ("lsec", "rsec"), None, None),
        P("ops", ("lsec", "rsec"), None, None),
        P(),
        P(),
        P(),
        P(),
        P(),
        P(),
    )
    return jax.shard_map(
        on_device,
        mesh=mesh,
        in_specs=placed,
        out_specs=(P(("lsec", "rsec"), None, None, None), P(("lsec", "rsec"), "ops", None, None)),
        check_vma=False,
    )
```

profile of v0, /device:TPU:1, one launch (start us, length us, event | category | flops | bytes accessed | tf_op | source)
XLA Modules:
  0.0 965.1 jit_solution(14850977967399252839)
XLA Ops:
  7.2 0.0 copy-start
  7.2 1.3 dynamic_slice.24
  9.8 0.0 copy-start.4
  9.8 0.0 copy-start.8
  9.8 0.0 copy-start.6
  9.8 0.0 copy-start.7
  9.8 0.0 copy-start.3
  9.8 3.2 copy.11
  13.7 0.0 copy-done.4
  13.7 0.6 dynamic_slice.26
  14.3 0.6 iota_compare_fusion.2
  15.0 0.6 dynamic_slice.25
  15.6 0.7 abs_compare_fusion
  16.3 0.1 iota_compare_fusion
  16.3 2.6 bitcast_select_fusion
  19.0 2.6 gather_fusion
  21.6 3.2 convert_bitcast_fusion.1
  24.8 17.4 %all-to-all-start = ((bf16[2,64,128,128]{3,2,0,1:T(8,128)(2,1)}), bf16[2,64,128,128]{3,2,0,1:T(8,128)(2,1)}, u32[]{:S(2)}, u32[]{:S(2)}) async-start(bf16[2,64,128,128]{3,2,0,1:T(8,128)(2,1)} %convert_bitcast_fusion.1), calls=%async_computation | async-start | bytes 8388608 | tf_op jit(solution)/shard_map/all_to_all | solution.py:10
  42.2 0.0 all-reduce.2.cloned.1.call-start
  42.2 0.0 copy-done.5
  42.3 0.8 scatter_custom_fusion
  43.1 186.0 %all-to-all-done = bf16[2,64,128,128]{3,2,0,1:T(8,128)(2,1)} async-done(((bf16[2,64,128,128]{3,2,0,1:T(8,128)(2,1)}), bf16[2,64,128,128]{3,2,0,1:T(8,128)(2,1)}, u32[]{:S(2)}, u32[]{:S(2)}) %all-to-all-start) | async-done | bytes 4194336 | tf_op jit(solution)/shard_map/all_to_all | solution.py:10
  229.0 3.4 convolution_bitcast_fusion.1
  232.5 2.1 gather_fusion.1
  234.6 0.0 all-reduce.2.cloned.1.call-update
  234.6 0.6 dynamic_slice.21
  237.2 0.6 dynamic_slice.23
  237.8 0.6 dynamic_slice.22
  238.4 0.6 iota_compare_fusion.3
  239.0 0.6 abs_compare_fusion.1
  239.7 0.1 fusion.7
  239.8 363.0 %all-reduce.2.cloned.1.call-done = bf16[64,128,128]{2,1,0:T(8,128)(2,1)} async-done(((bf16[64,128,128]{2,1,0:T(8,128)(2,1)}), bf16[64,128,128]{2,1,0:T(8,128)(2,1)}) %all-reduce.2.cloned.1.call-update) | async-done | bytes 2097168 | tf_op jit(solution)/shard_map/psum | solution.py:48
  602.8 4.4 select_convert_fusion
  607.2 2.5 gather_fusion.2
  609.7 3.2 convert_bitcast_fusion
  612.9 8.0 all-to-all-start.1
  621.0 0.0 reduce-scatter.2.cloned.1.call-start
  621.0 0.8 scatter_custom_fusion.1
  621.8 186.0 %all-to-all-done.1 = bf16[2,64,128,128]{2,3,0,1:T(8,128)(2,1)} async-done(((bf16[2,64,128,128]{2,3,0,1:T(8,128)(2,1)}), bf16[2,64,128,128]{2,3,0,1:T(8,128)(2,1)}, u32[]{:S(2)}, u32[]{:S(2)}) %all-to-all-start.1) | async-done | bytes 4194336 | tf_op jit(solution)/shard_map/all_to_all | solution.py:10
  807.8 3.4 convolution_bitcast_fusion
  811.2 2.2 gather_fusion.3
  813.4 0.0 reduce-scatter.2.cloned.1.call-update
  813.4 1.4 broadcast_and_fusion
  814.9 0.1 copy-done.1
  815.0 2.6 fusion.14
  817.6 138.8 %reduce-scatter.2.cloned.1.call-done = bf16[8,128,128]{1,2,0:T(8,128)(2,1)} async-done(((bf16[64,128,128]{1,2,0:T(8,128)(2,1)}), bf16[8,128,128]{1,2,0:T(8,128)(2,1)}) %reduce-scatter.2.cloned.1.call-update) | async-done | bytes 262160 | tf_op jit(solution)/shard_map/reduce_scatter | solution.py:59
  956.4 1.0 fusion.2
  957.4 0.9 copy.12
  (19 shorter events, 0.1 us)
Async XLA Ops:
  7.2 221.9 %copy-start = (bf16[2,1,128,128]{3,2,1,0:T(8,128)(2,1)S(1)}, bf16[2,1,128,128]{3,2,1,0:T(8,128)(2,1)}, u32[]{:S(2)}) copy-start(bf16[2,1,128,128]{3,2,1,0:T(8,128)(2,1)} %param.11) | copy-start | bytes 196612
  9.8 4.0 copy-start.4
  9.8 5.2 copy-start.8
  9.8 5.8 copy-start.6
  9.8 5.8 copy-start.7
  9.8 6.4 copy-start.3
  19.0 2.6 copy-start.2
  24.8 17.4 %copy-start.5 = (s32[64]{0:T(128)S(1)}, s32[64]{0:T(128)}, u32[]{:S(2)}) copy-start(s32[64]{0:T(128)} %param.12) | copy-start | bytes 772
  24.8 204.2 %all-to-all-start = ((bf16[2,64,128,128]{3,2,0,1:T(8,128)(2,1)}), bf16[2,64,128,128]{3,2,0,1:T(8,128)(2,1)}, u32[]{:S(2)}, u32[]{:S(2)}) async-start(bf16[2,64,128,128]{3,2,0,1:T(8,128)(2,1)} %convert_bitcast_fusion.1), calls=%async_computation | async-start | bytes 8388608 | tf_op jit(solution)/shard_map/all_to_all | solution.py:10
  42.2 560.6 %all-reduce.2.cloned.1.call-start = ((), (), s32[]{:S(2)}) async-start(), calls=%async_computation.3 | async-start | bytes 4194304 | tf_op jit(solution)/shard_map/psum | solution.py:48
  612.9 194.9 %all-to-all-start.1 = ((bf16[2,64,128,128]{2,3,0,1:T(8,128)(2,1)}), bf16[2,64,128,128]{2,3,0,1:T(8,128)(2,1)}, u32[]{:S(2)}, u32[]{:S(2)}) async-start(bf16[2,64,128,128]{2,3,0,1:T(8,128)(2,1)} %convert_bitcast_fusion), calls=%async_computation.1 | async-start | bytes 8388608 | tf_op jit(solution)/shard_map/all_to_all | solution.py:10
  621.0 335.4 %reduce-scatter.2.cloned.1.call-start = ((), (), s32[]{:S(2)}) async-start(), calls=%async_computation.4 | async-start | bytes 2359296 | tf_op jit(solution)/shard_map/reduce_scatter | solution.py:59
  813.4 1.6 copy-start.1
Sparse Core Ops, SparseCore 0:
  234.8 367.9 all-reduce.1
  813.5 142.7 reduce-scatter.1
where the time goes:
time: 966 us; the launch traced here: 965 us
  waiting for transfers between devices  874 us (90%)
  starting transfers between devices  25.5 us (3%)
  local copies, waits for them, and re-layouts  19.5 us (2%)
  between operations  18.2 us (2%)
  other arithmetic  14.9 us (2%)
  matrix products  13.3 us (1%)
    all_to_all x2, waiting for transfers between devices, relayout(): lax.all_to_all(blocks, ('lsec', 'rsec'), split_axis=1, concat_axis=1, til...  372 us
    psum x1, waiting for transfers between devices, on_device(): lax.psum(partial_value.astype(jnp.bfloat16), 'ops').astype(jnp.float32)  363 us
    reduce_scatter x1, waiting for transfers between devices, on_device(): lax.psum_scatter(second_partial.astype(jnp.bfloat16), 'ops', scatter_dime...  139 us
    all_to_all x2, starting transfers between devices, relayout(): lax.all_to_all(blocks, ('lsec', 'rsec'), split_axis=1, concat_axis=1, til...  25.4 us
  transfers between devices with their start and end apart: 4, of which 4 were waited for; matrix products, arithmetic and copies ran while one was open for 1% of the time, Pallas kernels for 0%

commit v1 on v0

v1 whole, which is shorter than its diff:
```python
import jax
import jax.numpy as jnp
import numpy as np
from jax import lax
from jax.sharding import Mesh
from jax.sharding import PartitionSpec as P

SPREAD = 1
NX, NC, NZ, NY, NH = 4, 2, 8, 4, 2
AXES = ("x", "c", "z", "y", "h")
SLOT = ("x", "c", "z")
SHIFT = np.array(
    [
        [[0, 4], [0, -4]],
        [[1, -3], [-1, 3]],
        [[-1, 3], [1, -3]],
        [[2, -2], [-2, 2]],
    ],
    np.int32,
)
HOLDER_Y = np.zeros((NC, NZ), np.int32)
HOLDER_N = np.zeros((NC, NZ), np.int32)
for _y in range(NY):
    for _c in range(NC):
        for _n in range(2):
            HOLDER_Y[_c, SHIFT[_y, _c, _n] % NZ] = _y
            HOLDER_N[_c, SHIFT[_y, _c, _n] % NZ] = _n


def index_of(x, c, z, y):
    return (((x * NC + c) * NZ + z % NZ) * NY + y) * NH + (z // NZ) % NH


def moved(target):
    pairs = []
    for x in range(NX):
        for c in range(NC):
            for z in range(NZ * NH):
                for y in range(NY):
                    pairs.append((index_of(x, c, z, y), index_of(*target(x, c, z % 16, y))))
    return pairs


def permute(value, target):
    return lax.ppermute(value, AXES, moved(lambda x, c, z, y: target(x, c, z, y)))


def shift_z(value, n, sign):
    return permute(
        value, lambda x, c, z, y: (x, c, (z + sign * int(SHIFT[y, c, n])) % 16, y)
    )


def swap_half(value):
    return permute(value, lambda x, c, z, y: (x, c, (z + 8) % 16, y))


def swap_core(value):
    return permute(value, lambda x, c, z, y: (x, 1 - c, z, y))


def inverse(order):
    count = order.shape[0]
    return jnp.zeros((count,), jnp.int32).at[order].set(jnp.arange(count, dtype=jnp.int32))


def on_device(
    psi, left_ops, right_ops, left_order, right_order, left_qn, right_qn, left_dims, right_dims
):
    x, c, z = lax.axis_index("x"), lax.axis_index("c"), lax.axis_index("z")
    y, h = lax.axis_index("y"), lax.axis_index("h")
    slot = (x * NC + c) * NZ + z
    m = psi.shape[-1]
    line = jnp.arange(m, dtype=jnp.int32)
    zero = jnp.zeros((), jnp.bfloat16)
    inv_left = inverse(left_order)
    inv_right = inverse(right_order)
    shift = jnp.asarray(SHIFT)
    holder_y = jnp.asarray(HOLDER_Y)
    holder_n = jnp.asarray(HOLDER_N)

    def mask(a, b):
        allowed = jnp.abs(left_qn[a] - right_qn[b]) <= SPREAD
        rows = line < left_dims[a][..., None]
        cols = line < right_dims[b][..., None]
        return allowed[..., None, None] & rows[..., :, None] & cols[..., None, :]

    with jax.named_scope("half_exchange"):
        own = jnp.concatenate([left_ops[:, 0], right_ops[:, 0]], 0)
        other = swap_half(own)
    low = jnp.where(h == 0, own, other)
    high = jnp.where(h == 0, other, own)
    left4 = jnp.concatenate([low[:2], high[:2]], 0)
    right4 = jnp.concatenate([low[2:], high[2:]], 0)
    with jax.named_scope("left_terms_over_y"):
        left16 = lax.all_to_all(
            jnp.broadcast_to(left4[None], (NY,) + left4.shape), "y", 0, 0, tiled=True
        ).reshape(16, m, m)
    with jax.named_scope("left_shift"):
        left_own = jnp.stack([shift_z(left16, n, -1) for n in range(2)])
    with jax.named_scope("right_over_xy"):
        right = lax.all_to_all(
            jnp.broadcast_to(right4[None], (NX * NY,) + right4.shape), ("x", "y"), 0, 0, tiled=True
        ).reshape(NX, 16, m, m)
    with jax.named_scope("left_core"):
        left = jnp.stack([left_own, swap_core(left_own)])

    here = left_order[slot]
    plane = jnp.arange(NX * NC, dtype=jnp.int32) * NZ
    with jax.named_scope("psi_shift"):
        moved_psi = []
        for n in range(2):
            target = (z - shift[y, c, n]) % NZ
            b = right_order[plane + target]
            block = jnp.where(mask(here, b), psi[0][b], zero)
            moved_psi.append(shift_z(block, n, -1))
        got = jnp.stack(moved_psi).reshape(2, NX, NC, m, m)
    with jax.named_scope("psi_core"):
        keep = jnp.where(c == 0, got[:, :, 0], got[:, :, 1])
        give = jnp.where(c == 0, got[:, :, 1], got[:, :, 0])
        start = jnp.stack([keep, swap_core(give)])

    core = jnp.stack([c, 1 - c])
    left_slot = (x * NC + core[:, None]) * NZ + (z + shift[y][core]) % NZ
    a4 = left_order[left_slot]
    b4 = right_order[(jnp.arange(NX) * NC + c) * NZ + z]
    mask16 = mask(a4[:, :, None], b4[None, None, :])

    with jax.named_scope("first"):
        inner = jnp.einsum(
            "cnkpq,cnxqr->cnxpkr", left, start, preferred_element_type=jnp.float32
        ).astype(jnp.bfloat16)
        first = jnp.einsum("cnxpkr,xksr->xcnps", inner, right, preferred_element_type=jnp.float32)
        first = jnp.where(jnp.moveaxis(mask16, 2, 0), first, 0.0).astype(jnp.bfloat16)
    with jax.named_scope("first_out"):
        sent = jnp.broadcast_to(first[:, None], (NX, NY) + first.shape[1:])
        came = lax.all_to_all(
            sent.reshape((NX * NY,) + first.shape[1:]), ("x", "y"), 0, 0, tiled=True
        ).reshape(64, m, m)
        from_slot = inv_left
        from_x, from_c, from_z = from_slot // (NC * NZ), (from_slot // NZ) % NC, from_slot % NZ
        delta = (from_z - z) % NZ
        place = (
            (from_x * NY + holder_y[from_c, delta]) * 4
            + jnp.where(from_c == c, 0, 2)
            + holder_n[from_c, delta]
        )
        first_out = came[place]

    with jax.named_scope("second"):
        inner = jnp.einsum(
            "xcnpq,xkrq->xcnkpr", first, right, preferred_element_type=jnp.float32
        ).astype(jnp.bfloat16)
        second = jnp.einsum(
            "cnkpq,xcnkqr->cnxpr", left, inner, preferred_element_type=jnp.float32
        ).astype(jnp.bfloat16)
    with jax.named_scope("second_core"):
        theirs = swap_core(second[1])
        both = jnp.where(
            c == 0, jnp.stack([second[0], theirs], 2), jnp.stack([theirs, second[0]], 2)
        ).reshape(2, NX * NC, m, m)
    with jax.named_scope("second_shift"):
        back = jnp.concatenate([shift_z(both[n], n, 1) for n in range(2)], 0)
    with jax.named_scope("second_over_y"):
        b_all = (
            (jnp.arange(NY, dtype=jnp.int32)[:, None] * NH + h) * 8
            + jnp.arange(8, dtype=jnp.int32)[None, :]
        )
        j = inv_right[b_all]
        j_xc, j_z = j // NZ, j % NZ
        delta = (z - j_z) % NZ
        owner = holder_y[c, delta]
        position = holder_n[c, delta] * (NX * NC) + j_xc
        packed = back[position.reshape(-1)]
        arrived = lax.all_to_all(packed, "y", 0, 0, tiled=True).reshape(NY, 8, m, m)
        chosen = arrived[owner[y], jnp.arange(8)]
        b8 = b_all[y]
        second_out = jnp.where(mask(here, b8), chosen, zero)
    return first_out[None], second_out[None]


def solution(mesh):
    fine = Mesh(mesh.devices.reshape(NX, NC, NZ, NY, NH), AXES)
    slots, ops = P(SLOT), P(("y", "h"), SLOT)
    return jax.shard_map(
        on_device,
        mesh=fine,
        in_specs=(slots, ops, ops, P(), P(), P(), P(), P(), P()),
        out_specs=(slots, P(SLOT, ("y", "h"))),
        check_vma=False,
    )
```

time: 966 us -> 210 us (0.22)
  waiting for transfers between devices: 874 us -> 55.7 us
  blocking collectives: 0 us -> 28.3 us
  starting transfers between devices: 25.5 us -> 53 us
  local copies, waits for them, and re-layouts: 19.5 us -> 37.6 us
  between operations: 18.2 us -> 4.17 us
    psum x1 -> x0, waiting for transfers between devices: 363 us -> none  [on_device(): lax.psum(partial_value.astype(jnp.bfloat16), 'ops').astype(jnp.float32)]
    all_to_all x2 -> x3, waiting for transfers between devices: 372 us -> 26.9 us  [the longest x1 19.9 us: on_device(): lax.all_to_all(sent.reshape((NX * NY,) + first.shape[1:]), ('x', 'y'), 0,...]
    reduce_scatter x1 -> x0, waiting for transfers between devices: 139 us -> none  [on_device(): lax.psum_scatter(second_partial.astype(jnp.bfloat16), 'ops', scatter_dime...]
    ppermute x0 -> x10, starting transfers between devices: none -> 37.1 us  [permute(): lax.ppermute(value, AXES, moved(lambda x, c, z, y: target(x, c, z, y)))]
    ppermute x0 -> x10, waiting for transfers between devices: none -> 28.8 us  [permute(): lax.ppermute(value, AXES, moved(lambda x, c, z, y: target(x, c, z, y)))]
    all_to_all x0 -> x1, blocking collectives: none -> 28.3 us  [on_device(): arrived = lax.all_to_all(packed, 'y', 0, 0, tiled=True).reshape(NY, 8, m, m)]
    gather x4 -> x28, local copies, waits for them, and re-layouts: 9.4 us -> 22.9 us  [the longest x5 4.52 us: mask(): allowed = jnp.abs(left_qn[a] - right_qn[b]) <= SPREAD]
    all_to_all x2 -> x3, starting transfers between devices: 25.4 us -> 15.8 us  [the longest x1 5.79 us: on_device(): lax.all_to_all(jnp.broadcast_to(left4[None], (NY,) + left4.shape), 'y', 0...]
  transfers between devices with their start and end apart: 4 -> 13, of which waited for: 4 -> 4; matrix products, arithmetic and copies ran while one was open for 1% -> 19% of each run, Pallas kernels for 0% -> 0%
where the time goes in v1:
time: 210 us; the launch traced here: 206 us
  waiting for transfers between devices  55.7 us (27%)
  starting transfers between devices  53 us (25%)
  local copies, waits for them, and re-layouts  37.6 us (18%)
  blocking collectives  28.3 us (13%)
  matrix products  14.7 us (7%)
  other arithmetic  12.8 us (6%)
  between operations  4.17 us (2%)
    ppermute x10, starting transfers between devices, permute(): lax.ppermute(value, AXES, moved(lambda x, c, z, y: target(x, c, z, y)))  37.1 us
    ppermute x10, waiting for transfers between devices, permute(): lax.ppermute(value, AXES, moved(lambda x, c, z, y: target(x, c, z, y)))  28.8 us
    all_to_all x1, blocking collectives, on_device(): arrived = lax.all_to_all(packed, 'y', 0, 0, tiled=True).reshape(NY, 8, m, m)  28.3 us
    all_to_all x1, waiting for transfers between devices, on_device(): lax.all_to_all(sent.reshape((NX * NY,) + first.shape[1:]), ('x', 'y'), 0,...  19.9 us
    dot_general x1, matrix products, on_device(): jnp.einsum('cnxpkr,xksr->xcnps', inner, right, preferred_element_type=jnp...  7.36 us
    dot_general x1, matrix products, on_device(): jnp.einsum('cnkpq,xcnkqr->cnxpr', left, inner, preferred_element_type=jnp...  7.32 us
    all_to_all x1, waiting for transfers between devices, on_device(): lax.all_to_all(jnp.broadcast_to(left4[None], (NY,) + left4.shape), 'y', 0...  7.01 us
    all_to_all x1, starting transfers between devices, on_device(): lax.all_to_all(jnp.broadcast_to(left4[None], (NY,) + left4.shape), 'y', 0...  5.79 us
  transfers between devices with their start and end apart: 13, of which 4 were waited for; matrix products, arithmetic and copies ran while one was open for 19% of the time, Pallas kernels for 0%

profile of v1, /device:TPU:1, one launch (start us, length us, event | category | flops | bytes accessed | tf_op | source)
XLA Modules:
  0.0 206.2 jit_solution(16912003621779600191)
XLA Ops:
  0.7 1.0 pad_maximum_fusion.7
  1.7 16.3 %collective-permute-start.3 = (bf16[4,128,128]{2,1,0:T(8,128)(2,1)S(1)}, bf16[4,128,128]{2,1,0:T(8,128)(2,1)S(1)}, u32[]{:S(2)}, u32[]{:S(2)}) collective-permute-start(bf16[4,128,128]{2,1,0:T(8,128)(2,1)S(1)} %pad_maximum_fusion.7), channel_id=1, source_target_pairs={{0,1},{2,3},{4,5},{6,7},{8,9},{10,11},{12,13},{14,15},{16,17},{18,... | collective-permute-start | bytes 393224 | tf_op jit(solution)/shard_map/half_exchange/ppermute | solution.py:45
  18.0 1.2 dynamic_slice.29
  20.4 1.3 constant_dynamic-slice_fusion.2
  23.6 1.2 dynamic_slice.32
  24.9 1.2 dynamic_slice.30
  26.9 1.3 gather_fusion.7
  28.2 1.3 gather_fusion.18
  29.5 1.3 gather_fusion.8
  35.6 0.9 and_select_fusion.2
  36.5 1.6 collective-permute-start
  39.4 0.9 and_select_fusion.1
  40.3 4.1 %collective-permute-start.1 = (bf16[8,128,128]{2,1,0:T(8,128)(2,1)}, bf16[8,128,128]{2,1,0:T(8,128)(2,1)}, u32[]{:S(2)}, u32[]{:S(2)}) collective-permute-start(bf16[8,128,128]{2,1,0:T(8,128)(2,1)} %and_select_fusion.1), channel_id=1, source_target_pairs={{0,33},{2,26},{4,45},{6,22},{8,41},{10,34},{12,53},{14,30},{16,49}... | collective-permute-start | bytes 786440 | tf_op jit(solution)/shard_map/psi_shift/ppermute | solution.py:45
  44.5 0.7 dynamic-slice_bitcast_fusion
  47.0 0.9 broadcast_in_dim.32
  47.9 5.8 %all-to-all-start = ((bf16[4,4,128,128]{3,2,1,0:T(8,128)(2,1)}), bf16[4,4,128,128]{3,2,1,0:T(8,128)(2,1)S(1)}, u32[]{:S(2)}, u32[]{:S(2)}) async-start(bf16[4,4,128,128]{3,2,1,0:T(8,128)(2,1)} %broadcast_in_dim.32), calls=%async_computation | async-start | bytes 1048576 | tf_op jit(solution)/shard_map/left_terms_over_y/all_to_all | solution.py:96
  55.6 7.0 %all-to-all-done = bf16[4,4,128,128]{3,2,1,0:T(8,128)(2,1)S(1)} async-done(((bf16[4,4,128,128]{3,2,1,0:T(8,128)(2,1)}), bf16[4,4,128,128]{3,2,1,0:T(8,128)(2,1)S(1)}, u32[]{:S(2)}, u32[]{:S(2)}) %all-to-all-start) | async-done | bytes 524320 | tf_op jit(solution)/shard_map/left_terms_over_y/all_to_all | solution.py:96
  62.6 1.8 broadcast_in_dim.33
  64.5 4.8 %all-to-all-start.1 = ((bf16[16,4,128,128]{3,2,1,0:T(8,128)(2,1)}), bf16[16,4,128,128]{3,2,1,0:T(8,128)(2,1)}, u32[]{:S(2)}, u32[]{:S(2)}) async-start(bf16[16,4,128,128]{3,2,1,0:T(8,128)(2,1)} %broadcast_in_dim.33), calls=%async_computation.1 | async-start | bytes 4194304 | tf_op jit(solution)/shard_map/right_over_xy/all_to_all | solution.py:102
  69.3 2.4 %collective-permute-start.5 = (bf16[16,128,128]{2,1,0:T(8,128)(2,1)S(1)}, bf16[16,128,128]{2,1,0:T(8,128)(2,1)}, u32[]{:S(2)}, u32[]{:S(2)}) collective-permute-start(bf16[16,128,128]{2,1,0:T(8,128)(2,1)S(1)} %bitcast.196), channel_id=1, source_target_pairs={{0,33},{2,26},{4,45},{6,22},{8,41},{10,34},{12,53},{14,30},{16,49}... | collective-permute-start | bytes 1572872 | tf_op jit(solution)/shard_map/left_shift/ppermute | solution.py:45
  71.7 1.4 collective-permute-start.4
  74.1 19.6 %collective-permute-done.5 = bf16[16,128,128]{2,1,0:T(8,128)(2,1)} collective-permute-done((bf16[16,128,128]{2,1,0:T(8,128)(2,1)S(1)}, bf16[16,128,128]{2,1,0:T(8,128)(2,1)}, u32[]{:S(2)}, u32[]{:S(2)}) %collective-permute-start.5) | collective-permute-done | bytes 524320 | tf_op jit(solution)/shard_map/left_shift/ppermute | solution.py:45
  93.7 2.3 %fusion.87 = (bf16[1,2,16,128,128]{4,3,2,1,0:T(8,128)(2,1)S(1)}, bf16[2,16,128,128]{3,2,1,0:T(8,128)(2,1)}) fusion(bf16[1,16,128,128]{3,2,1,0:T(8,128)(2,1)} %bitcast.35, bf16[1,16,128,128]{3,2,1,0:T(8,128)(2,1)} %bitcast.34), kind=kLoop, calls=%fused_computation.191 | loop fusion | flops 524288 | bytes 3145728 | tf_op jit(solution)/shard_map/left_core/stack | solution.py:106
  96.0 4.2 %collective-permute-start.6 = (bf16[2,16,128,128]{3,2,1,0:T(8,128)(2,1)}, bf16[2,16,128,128]{3,2,1,0:T(8,128)(2,1)}, u32[]{:S(2)}, u32[]{:S(2)}) collective-permute-start(bf16[2,16,128,128]{3,2,1,0:T(8,128)(2,1)} %get-tuple-element.5), channel_id=1, source_target_pairs={{0,64},{2,66},{4,68},{6,70},{8,72},{10,74},{12,76},{14,78},{16,80}... | collective-permute-start | bytes 3145736 | tf_op jit(solution)/shard_map/left_core/ppermute | solution.py:45
  101.1 1.0 fusion.47
  102.1 1.9 collective-permute-start.2
  104.1 1.7 fusion.49
  105.9 0.7 copy-done.12
  106.6 7.4 %fusion.38 = bf16[4,2,2,128,128]{4,3,2,1,0:T(8,128)(2,1)} fusion(bf16[4,16,128,128,1,1]{3,2,1,5,4,0:T(8,128)(2,1)} %bitcast.42, bf16[1,2,16,128,128]{4,3,2,1,0:T(8,128)(2,1)} %bitcast.37, bf16[1,2,16,128,128]{4,3,2,1,0:T(8,128)(2,1)S(1)} %get-tuple-element.4, pred[4,128]{1,0:T(4,128)(4,1)S(1)} %iota_compare_fusion.3, ...), kind=kOutput, calls=%fused_computation.43 | convolution fusion | flops 2156920832 | bytes 5245440 | tf_op jit(solution)/shard_map/first/cnxpkr,xksr->xcnps/dot_general | solution.py:133
  113.9 7.3 %fusion.28 = bf16[2,2,4,128,128]{3,4,2,1,0:T(8,128)(2,1)} fusion(bf16[1,2,16,128,128]{4,3,2,1,0:T(8,128)(2,1)} %bitcast.37, bf16[1,2,16,128,128]{4,3,2,1,0:T(8,128)(2,1)S(1)} %get-tuple-element.4, bf16[4,16,128,128,1,1]{3,2,1,0,5,4:T(8,128)(2,1)} %bitcast.51, bf16[4,2,2,128,128]{4,3,2,1,0:T(8,128)(2,1)} %fusion.38), kind=kOutput, calls=%fused_computation.41 | convolution fusion | flops 2152988672 | bytes 5242880 | tf_op jit(solution)/shard_map/second/cnkpq,xcnkqr->cnxpr/dot_general | solution.py:154
  121.2 1.1 slice_bitcast_fusion.1
  122.3 2.6 %collective-permute-start.7 = (bf16[2,4,128,128]{2,3,1,0:T(8,128)(2,1)S(1)}, bf16[2,4,128,128]{2,3,1,0:T(8,128)(2,1)S(1)}, u32[]{:S(2)}, u32[]{:S(2)}) collective-permute-start(bf16[2,4,128,128]{2,3,1,0:T(8,128)(2,1)S(1)} %get-tuple-element.9), channel_id=1, source_target_pairs={{0,64},{2,66},{4,68},{6,70},{8,72},{10,74},{12,76},{14,78},{16,80}... | collective-permute-start | bytes 786440 | tf_op jit(solution)/shard_map/second_core/ppermute | solution.py:45
  125.0 0.8 scatter_custom_fusion.1
  125.7 0.7 gather_fusion.20
  126.6 0.8 gather_fusion.21
  127.9 1.9 collective-permute-start.9
  130.6 9.1 %collective-permute-done.9 = bf16[8,128,128]{2,1,0:T(8,128)(2,1)S(1)} collective-permute-done((bf16[8,128,128]{2,1,0:T(8,128)(2,1)S(1)}, bf16[8,128,128]{2,1,0:T(8,128)(2,1)S(1)}, u32[]{:S(2)}, u32[]{:S(2)}) %collective-permute-start.9) | collective-permute-done | bytes 262176 | tf_op jit(solution)/shard_map/second_shift/ppermute | solution.py:45
  139.8 1.7 gather_fusion.22
  141.4 28.3 %all_to_all.20 = bf16[32,128,128]{2,1,0:T(8,128)(2,1)S(1)} all-to-all(bf16[32,128,128]{2,1,0:T(8,128)(2,1)} %gather_fusion.22), channel_id=1, replica_groups=mesh['x'=4,'c'=2,'z'=8,'y'=4,'h'=2] {'y'}, dimensions={0} | all-to-all | bytes 2097152 | tf_op jit(solution)/shard_map/second_over_y/all_to_all | solution.py:175
  169.7 1.9 broadcast_in_dim.35
  171.6 5.2 %all-to-all-start.2 = ((bf16[16,2,2,128,128]{4,3,2,1,0:T(8,128)(2,1)}), bf16[16,2,2,128,128]{4,3,2,1,0:T(8,128)(2,1)}, u32[]{:S(2)}, u32[]{:S(2)}) async-start(bf16[16,2,2,128,128]{4,3,2,1,0:T(8,128)(2,1)} %bitcast.191), calls=%async_computation.2 | async-start | bytes 4194304 | tf_op jit(solution)/shard_map/first_out/all_to_all | solution.py:137
  177.5 0.8 scatter_custom_fusion
  178.4 0.9 gather_fusion.16
  179.2 0.9 gather_fusion.15
  180.1 0.8 gather_fusion.23
  181.7 0.9 and_select_fusion
  182.6 19.9 %all-to-all-done.2 = bf16[16,2,2,128,128]{4,3,2,1,0:T(8,128)(2,1)} async-done(((bf16[16,2,2,128,128]{4,3,2,1,0:T(8,128)(2,1)}), bf16[16,2,2,128,128]{4,3,2,1,0:T(8,128)(2,1)}, u32[]{:S(2)}, u32[]{:S(2)}) %all-to-all-start.2) | async-done | bytes 2097184 | tf_op jit(solution)/shard_map/first_out/all_to_all | solution.py:137
  202.5 3.7 %gather_fusion.17 = bf16[64,128,128]{2,1,0:T(8,128)(2,1)} fusion(bf16[64,128,128]{2,1,0:T(8,128)(2,1)} %bitcast.46, s32[1024]{0:T(1024)S(1)} %pad_clamp_fusion.3), kind=kCustom, calls=%fused_computation.17 | custom fusion | bytes 4194560 | tf_op jit(solution)/shard_map/first_out/gather | solution.py:148
  (114 shorter events, 15.4 us)
Async XLA Ops:
  0.6 34.3 %copy-start = (bf16[1,64,128,128]{3,2,1,0:T(8,128)(2,1)S(1)}, bf16[1,64,128,128]{3,2,1,0:T(8,128)(2,1)}, u32[]{:S(2)}) copy-start(bf16[1,64,128,128]{3,2,1,0:T(8,128)(2,1)} %param.12) | copy-start | bytes 6291460
  0.6 32.2 %copy-start.5 = (s32[64]{0:T(128)S(1)}, s32[64]{0:T(128)}, u32[]{:S(2)}) copy-start(s32[64]{0:T(128)} %param.16) | copy-start | bytes 772
  0.7 32.9 %copy-start.1 = (s32[64]{0:T(128)S(1)}, s32[64]{0:T(128)}, u32[]{:S(2)}) copy-start(s32[64]{0:T(128)} %param.18) | copy-start | bytes 772
  0.7 30.1 %copy-start.2 = (s32[64]{0:T(128)S(1)}, s32[64]{0:T(128)}, u32[]{:S(2)}) copy-start(s32[64]{0:T(128)} %param.20) | copy-start | bytes 772
  1.7 45.2 %collective-permute-start.3 = (bf16[4,128,128]{2,1,0:T(8,128)(2,1)S(1)}, bf16[4,128,128]{2,1,0:T(8,128)(2,1)S(1)}, u32[]{:S(2)}, u32[]{:S(2)}) collective-permute-start(bf16[4,128,128]{2,1,0:T(8,128)(2,1)S(1)} %pad_maximum_fusion.7), channel_id=1, source_target_pairs={{0,1},{2,3},{4,5},{6,7},{8,9},{10,11},{12,13},{14,15},{16,17},{18,... | collective-permute-start | bytes 393224 | tf_op jit(solution)/shard_map/half_exchange/ppermute | solution.py:45
  30.8 15.3 %copy-start.6 = (s32[64]{0:T(128)S(1)}, s32[64]{0:T(128)}, u32[]{:S(2)}) copy-start(s32[64]{0:T(128)} %param.15) | copy-start | bytes 772
  33.6 13.3 %copy-start.10 = (bf16[2,1,128,128]{3,2,1,0:T(8,128)(2,1)S(1)}, bf16[2,1,128,128]{3,2,1,0:T(8,128)(2,1)}, u32[]{:S(2)}) copy-start(bf16[2,1,128,128]{3,2,1,0:T(8,128)(2,1)} %param.14) | copy-start | bytes 196612
  33.6 13.3 %copy-start.11 = (bf16[2,1,128,128]{3,2,1,0:T(8,128)(2,1)S(1)}, bf16[2,1,128,128]{3,2,1,0:T(8,128)(2,1)}, u32[]{:S(2)}) copy-start(bf16[2,1,128,128]{3,2,1,0:T(8,128)(2,1)} %param.13) | copy-start | bytes 196612
  36.5 64.6 %collective-permute-start = (bf16[8,128,128]{2,1,0:T(8,128)(2,1)}, bf16[8,128,128]{2,1,0:T(8,128)(2,1)S(1)}, u32[]{:S(2)}, u32[]{:S(2)}) collective-permute-start(bf16[8,128,128]{2,1,0:T(8,128)(2,1)} %and_select_fusion.2), channel_id=1, source_target_pairs={{0,0},{2,59},{4,12},{6,55},{8,8},{10,2},{12,20},{14,63},{16,16},{1... | collective-permute-start | bytes 786440 | tf_op jit(solution)/shard_map/psi_shift/ppermute | solution.py:45
  40.3 13.3 %copy-start.7 = (s32[64]{0:T(128)S(1)}, s32[64]{0:T(128)}, u32[]{:S(2)}) copy-start(s32[64]{0:T(128)} %param.19) | copy-start | bytes 772
  40.3 60.8 %collective-permute-start.1 = (bf16[8,128,128]{2,1,0:T(8,128)(2,1)}, bf16[8,128,128]{2,1,0:T(8,128)(2,1)}, u32[]{:S(2)}, u32[]{:S(2)}) collective-permute-start(bf16[8,128,128]{2,1,0:T(8,128)(2,1)} %and_select_fusion.1), channel_id=1, source_target_pairs={{0,33},{2,26},{4,45},{6,22},{8,41},{10,34},{12,53},{14,30},{16,49}... | collective-permute-start | bytes 786440 | tf_op jit(solution)/shard_map/psi_shift/ppermute | solution.py:45
  46.7 7.6 %copy-start.8 = (s32[64]{0:T(128)S(1)}, s32[64]{0:T(128)}, u32[]{:S(2)}) copy-start(s32[64]{0:T(128)} %param.17) | copy-start | bytes 772
  47.9 14.8 %all-to-all-start = ((bf16[4,4,128,128]{3,2,1,0:T(8,128)(2,1)}), bf16[4,4,128,128]{3,2,1,0:T(8,128)(2,1)S(1)}, u32[]{:S(2)}, u32[]{:S(2)}) async-start(bf16[4,4,128,128]{3,2,1,0:T(8,128)(2,1)} %broadcast_in_dim.32), calls=%async_computation | async-start | bytes 1048576 | tf_op jit(solution)/shard_map/left_terms_over_y/all_to_all | solution.py:96
  64.5 42.1 %all-to-all-start.1 = ((bf16[16,4,128,128]{3,2,1,0:T(8,128)(2,1)}), bf16[16,4,128,128]{3,2,1,0:T(8,128)(2,1)}, u32[]{:S(2)}, u32[]{:S(2)}) async-start(bf16[16,4,128,128]{3,2,1,0:T(8,128)(2,1)} %broadcast_in_dim.33), calls=%async_computation.1 | async-start | bytes 4194304 | tf_op jit(solution)/shard_map/right_over_xy/all_to_all | solution.py:102
  69.3 24.4 %collective-permute-start.5 = (bf16[16,128,128]{2,1,0:T(8,128)(2,1)S(1)}, bf16[16,128,128]{2,1,0:T(8,128)(2,1)}, u32[]{:S(2)}, u32[]{:S(2)}) collective-permute-start(bf16[16,128,128]{2,1,0:T(8,128)(2,1)S(1)} %bitcast.196), channel_id=1, source_target_pairs={{0,33},{2,26},{4,45},{6,22},{8,41},{10,34},{12,53},{14,30},{16,49}... | collective-permute-start | bytes 1572872 | tf_op jit(solution)/shard_map/left_shift/ppermute | solution.py:45
  71.7 22.0 %collective-permute-start.4 = (bf16[16,128,128]{2,1,0:T(8,128)(2,1)S(1)}, bf16[16,128,128]{2,1,0:T(8,128)(2,1)}, u32[]{:S(2)}, u32[]{:S(2)}) collective-permute-start(bf16[16,128,128]{2,1,0:T(8,128)(2,1)S(1)} %bitcast.197), channel_id=1, source_target_pairs={{0,0},{2,59},{4,12},{6,55},{8,8},{10,2},{12,20},{14,63},{16,16},{1... | collective-permute-start | bytes 1572872 | tf_op jit(solution)/shard_map/left_shift/ppermute | solution.py:45
  96.0 10.6 %collective-permute-start.6 = (bf16[2,16,128,128]{3,2,1,0:T(8,128)(2,1)}, bf16[2,16,128,128]{3,2,1,0:T(8,128)(2,1)}, u32[]{:S(2)}, u32[]{:S(2)}) collective-permute-start(bf16[2,16,128,128]{3,2,1,0:T(8,128)(2,1)} %get-tuple-element.5), channel_id=1, source_target_pairs={{0,64},{2,66},{4,68},{6,70},{8,72},{10,74},{12,76},{14,78},{16,80}... | collective-permute-start | bytes 3145736 | tf_op jit(solution)/shard_map/left_core/ppermute | solution.py:45
  102.1 3.7 %collective-permute-start.2 = (bf16[2,4,128,128]{3,2,1,0:T(8,128)(2,1)S(1)}, bf16[2,4,128,128]{3,2,1,0:T(8,128)(2,1)S(1)}, u32[]{:S(2)}, u32[]{:S(2)}) collective-permute-start(bf16[2,4,128,128]{3,2,1,0:T(8,128)(2,1)S(1)} %fusion.47), channel_id=1, source_target_pairs={{0,64},{2,66},{4,68},{6,70},{8,72},{10,74},{12,76},{14,78},{16,80}... | collective-permute-start | bytes 786440 | tf_op jit(solution)/shard_map/psi_core/ppermute | solution.py:45
  105.9 0.7 copy-start.12
  121.2 5.4 %copy-start.4 = (s32[2,8]{1,0:T(2,128)S(1)}, s32[2,8]{1,0:T(2,128)}, u32[]{:S(2)}) copy-start(s32[2,8]{1,0:T(2,128)} %constant.163.clone) | copy-start | bytes 196
  122.3 5.1 %collective-permute-start.7 = (bf16[2,4,128,128]{2,3,1,0:T(8,128)(2,1)S(1)}, bf16[2,4,128,128]{2,3,1,0:T(8,128)(2,1)S(1)}, u32[]{:S(2)}, u32[]{:S(2)}) collective-permute-start(bf16[2,4,128,128]{2,3,1,0:T(8,128)(2,1)S(1)} %get-tuple-element.9), channel_id=1, source_target_pairs={{0,64},{2,66},{4,68},{6,70},{8,72},{10,74},{12,76},{14,78},{16,80}... | collective-permute-start | bytes 786440 | tf_op jit(solution)/shard_map/second_core/ppermute | solution.py:45
  127.9 11.8 %collective-permute-start.9 = (bf16[8,128,128]{2,1,0:T(8,128)(2,1)S(1)}, bf16[8,128,128]{2,1,0:T(8,128)(2,1)S(1)}, u32[]{:S(2)}, u32[]{:S(2)}) collective-permute-start(bf16[8,128,128]{2,1,0:T(8,128)(2,1)S(1)} %bitcast.199), channel_id=1, source_target_pairs={{0,32},{2,43},{4,28},{6,55},{8,40},{10,51},{12,36},{14,63},{16,48}... | collective-permute-start | bytes 786440 | tf_op jit(solution)/shard_map/second_shift/ppermute | solution.py:45
  129.8 9.9 %collective-permute-start.8 = (bf16[8,128,128]{2,1,0:T(8,128)(2,1)S(1)}, bf16[8,128,128]{2,1,0:T(8,128)(2,1)S(1)}, u32[]{:S(2)}, u32[]{:S(2)}) collective-permute-start(bf16[8,128,128]{2,1,0:T(8,128)(2,1)S(1)} %bitcast.198), channel_id=1, source_target_pairs={{0,0},{2,10},{4,61},{6,22},{8,8},{10,18},{12,4},{14,30},{16,16},{1... | collective-permute-start | bytes 786440 | tf_op jit(solution)/shard_map/second_shift/ppermute | solution.py:45
  141.4 28.3 %copy-start.9 = (bf16[4,2,2,128,128]{4,3,2,1,0:T(8,128)(2,1)S(1)}, bf16[4,2,2,128,128]{4,3,2,1,0:T(8,128)(2,1)}, u32[]{:S(2)}) copy-start(bf16[4,2,2,128,128]{4,3,2,1,0:T(8,128)(2,1)} %fusion.38) | copy-start | bytes 1572868
  171.6 7.6 %copy-start.3 = (s32[2,8]{1,0:T(2,128)S(1)}, s32[2,8]{1,0:T(2,128)}, u32[]{:S(2)}) copy-start(s32[2,8]{1,0:T(2,128)} %constant.162.clone) | copy-start | bytes 196
  171.6 30.8 %all-to-all-start.2 = ((bf16[16,2,2,128,128]{4,3,2,1,0:T(8,128)(2,1)}), bf16[16,2,2,128,128]{4,3,2,1,0:T(8,128)(2,1)}, u32[]{:S(2)}, u32[]{:S(2)}) async-start(bf16[16,2,2,128,128]{4,3,2,1,0:T(8,128)(2,1)} %bitcast.191), calls=%async_computation.2 | async-start | bytes 4194304 | tf_op jit(solution)/shard_map/first_out/all_to_all | solution.py:137

commit v2 on v0

v2 whole, which is shorter than its diff:
```python
import jax
import jax.numpy as jnp
import numpy as np
from jax import lax
from jax.experimental import pallas as pl
from jax.experimental.pallas import tpu as pltpu
from jax.sharding import Mesh
from jax.sharding import PartitionSpec as P

SPREAD = 1
M = 128
NX, NC, NZ, NY, NH = 4, 2, 8, 4, 2
NK = 16
AXES = ("x", "c", "z", "y", "h")
SLOT = ("x", "c", "z")
SHIFT = np.array(
    [
        [[0, 4], [0, -4]],
        [[1, -3], [-1, 3]],
        [[-1, 3], [1, -3]],
        [[2, -2], [-2, 2]],
    ],
    np.int32,
)
HOLDER_Y = np.zeros((NC, NZ), np.int32)
for _y in range(NY):
    for _c in range(NC):
        for _n in range(2):
            HOLDER_Y[_c, SHIFT[_y, _c, _n] % NZ] = _y
LEFT_ORDER, RIGHT_ORDER, LEFT_QN, RIGHT_QN, LEFT_DIMS, RIGHT_DIMS, SHIFTS, HOLDERS = range(8)
CONSTANT_ROWS = np.zeros((2, 64), np.int32)
CONSTANT_ROWS[0, : SHIFT.size] = SHIFT.reshape(-1)
CONSTANT_ROWS[1, : HOLDER_Y.size] = HOLDER_Y.reshape(-1)


def index_of(x, c, z, y):
    return (((x * NC + c) * NZ + z % NZ) * NY + y) * NH + (z // NZ) % NH


def permute(value, target):
    pairs = []
    for x in range(NX):
        for c in range(NC):
            for z in range(NZ * NH):
                for y in range(NY):
                    to_c, to_z = target(c, z, y)
                    pairs.append((index_of(x, c, z, y), index_of(x, to_c, to_z % 16, y)))
    return lax.ppermute(value, AXES, pairs)


def here():
    return tuple(lax.axis_index(name) for name in AXES)


def shift_of(tab, y, c, n):
    return tab[SHIFTS, (y * NC + c) * 2 + n]


def slot_of(x, c, z):
    return (x * NC + c) * NZ + lax.rem(z + 2 * NZ, NZ)


def limits(tab, a, b):
    allowed = jnp.abs(tab[LEFT_QN, a] - tab[RIGHT_QN, b]) <= SPREAD
    return jnp.where(allowed, tab[LEFT_DIMS, a], 0), tab[RIGHT_DIMS, b]


def masked(block, tab, a, b):
    rows, cols = limits(tab, a, b)
    row = lax.broadcasted_iota(jnp.int32, (M, M), 0)
    col = lax.broadcasted_iota(jnp.int32, (M, M), 1)
    return jnp.where((row < rows) & (col < cols), block.astype(jnp.float32), 0.0)


def psi_kernel(tab, psi, keep0, keep1, give0, give1, sems):
    x, c, z, y, h = here()
    a = tab[LEFT_ORDER, slot_of(x, c, z)]
    work = []
    for n, (keep, give) in enumerate(((keep0, give0), (keep1, give1))):
        to_z = z - shift_of(tab, y, c, n)
        for out, to_c in ((keep, c), (give, 1 - c)):
            for to_x in range(NX):
                b = tab[RIGHT_ORDER, slot_of(to_x, to_c, to_z)]
                copy = pltpu.make_async_copy(psi.at[b], out.at[to_x], sems.at[len(work)])
                copy.start()
                work.append((copy, out, to_x, b))
    for copy, out, to_x, b in work:
        copy.wait()
        out[to_x] = masked(out[to_x], tab, a, b).astype(jnp.bfloat16)


def products_kernel(
    tab, lo0, lo1, lx0, lx1, right, so0, so1, sx0, sx1,
    send, keep0, keep1, give0, give1,
    left_v, right_v, state_v, inner_v, sems_l, sems_r, sems_s, sems_o,
):
    x, c, z, y, h = here()
    state_copies, right_copies, left_copies = [], [], []
    for i, source in enumerate((so0, so1, sx0, sx1)):
        copy = pltpu.make_async_copy(source, state_v.at[:, i], sems_s.at[i])
        copy.start()
        state_copies.append(copy)
    for j in range(NX):
        copy = pltpu.make_async_copy(right.at[j], right_v.at[j], sems_r.at[j])
        copy.start()
        right_copies.append(copy)
    for i, source in enumerate((lo0, lo1, lx0, lx1)):
        for k in range(NK):
            copy = pltpu.make_async_copy(
                source.at[k], left_v.at[i, :, pl.ds(k * M, M)], sems_l.at[i, k]
            )
            copy.start()
            left_copies.append(copy)

    def product(ready):
        for j in range(NX):
            if ready is not None:
                ready[j].wait()
            state = state_v[j].reshape(4 * M, M)
            for pair in range(NK // 2):
                term = right_v[j, 2 * pair : 2 * pair + 2].reshape(2 * M, M)
                inner = lax.dot_general(
                    state, term, (((1,), (1,)), ((), ())), preferred_element_type=jnp.float32
                ).astype(jnp.bfloat16)
                for i in range(4):
                    for half in range(2):
                        k = 2 * pair + half
                        inner_v[i, k * M : (k + 1) * M, j * M : (j + 1) * M] = inner[
                            i * M : (i + 1) * M, half * M : (half + 1) * M
                        ]

    def total(i):
        return jnp.dot(left_v[i], inner_v[i], preferred_element_type=jnp.float32)

    for copy in state_copies:
        copy.wait()
    product(right_copies)
    for copy in left_copies:
        copy.wait()
    for i in range(4):
        value = total(i)
        core = c if i < 2 else 1 - c
        a = tab[LEFT_ORDER, slot_of(x, core, z + shift_of(tab, y, core, i % 2))]
        for j in range(NX):
            b = tab[RIGHT_ORDER, slot_of(j, c, z)]
            state_v[j, i] = masked(value[:, j * M : (j + 1) * M], tab, a, b).astype(jnp.bfloat16)
    out_copies = []
    for j in range(NX):
        for to_y in range(NY):
            copy = pltpu.make_async_copy(
                state_v.at[j], send.at[j, to_y], sems_o.at[j, to_y]
            )
            copy.start()
            out_copies.append(copy)
    product(None)
    for i, out in enumerate((keep0, keep1, give0, give1)):
        value = total(i).astype(jnp.bfloat16)
        for j in range(NX):
            out[j] = value[:, j * M : (j + 1) * M]
    for copy in out_copies:
        copy.wait()


def first_kernel(tab, came, out, sem):
    x, c, z, y, h = here()
    copies = []
    for from_x in range(NX):
        for from_y in range(NY):
            for i in range(4):
                core = c if i < 2 else 1 - c
                slot = slot_of(from_x, core, z + shift_of(tab, from_y, core, i % 2))
                a = tab[LEFT_ORDER, slot]
                place = (from_x * NY + from_y) * 4 + i
                copy = pltpu.make_async_copy(came.at[place], out.at[a], sem.at[place])
                copy.start()
                copies.append(copy)
    for copy in copies:
        copy.wait()


def pack_kernel(tab, keep0, keep1, give0, give1, out, sems):
    x, c, z, y, h = here()
    work = []
    for n, (keep, give) in enumerate(((keep0, give0), (keep1, give1))):
        from_z = z - shift_of(tab, y, c, n)
        for source, from_c in ((keep, c), (give, 1 - c)):
            for from_x in range(NX):
                b = tab[RIGHT_ORDER, slot_of(from_x, from_c, from_z)]
                group = b // 8
                wanted = lax.rem(group, NH) == h
                copy = pltpu.make_async_copy(
                    source.at[from_x], out.at[group // NH, lax.rem(b, 8)], sems.at[len(work)]
                )
                work.append((wanted, copy))
    for wanted, copy in work:
        pl.when(wanted)(copy.start)
    for wanted, copy in work:
        pl.when(wanted)(copy.wait)


def second_kernel(tab, arrived, out, sems):
    x, c, z, y, h = here()
    a = tab[LEFT_ORDER, slot_of(x, c, z)]
    mine = y * NH + h

    def visit(slot, carry):
        b = tab[RIGHT_ORDER, slot]
        from_y = tab[HOLDERS, c * NZ + lax.rem(z - lax.rem(slot, NZ) + NZ, NZ)]
        q = lax.rem(b, 8)

        @pl.when(b // 8 == mine)
        def _():
            pltpu.make_async_copy(arrived.at[from_y, q], out.at[q], sems.at[q]).start()

        return carry

    lax.fori_loop(0, 64, visit, 0)
    for q in range(8):
        pltpu.make_async_copy(arrived.at[0, q], out.at[q], sems.at[q]).wait()
        out[q] = masked(out[q], tab, a, mine * 8 + q).astype(jnp.bfloat16)


ANY = pl.BlockSpec(memory_space=pl.ANY)
VMEM = pl.BlockSpec(memory_space=pltpu.VMEM)
SMEM = pl.BlockSpec(memory_space=pltpu.SMEM)
DMA = pltpu.SemaphoreType.DMA


def blocks(*shape):
    return jax.ShapeDtypeStruct(shape + (M, M), jnp.bfloat16)


def call(kernel, name, inputs, out_shape, out_specs, scratch, flops=0, size=0, vmem=32 << 20):
    return pl.pallas_call(
        kernel,
        name=name,
        out_shape=out_shape,
        in_specs=[SMEM] + [ANY] * (len(inputs) - 1),
        out_specs=out_specs,
        scratch_shapes=scratch,
        cost_estimate=pl.CostEstimate(flops=flops, bytes_accessed=size, transcendentals=0),
        compiler_params=pltpu.CompilerParams(vmem_limit_bytes=vmem),
    )(*inputs)


def on_device(
    psi, left_ops, right_ops, left_order, right_order, left_qn, right_qn, left_dims, right_dims
):
    h = lax.axis_index("h")
    tab = jnp.concatenate(
        [
            jnp.stack([left_order, right_order, left_qn, right_qn, left_dims, right_dims]),
            jnp.asarray(CONSTANT_ROWS),
        ]
    )

    with jax.named_scope("half_exchange"):
        left_own, right_own = left_ops[:, 0], right_ops[:, 0]
        left_other = permute(left_own, lambda c, z, y: (c, z + 8))
        right_other = permute(right_own, lambda c, z, y: (c, z + 8))

    def both(own, other):
        return jnp.where(
            h == 0, jnp.concatenate([own, other], 0), jnp.concatenate([other, own], 0)
        )

    with jax.named_scope("psi_shift"):
        packed = call(
            psi_kernel, "psi_pack", (tab, psi[0]), [blocks(NX)] * 4, [VMEM] * 4, [DMA((16,))],
            size=1 << 20,
        )
        starts = []
        for part in range(2):
            for n in range(2):
                starts.append(
                    permute(
                        packed[2 * part + n],
                        lambda c, z, y: (c ^ part, z - int(SHIFT[y, c, n])),
                    )
                )

    with jax.named_scope("left_over_y"):
        left4 = both(left_own, left_other)
        left16 = lax.all_to_all(
            jnp.broadcast_to(left4[None], (NY,) + left4.shape), "y", 0, 0, tiled=True
        ).reshape(NK, M, M)
    with jax.named_scope("left_shift"):
        left_kept = [
            permute(left16, lambda c, z, y: (c, z - int(SHIFT[y, c, n]))) for n in range(2)
        ]
    with jax.named_scope("left_core"):
        left_got = [permute(value, lambda c, z, y: (1 - c, z)) for value in left_kept]
    with jax.named_scope("right_over_xy"):
        right4 = both(right_own, right_other)
        right4, left16 = lax.optimization_barrier((right4, left16))
        right = lax.all_to_all(
            jnp.broadcast_to(right4[None], (NX * NY,) + right4.shape), ("x", "y"), 0, 0, tiled=True
        ).reshape(NX, NK, M, M)

    with jax.named_scope("products"):
        sent, *seconds = call(
            products_kernel,
            "products",
            (tab, *left_kept, *left_got, right, *starts),
            [blocks(NX, NY, 4)] + [blocks(NX)] * 4,
            [ANY] + [VMEM] * 4,
            [
                pltpu.VMEM((4, M, NK * M), jnp.bfloat16),
                pltpu.VMEM((NX, NK, M, M), jnp.bfloat16),
                pltpu.VMEM((NX, 4, M, M), jnp.bfloat16),
                pltpu.VMEM((4, NK * M, NX * M), jnp.bfloat16),
                DMA((4, NK)), DMA((NX,)), DMA((4,)), DMA((NX, NY)),
            ],
            flops=2 * 2 * 16 * NK * 2 * M**3,
            size=8 << 20,
            vmem=48 << 20,
        )
    with jax.named_scope("first_out"):
        came = lax.all_to_all(
            sent.reshape(NX * NY, 4, M, M), ("x", "y"), 0, 0, tiled=True
        ).reshape(64, M, M)
    with jax.named_scope("second_shift"):
        back = []
        for part in range(2):
            for n in range(2):
                back.append(
                    permute(
                        seconds[2 * part + n],
                        lambda c, z, y: (c ^ part, z + int(SHIFT[y, c ^ part, n])),
                    )
                )
    with jax.named_scope("second_over_y"):
        gathered = call(
            pack_kernel, "second_pack", (tab, *back), blocks(NY, 8), ANY, [DMA((16,))],
            size=1 << 20,
        )
        gathered, came = lax.optimization_barrier((gathered, came))
        arrived = lax.all_to_all(gathered, "y", 0, 0, tiled=True)
    with jax.named_scope("first_order"):
        first_out = call(
            first_kernel, "first_order", (tab, came), blocks(64), ANY, [DMA((64,))], size=4 << 20
        )
    with jax.named_scope("second_pick"):
        second_out = call(
            second_kernel, "second_pick", (tab, arrived), blocks(8), VMEM, [DMA((8,))],
            size=1 << 19,
        )
    return first_out[None], second_out[None]


def solution(mesh):
    fine = Mesh(mesh.devices.reshape(NX, NC, NZ, NY, NH), AXES)
    slots, ops = P(SLOT), P(("y", "h"), SLOT)
    return jax.shard_map(
        on_device,
        mesh=fine,
        in_specs=(slots, ops, ops, P(), P(), P(), P(), P(), P()),
        out_specs=(slots, P(SLOT, ("y", "h"))),
        check_vma=False,
    )
```

time: 966 us -> 189 us (0.20)
  waiting for transfers between devices: 874 us -> 47.4 us
  starting transfers between devices: 25.5 us -> 109 us
  Pallas kernels: 0 us -> 22.7 us
  between operations: 18.2 us -> 0.99 us
  local copies, waits for them, and re-layouts: 19.5 us -> 5.74 us
  matrix products: 13.3 us -> 0 us
  other arithmetic: 14.9 us -> 1.87 us
    psum x1 -> x0, waiting for transfers between devices: 363 us -> none  [on_device(): lax.psum(partial_value.astype(jnp.bfloat16), 'ops').astype(jnp.float32)]
    all_to_all x2 -> x4, waiting for transfers between devices: 372 us -> 15.9 us  [the longest x1 12.4 us: on_device(): arrived = lax.all_to_all(gathered, 'y', 0, 0, tiled=True)]
    reduce_scatter x1 -> x0, waiting for transfers between devices: 139 us -> none  [on_device(): lax.psum_scatter(second_partial.astype(jnp.bfloat16), 'ops', scatter_dime...]
    ppermute x0 -> x14, starting transfers between devices: none -> 86.5 us  [permute(): return lax.ppermute(value, AXES, pairs)]
    ppermute x0 -> x14, waiting for transfers between devices: none -> 31.5 us  [permute(): return lax.ppermute(value, AXES, pairs)]
    pallas_call x0 -> x5, Pallas kernels: none -> 22.7 us  [call(): pl.pallas_call(kernel, name=name, out_shape=out_shape, in_specs=[SMEM] +...]
    dot_general x4 -> x0, matrix products: 13.3 us -> none  [the longest x1 3.43 us: on_device(): jnp.einsum('kixy,kzy->ixz', arrived, right_here, preferred_element_type=j...]
    all_to_all x2 -> x4, starting transfers between devices: 25.4 us -> 22.5 us  [the longest x1 7.64 us: on_device(): lax.all_to_all(sent.reshape(NX * NY, 4, M, M), ('x', 'y'), 0, 0, tiled=True)]
  transfers between devices with their start and end apart: 4 -> 18, of which waited for: 4 -> 7; matrix products, arithmetic and copies ran while one was open for 1% -> 1% of each run, Pallas kernels for 0% -> 3%
where the time goes in v2:
time: 189 us; the launch traced here: 188 us
  starting transfers between devices  109 us (58%)
  waiting for transfers between devices  47.4 us (25%)
  Pallas kernels  22.7 us (12%)
  local copies, waits for them, and re-layouts  5.74 us (3%)
    ppermute x14, starting transfers between devices, permute(): return lax.ppermute(value, AXES, pairs)  86.5 us
    ppermute x14, waiting for transfers between devices, permute(): return lax.ppermute(value, AXES, pairs)  31.5 us
    pallas_call x5, Pallas kernels, call(): pl.pallas_call(kernel, name=name, out_shape=out_shape, in_specs=[SMEM] +...  22.7 us
    all_to_all x1, waiting for transfers between devices, on_device(): arrived = lax.all_to_all(gathered, 'y', 0, 0, tiled=True)  12.4 us
    all_to_all x1, starting transfers between devices, on_device(): lax.all_to_all(sent.reshape(NX * NY, 4, M, M), ('x', 'y'), 0, 0, tiled=True)  7.64 us
    all_to_all x1, starting transfers between devices, on_device(): lax.all_to_all(jnp.broadcast_to(right4[None], (NX * NY,) + right4.shape),...  7 us
    all_to_all x1, starting transfers between devices, on_device(): lax.all_to_all(jnp.broadcast_to(left4[None], (NY,) + left4.shape), 'y', 0...  4.18 us
  transfers between devices with their start and end apart: 18, of which 7 were waited for; matrix products, arithmetic and copies ran while one was open for 1% of the time, Pallas kernels for 3%

profile of v2, /device:TPU:1, one launch (start us, length us, event | category | flops | bytes accessed | tf_op | source)
XLA Modules:
  0.0 187.7 jit_solution(3107144403554417144)
XLA Ops:
  0.6 16.3 %collective-permute-start = (bf16[2,128,128]{2,1,0:T(8,128)(2,1)}, bf16[2,128,128]{2,1,0:T(8,128)(2,1)S(1)}, u32[]{:S(2)}, u32[]{:S(2)}) collective-permute-start(bf16[2,128,128]{2,1,0:T(8,128)(2,1)} %bitcast.20), channel_id=1, source_target_pairs={{0,1},{2,3},{4,5},{6,7},{8,9},{10,11},{12,13},{14,15},{16,17},{18,... | collective-permute-start | bytes 196616 | tf_op jit(solution)/shard_map/half_exchange/ppermute | solution.py:48
  16.9 2.1 %collective-permute-done = bf16[2,128,128]{2,1,0:T(8,128)(2,1)S(1)} collective-permute-done((bf16[2,128,128]{2,1,0:T(8,128)(2,1)}, bf16[2,128,128]{2,1,0:T(8,128)(2,1)S(1)}, u32[]{:S(2)}, u32[]{:S(2)}) %collective-permute-start) | collective-permute-done | bytes 65568 | tf_op jit(solution)/shard_map/half_exchange/ppermute | solution.py:48
  19.0 0.9 maximum_select_fusion
  19.9 0.9 broadcast_in_dim.8
  20.8 4.2 %all-to-all-start = ((bf16[4,4,128,128]{3,2,1,0:T(8,128)(2,1)}), bf16[4,4,128,128]{3,2,1,0:T(8,128)(2,1)}, u32[]{:S(2)}, u32[]{:S(2)}) async-start(bf16[4,4,128,128]{3,2,1,0:T(8,128)(2,1)} %broadcast_in_dim.8), calls=%async_computation | async-start | bytes 1048576 | tf_op jit(solution)/shard_map/left_over_y/all_to_all | solution.py:284
  25.0 11.9 %collective-permute-start.5 = (bf16[2,128,128]{2,1,0:T(8,128)(2,1)}, bf16[2,128,128]{2,1,0:T(8,128)(2,1)S(1)}, u32[]{:S(2)}, u32[]{:S(2)}) collective-permute-start(bf16[2,128,128]{2,1,0:T(8,128)(2,1)} %bitcast.22), channel_id=1, source_target_pairs={{0,1},{2,3},{4,5},{6,7},{8,9},{10,11},{12,13},{14,15},{16,17},{18,... | collective-permute-start | bytes 196616 | tf_op jit(solution)/shard_map/half_exchange/ppermute | solution.py:48
  36.9 2.1 %collective-permute-done.5 = bf16[2,128,128]{2,1,0:T(8,128)(2,1)S(1)} collective-permute-done((bf16[2,128,128]{2,1,0:T(8,128)(2,1)}, bf16[2,128,128]{2,1,0:T(8,128)(2,1)S(1)}, u32[]{:S(2)}, u32[]{:S(2)}) %collective-permute-start.5) | collective-permute-done | bytes 65568 | tf_op jit(solution)/shard_map/half_exchange/ppermute | solution.py:48
  39.0 0.9 maximum_select_fusion.1
  40.0 0.0 all-to-all-done
  40.0 1.8 broadcast_in_dim.9
  41.8 0.0 copy-start.9
  41.8 0.0 copy-start.10
  41.8 0.0 copy-start.11
  41.8 0.0 copy-start.1
  41.8 7.0 %all-to-all-start.1 = ((bf16[16,4,128,128]{3,2,1,0:T(8,128)(2,1)}), bf16[16,4,128,128]{3,2,1,0:T(8,128)(2,1)}, u32[]{:S(2)}, u32[]{:S(2)}) async-start(bf16[16,4,128,128]{3,2,1,0:T(8,128)(2,1)} %broadcast_in_dim.9), calls=%async_computation.1 | async-start | bytes 4194304 | tf_op jit(solution)/shard_map/right_over_xy/all_to_all | solution.py:296
  48.9 5.2 %collective-permute-start.2 = (bf16[16,128,128]{2,1,0:T(8,128)(2,1)}, bf16[16,128,128]{2,1,0:T(8,128)(2,1)S(1)}, u32[]{:S(2)}, u32[]{:S(2)}) collective-permute-start(bf16[16,128,128]{2,1,0:T(8,128)(2,1)} %bitcast.7), channel_id=1, source_target_pairs={{0,33},{2,26},{4,45},{6,22},{8,41},{10,34},{12,53},{14,30},{16,49}... | collective-permute-start | bytes 1572872 | tf_op jit(solution)/shard_map/left_shift/ppermute | solution.py:48
  54.0 1.7 collective-permute-start.1
  55.7 14.0 %collective-permute-done.2.lo1 = bf16[16,128,128]{2,1,0:T(8,128)(2,1)S(1)} collective-permute-done((bf16[16,128,128]{2,1,0:T(8,128)(2,1)}, bf16[16,128,128]{2,1,0:T(8,128)(2,1)S(1)}, u32[]{:S(2)}, u32[]{:S(2)}) %collective-permute-start.2) | collective-permute-done | bytes 524320 | tf_op jit(solution)/shard_map/left_shift/ppermute | solution.py:48
  69.8 10.1 %collective-permute-start.4 = (bf16[16,128,128]{2,1,0:T(8,128)(2,1)S(1)}, bf16[16,128,128]{2,1,0:T(8,128)(2,1)}, u32[]{:S(2)}, u32[]{:S(2)}) collective-permute-start(bf16[16,128,128]{2,1,0:T(8,128)(2,1)S(1)} %collective-permute-done.2.lo1), channel_id=1, source_target_pairs={{0,64},{2,66},{4,68},{6,70},{8,72},{10,74},{12,76},{14,78},{16,80}... | collective-permute-start | bytes 1572872 | tf_op jit(solution)/shard_map/left_core/ppermute | solution.py:48
  79.9 0.0 collective-permute-done.1.lo0
  79.9 1.9 %collective-permute-start.3 = (bf16[16,128,128]{2,1,0:T(8,128)(2,1)S(1)}, bf16[16,128,128]{2,1,0:T(8,128)(2,1)}, u32[]{:S(2)}, u32[]{:S(2)}) collective-permute-start(bf16[16,128,128]{2,1,0:T(8,128)(2,1)S(1)} %collective-permute-done.1.lo0), channel_id=1, source_target_pairs={{0,64},{2,66},{4,68},{6,70},{8,72},{10,74},{12,76},{14,78},{16,80}... | collective-permute-start | bytes 1572872 | tf_op jit(solution)/shard_map/left_core/ppermute | solution.py:48
  81.9 1.9 psi_pack.1
  83.8 0.7 collective-permute-start.6
  84.4 8.9 %collective-permute-start.7 = (bf16[4,128,128]{2,1,0:T(8,128)(2,1)S(1)}, bf16[4,128,128]{2,1,0:T(8,128)(2,1)S(1)}, u32[]{:S(2)}, u32[]{:S(2)}) collective-permute-start(bf16[4,128,128]{2,1,0:T(8,128)(2,1)S(1)} %get-tuple-element.16), channel_id=1, source_target_pairs={{0,33},{2,26},{4,45},{6,22},{8,41},{10,34},{12,53},{14,30},{16,49}... | collective-permute-start | bytes 393224 | tf_op jit(solution)/shard_map/psi_shift/ppermute | solution.py:48
  93.4 4.1 %collective-permute-start.8 = (bf16[4,128,128]{2,1,0:T(8,128)(2,1)S(1)}, bf16[4,128,128]{2,1,0:T(8,128)(2,1)S(1)}, u32[]{:S(2)}, u32[]{:S(2)}) collective-permute-start(bf16[4,128,128]{2,1,0:T(8,128)(2,1)S(1)} %get-tuple-element.17), channel_id=1, source_target_pairs={{0,64},{2,123},{4,76},{6,119},{8,72},{10,66},{12,84},{14,127},{16,... | collective-permute-start | bytes 393224 | tf_op jit(solution)/shard_map/psi_shift/ppermute | solution.py:48
  97.5 0.0 collective-permute-done.6.so0
  97.5 11.3 %collective-permute-start.9 = (bf16[4,128,128]{2,1,0:T(8,128)(2,1)S(1)}, bf16[4,128,128]{2,1,0:T(8,128)(2,1)S(1)}, u32[]{:S(2)}, u32[]{:S(2)}) collective-permute-start(bf16[4,128,128]{2,1,0:T(8,128)(2,1)S(1)} %get-tuple-element.18), channel_id=1, source_target_pairs={{0,97},{2,90},{4,109},{6,86},{8,105},{10,98},{12,117},{14,94},{16,... | collective-permute-start | bytes 393224 | tf_op jit(solution)/shard_map/psi_shift/ppermute | solution.py:48
  108.9 0.0 collective-permute-done.8.sx0
  108.9 4.1 %collective-permute-done.9.sx1 = bf16[4,128,128]{2,1,0:T(8,128)(2,1)S(1)} collective-permute-done((bf16[4,128,128]{2,1,0:T(8,128)(2,1)S(1)}, bf16[4,128,128]{2,1,0:T(8,128)(2,1)S(1)}, u32[]{:S(2)}, u32[]{:S(2)}) %collective-permute-start.9) | collective-permute-done | bytes 131104 | tf_op jit(solution)/shard_map/psi_shift/ppermute | solution.py:48
  113.0 0.0 all-to-all-done.1
  113.0 13.5 %products.1 = (bf16[4,4,4,128,128]{4,3,2,1,0:T(8,128)(2,1)S(1)}, bf16[4,128,128]{2,1,0:T(8,128)(2,1)S(1)}, bf16[4,128,128]{2,1,0:T(8,128)(2,1)S(1)}, bf16[4,128,...) custom-call(s32[8,64]{1,0:T(8,128)S(1)} %concatenate.25.tab, bf16[16,128,128]{2,1,0:T(8,128)(2,1)S(1)} %collective-permute-done.1.lo0, ...), custom_call_target="tpu_custom_call" | custom-call | flops 4294967296 | bytes 8388608 | tf_op jit(solution)/shard_map/products/products/pallas_call | solution.py:234
  126.6 0.0 copy-start.2
  126.6 1.3 copy-done.2
  127.9 0.7 copy-done.3
  128.6 7.6 %all-to-all-start.2 = ((bf16[16,4,128,128]{3,2,1,0:T(8,128)(2,1)}), bf16[16,4,128,128]{3,2,1,0:T(8,128)(2,1)S(1)}, u32[]{:S(2)}, u32[]{:S(2)}) async-start(bf16[16,4,128,128]{3,2,1,0:T(8,128)(2,1)} %bitcast.17), calls=%async_computation.2 | async-start | bytes 4194304 | tf_op jit(solution)/shard_map/first_out/all_to_all | solution.py:319
  136.2 0.7 collective-permute-start.10
  136.9 6.3 %collective-permute-start.11 = (bf16[4,128,128]{2,1,0:T(8,128)(2,1)S(1)}, bf16[4,128,128]{2,1,0:T(8,128)(2,1)S(1)}, u32[]{:S(2)}, u32[]{:S(2)}) collective-permute-start(bf16[4,128,128]{2,1,0:T(8,128)(2,1)S(1)} %get-tuple-element.20), channel_id=1, source_target_pairs={{0,32},{2,43},{4,28},{6,55},{8,40},{10,51},{12,36},{14,63},{16,48}... | collective-permute-start | bytes 393224 | tf_op jit(solution)/shard_map/second_shift/ppermute | solution.py:48
  143.2 1.9 %collective-permute-start.12 = (bf16[4,128,128]{2,1,0:T(8,128)(2,1)S(1)}, bf16[4,128,128]{2,1,0:T(8,128)(2,1)S(1)}, u32[]{:S(2)}, u32[]{:S(2)}) collective-permute-start(bf16[4,128,128]{2,1,0:T(8,128)(2,1)S(1)} %get-tuple-element.21), channel_id=1, source_target_pairs={{0,64},{2,123},{4,76},{6,119},{8,72},{10,66},{12,84},{14,127},{16,... | collective-permute-start | bytes 393224 | tf_op jit(solution)/shard_map/second_shift/ppermute | solution.py:48
  145.1 5.5 %collective-permute-start.13 = (bf16[4,128,128]{2,1,0:T(8,128)(2,1)S(1)}, bf16[4,128,128]{2,1,0:T(8,128)(2,1)S(1)}, u32[]{:S(2)}, u32[]{:S(2)}) collective-permute-start(bf16[4,128,128]{2,1,0:T(8,128)(2,1)S(1)} %get-tuple-element.22), channel_id=1, source_target_pairs={{0,97},{2,90},{4,109},{6,86},{8,105},{10,98},{12,117},{14,94},{16,... | collective-permute-start | bytes 393224 | tf_op jit(solution)/shard_map/second_shift/ppermute | solution.py:48
  150.6 0.0 collective-permute-done.10.keep0
  150.7 9.2 %collective-permute-done.13.give1 = bf16[4,128,128]{2,1,0:T(8,128)(2,1)S(1)} collective-permute-done((bf16[4,128,128]{2,1,0:T(8,128)(2,1)S(1)}, bf16[4,128,128]{2,1,0:T(8,128)(2,1)S(1)}, u32[]{:S(2)}, u32[]{:S(2)}) %collective-permute-start.13) | collective-permute-done | bytes 131104 | tf_op jit(solution)/shard_map/second_shift/ppermute | solution.py:48
  159.8 1.4 second_pack.1
  161.3 1.0 copy-done
  162.2 3.4 %all-to-all-done.2 = bf16[16,4,128,128]{3,2,1,0:T(8,128)(2,1)S(1)} async-done(((bf16[16,4,128,128]{3,2,1,0:T(8,128)(2,1)}), bf16[16,4,128,128]{3,2,1,0:T(8,128)(2,1)S(1)}, u32[]{:S(2)}, u32[]{:S(2)}) %all-to-all-start.2) | async-done | bytes 2097184 | tf_op jit(solution)/shard_map/first_out/all_to_all | solution.py:319
  165.7 3.7 %all-to-all-start.3 = ((bf16[4,8,128,128]{3,2,1,0:T(8,128)(2,1)}), bf16[4,8,128,128]{3,2,1,0:T(8,128)(2,1)S(1)}, u32[]{:S(2)}, u32[]{:S(2)}) async-start(bf16[4,8,128,128]{3,2,1,0:T(8,128)(2,1)} %copy-done), calls=%async_computation.3 | async-start | bytes 2097152 | tf_op jit(solution)/shard_map/second_over_y/all_to_all | solution.py:338
  169.4 2.5 %first_order.1 = bf16[64,128,128]{2,1,0:T(8,128)(2,1)} custom-call(s32[8,64]{1,0:T(8,128)S(1)} %concatenate.25.tab, bf16[64,128,128]{2,1,0:T(8,128)(2,1)S(1)} %bitcast.15), custom_call_target="tpu_custom_call" | custom-call | bytes 4194304 | tf_op jit(solution)/shard_map/first_order/first_order/pallas_call | solution.py:234
  171.8 12.4 %all-to-all-done.3.arrived = bf16[4,8,128,128]{3,2,1,0:T(8,128)(2,1)S(1)} async-done(((bf16[4,8,128,128]{3,2,1,0:T(8,128)(2,1)}), bf16[4,8,128,128]{3,2,1,0:T(8,128)(2,1)S(1)}, u32[]{:S(2)}, u32[]{:S(2)}) %all-to-all-start.3) | async-done | bytes 1048608 | tf_op jit(solution)/shard_map/second_over_y/all_to_all | solution.py:338
  184.3 3.4 %second_pick.1 = bf16[8,128,128]{2,1,0:T(8,128)(2,1)} custom-call(s32[8,64]{1,0:T(8,128)S(1)} %concatenate.25.tab, bf16[4,8,128,128]{3,2,1,0:T(8,128)(2,1)S(1)} %all-to-all-done.3.arrived), custom_call_target="tpu_custom_call" | custom-call | bytes 524288 | tf_op jit(solution)/shard_map/second_pick/second_pick/pallas_call | solution.py:234
  (22 shorter events, 0.1 us)
Async XLA Ops:
  0.6 18.3 %collective-permute-start = (bf16[2,128,128]{2,1,0:T(8,128)(2,1)}, bf16[2,128,128]{2,1,0:T(8,128)(2,1)S(1)}, u32[]{:S(2)}, u32[]{:S(2)}) collective-permute-start(bf16[2,128,128]{2,1,0:T(8,128)(2,1)} %bitcast.20), channel_id=1, source_target_pairs={{0,1},{2,3},{4,5},{6,7},{8,9},{10,11},{12,13},{14,15},{16,17},{18,... | collective-permute-start | bytes 196616 | tf_op jit(solution)/shard_map/half_exchange/ppermute | solution.py:48
  20.8 19.2 %all-to-all-start = ((bf16[4,4,128,128]{3,2,1,0:T(8,128)(2,1)}), bf16[4,4,128,128]{3,2,1,0:T(8,128)(2,1)}, u32[]{:S(2)}, u32[]{:S(2)}) async-start(bf16[4,4,128,128]{3,2,1,0:T(8,128)(2,1)} %broadcast_in_dim.8), calls=%async_computation | async-start | bytes 1048576 | tf_op jit(solution)/shard_map/left_over_y/all_to_all | solution.py:284
  25.0 14.0 %collective-permute-start.5 = (bf16[2,128,128]{2,1,0:T(8,128)(2,1)}, bf16[2,128,128]{2,1,0:T(8,128)(2,1)S(1)}, u32[]{:S(2)}, u32[]{:S(2)}) collective-permute-start(bf16[2,128,128]{2,1,0:T(8,128)(2,1)} %bitcast.22), channel_id=1, source_target_pairs={{0,1},{2,3},{4,5},{6,7},{8,9},{10,11},{12,13},{14,15},{16,17},{18,... | collective-permute-start | bytes 196616 | tf_op jit(solution)/shard_map/half_exchange/ppermute | solution.py:48
  41.8 40.0 %copy-start.5 = (s32[2,64]{1,0:T(2,128)S(1)}, s32[2,64]{1,0:T(2,128)}, u32[]{:S(2)}) copy-start(s32[2,64]{1,0:T(2,128)} %constant.8.clone) | copy-start | bytes 1540
  41.8 40.0 %copy-start.6 = (s32[64]{0:T(128)S(1)}, s32[64]{0:T(128)}, u32[]{:S(2)}) copy-start(s32[64]{0:T(128)} %param.13) | copy-start | bytes 772
  41.8 40.0 %copy-start.7 = (s32[64]{0:T(128)S(1)}, s32[64]{0:T(128)}, u32[]{:S(2)}) copy-start(s32[64]{0:T(128)} %param.14) | copy-start | bytes 772
  41.8 40.0 %copy-start.8 = (s32[64]{0:T(128)S(1)}, s32[64]{0:T(128)}, u32[]{:S(2)}) copy-start(s32[64]{0:T(128)} %param.15) | copy-start | bytes 772
  41.8 40.0 %copy-start.9 = (s32[64]{0:T(128)S(1)}, s32[64]{0:T(128)}, u32[]{:S(2)}) copy-start(s32[64]{0:T(128)} %param.16) | copy-start | bytes 772
  41.8 40.0 %copy-start.10 = (s32[64]{0:T(128)S(1)}, s32[64]{0:T(128)}, u32[]{:S(2)}) copy-start(s32[64]{0:T(128)} %param.17) | copy-start | bytes 772
  41.8 40.0 %copy-start.11 = (s32[64]{0:T(128)S(1)}, s32[64]{0:T(128)}, u32[]{:S(2)}) copy-start(s32[64]{0:T(128)} %param.18) | copy-start | bytes 772
  41.8 40.1 %copy-start.1 = (bf16[1,64,128,128]{3,2,1,0:T(8,128)(2,1)S(1)}, bf16[1,64,128,128]{3,2,1,0:T(8,128)(2,1)}, u32[]{:S(2)}) copy-start(bf16[1,64,128,128]{3,2,1,0:T(8,128)(2,1)} %param.10) | copy-start | bytes 6291460
  41.8 71.2 %all-to-all-start.1 = ((bf16[16,4,128,128]{3,2,1,0:T(8,128)(2,1)}), bf16[16,4,128,128]{3,2,1,0:T(8,128)(2,1)}, u32[]{:S(2)}, u32[]{:S(2)}) async-start(bf16[16,4,128,128]{3,2,1,0:T(8,128)(2,1)} %broadcast_in_dim.9), calls=%async_computation.1 | async-start | bytes 4194304 | tf_op jit(solution)/shard_map/right_over_xy/all_to_all | solution.py:296
  48.9 20.9 %collective-permute-start.2 = (bf16[16,128,128]{2,1,0:T(8,128)(2,1)}, bf16[16,128,128]{2,1,0:T(8,128)(2,1)S(1)}, u32[]{:S(2)}, u32[]{:S(2)}) collective-permute-start(bf16[16,128,128]{2,1,0:T(8,128)(2,1)} %bitcast.7), channel_id=1, source_target_pairs={{0,33},{2,26},{4,45},{6,22},{8,41},{10,34},{12,53},{14,30},{16,49}... | collective-permute-start | bytes 1572872 | tf_op jit(solution)/shard_map/left_shift/ppermute | solution.py:48
  54.0 25.8 %collective-permute-start.1 = (bf16[16,128,128]{2,1,0:T(8,128)(2,1)}, bf16[16,128,128]{2,1,0:T(8,128)(2,1)S(1)}, u32[]{:S(2)}, u32[]{:S(2)}) collective-permute-start(bf16[16,128,128]{2,1,0:T(8,128)(2,1)} %bitcast.7), channel_id=1, source_target_pairs={{0,0},{2,59},{4,12},{6,55},{8,8},{10,2},{12,20},{14,63},{16,16},{1... | collective-permute-start | bytes 1572872 | tf_op jit(solution)/shard_map/left_shift/ppermute | solution.py:48
  69.8 43.3 %collective-permute-start.4 = (bf16[16,128,128]{2,1,0:T(8,128)(2,1)S(1)}, bf16[16,128,128]{2,1,0:T(8,128)(2,1)}, u32[]{:S(2)}, u32[]{:S(2)}) collective-permute-start(bf16[16,128,128]{2,1,0:T(8,128)(2,1)S(1)} %collective-permute-done.2.lo1), channel_id=1, source_target_pairs={{0,64},{2,66},{4,68},{6,70},{8,72},{10,74},{12,76},{14,78},{16,80}... | collective-permute-start | bytes 1572872 | tf_op jit(solution)/shard_map/left_core/ppermute | solution.py:48
  79.9 33.2 %collective-permute-start.3 = (bf16[16,128,128]{2,1,0:T(8,128)(2,1)S(1)}, bf16[16,128,128]{2,1,0:T(8,128)(2,1)}, u32[]{:S(2)}, u32[]{:S(2)}) collective-permute-start(bf16[16,128,128]{2,1,0:T(8,128)(2,1)S(1)} %collective-permute-done.1.lo0), channel_id=1, source_target_pairs={{0,64},{2,66},{4,68},{6,70},{8,72},{10,74},{12,76},{14,78},{16,80}... | collective-permute-start | bytes 1572872 | tf_op jit(solution)/shard_map/left_core/ppermute | solution.py:48
  83.8 13.7 %collective-permute-start.6 = (bf16[4,128,128]{2,1,0:T(8,128)(2,1)S(1)}, bf16[4,128,128]{2,1,0:T(8,128)(2,1)S(1)}, u32[]{:S(2)}, u32[]{:S(2)}) collective-permute-start(bf16[4,128,128]{2,1,0:T(8,128)(2,1)S(1)} %get-tuple-element.15), channel_id=1, source_target_pairs={{0,0},{2,59},{4,12},{6,55},{8,8},{10,2},{12,20},{14,63},{16,16},{1... | collective-permute-start | bytes 393224 | tf_op jit(solution)/shard_map/psi_shift/ppermute | solution.py:48
  84.4 24.4 %collective-permute-start.7 = (bf16[4,128,128]{2,1,0:T(8,128)(2,1)S(1)}, bf16[4,128,128]{2,1,0:T(8,128)(2,1)S(1)}, u32[]{:S(2)}, u32[]{:S(2)}) collective-permute-start(bf16[4,128,128]{2,1,0:T(8,128)(2,1)S(1)} %get-tuple-element.16), channel_id=1, source_target_pairs={{0,33},{2,26},{4,45},{6,22},{8,41},{10,34},{12,53},{14,30},{16,49}... | collective-permute-start | bytes 393224 | tf_op jit(solution)/shard_map/psi_shift/ppermute | solution.py:48
  93.4 15.5 %collective-permute-start.8 = (bf16[4,128,128]{2,1,0:T(8,128)(2,1)S(1)}, bf16[4,128,128]{2,1,0:T(8,128)(2,1)S(1)}, u32[]{:S(2)}, u32[]{:S(2)}) collective-permute-start(bf16[4,128,128]{2,1,0:T(8,128)(2,1)S(1)} %get-tuple-element.17), channel_id=1, source_target_pairs={{0,64},{2,123},{4,76},{6,119},{8,72},{10,66},{12,84},{14,127},{16,... | collective-permute-start | bytes 393224 | tf_op jit(solution)/shard_map/psi_shift/ppermute | solution.py:48
  97.5 15.5 %collective-permute-start.9 = (bf16[4,128,128]{2,1,0:T(8,128)(2,1)S(1)}, bf16[4,128,128]{2,1,0:T(8,128)(2,1)S(1)}, u32[]{:S(2)}, u32[]{:S(2)}) collective-permute-start(bf16[4,128,128]{2,1,0:T(8,128)(2,1)S(1)} %get-tuple-element.18), channel_id=1, source_target_pairs={{0,97},{2,90},{4,109},{6,86},{8,105},{10,98},{12,117},{14,94},{16,... | collective-permute-start | bytes 393224 | tf_op jit(solution)/shard_map/psi_shift/ppermute | solution.py:48
  126.6 1.3 copy-start.2
  127.9 0.7 copy-start.3
  128.6 7.7 %copy-start.4 = (bf16[4,128,128]{2,1,0:T(8,128)(2,1)S(1)}, bf16[4,128,128]{2,1,0:T(8,128)(2,1)}, u32[]{:S(2)}) copy-start(bf16[4,128,128]{2,1,0:T(8,128)(2,1)} %copy-done.3) | copy-start | bytes 393220
  128.6 37.1 %all-to-all-start.2 = ((bf16[16,4,128,128]{3,2,1,0:T(8,128)(2,1)}), bf16[16,4,128,128]{3,2,1,0:T(8,128)(2,1)S(1)}, u32[]{:S(2)}, u32[]{:S(2)}) async-start(bf16[16,4,128,128]{3,2,1,0:T(8,128)(2,1)} %bitcast.17), calls=%async_computation.2 | async-start | bytes 4194304 | tf_op jit(solution)/shard_map/first_out/all_to_all | solution.py:319
  136.2 14.4 %collective-permute-start.10 = (bf16[4,128,128]{2,1,0:T(8,128)(2,1)S(1)}, bf16[4,128,128]{2,1,0:T(8,128)(2,1)S(1)}, u32[]{:S(2)}, u32[]{:S(2)}) collective-permute-start(bf16[4,128,128]{2,1,0:T(8,128)(2,1)S(1)} %copy-done.4), channel_id=1, source_target_pairs={{0,0},{2,10},{4,61},{6,22},{8,8},{10,18},{12,4},{14,30},{16,16},{1... | collective-permute-start | bytes 393224 | tf_op jit(solution)/shard_map/second_shift/ppermute | solution.py:48
  136.9 13.8 %collective-permute-start.11 = (bf16[4,128,128]{2,1,0:T(8,128)(2,1)S(1)}, bf16[4,128,128]{2,1,0:T(8,128)(2,1)S(1)}, u32[]{:S(2)}, u32[]{:S(2)}) collective-permute-start(bf16[4,128,128]{2,1,0:T(8,128)(2,1)S(1)} %get-tuple-element.20), channel_id=1, source_target_pairs={{0,32},{2,43},{4,28},{6,55},{8,40},{10,51},{12,36},{14,63},{16,48}... | collective-permute-start | bytes 393224 | tf_op jit(solution)/shard_map/second_shift/ppermute | solution.py:48
  143.2 7.5 %collective-permute-start.12 = (bf16[4,128,128]{2,1,0:T(8,128)(2,1)S(1)}, bf16[4,128,128]{2,1,0:T(8,128)(2,1)S(1)}, u32[]{:S(2)}, u32[]{:S(2)}) collective-permute-start(bf16[4,128,128]{2,1,0:T(8,128)(2,1)S(1)} %get-tuple-element.21), channel_id=1, source_target_pairs={{0,64},{2,123},{4,76},{6,119},{8,72},{10,66},{12,84},{14,127},{16,... | collective-permute-start | bytes 393224 | tf_op jit(solution)/shard_map/second_shift/ppermute | solution.py:48
  145.1 14.7 %collective-permute-start.13 = (bf16[4,128,128]{2,1,0:T(8,128)(2,1)S(1)}, bf16[4,128,128]{2,1,0:T(8,128)(2,1)S(1)}, u32[]{:S(2)}, u32[]{:S(2)}) collective-permute-start(bf16[4,128,128]{2,1,0:T(8,128)(2,1)S(1)} %get-tuple-element.22), channel_id=1, source_target_pairs={{0,97},{2,90},{4,109},{6,86},{8,105},{10,98},{12,117},{14,94},{16,... | collective-permute-start | bytes 393224 | tf_op jit(solution)/shard_map/second_shift/ppermute | solution.py:48
  161.3 1.0 copy-start
  165.7 18.6 %all-to-all-start.3 = ((bf16[4,8,128,128]{3,2,1,0:T(8,128)(2,1)}), bf16[4,8,128,128]{3,2,1,0:T(8,128)(2,1)S(1)}, u32[]{:S(2)}, u32[]{:S(2)}) async-start(bf16[4,8,128,128]{3,2,1,0:T(8,128)(2,1)} %copy-done), calls=%async_computation.3 | async-start | bytes 2097152 | tf_op jit(solution)/shard_map/second_over_y/all_to_all | solution.py:338

commit v3 on v0

v3 whole, which is shorter than its diff:
```python
import functools

import jax
import jax.numpy as jnp
import numpy as np
from jax import lax
from jax.experimental import pallas as pl
from jax.experimental.pallas import tpu as pltpu
from jax.sharding import Mesh
from jax.sharding import PartitionSpec as P

SPREAD = 1
PSI_FIRST = True
OUT_FIRST = True
M = 128
NX, NC, NZ, NY, NH = 4, 2, 8, 4, 2
NK = 16
AXES = ("x", "c", "z", "y", "h")
SLOT = ("x", "c", "z")
SHIFT = np.array(
    [
        [[0, 4], [0, -4]],
        [[1, -3], [-1, 3]],
        [[-1, 3], [1, -3]],
        [[2, -2], [-2, 2]],
    ],
    np.int32,
)
HOLDER_Y = np.zeros((NC, NZ), np.int32)
for _y in range(NY):
    for _c in range(NC):
        for _n in range(2):
            HOLDER_Y[_c, SHIFT[_y, _c, _n] % NZ] = _y
LEFT_ORDER, RIGHT_ORDER, LEFT_QN, RIGHT_QN, LEFT_DIMS, RIGHT_DIMS, SHIFTS, HOLDERS = range(8)
CONSTANT_ROWS = np.zeros((2, 64), np.int32)
CONSTANT_ROWS[0, : SHIFT.size] = SHIFT.reshape(-1)
CONSTANT_ROWS[1, : HOLDER_Y.size] = HOLDER_Y.reshape(-1)


def index_of(x, c, z, y):
    return (((x * NC + c) * NZ + z % NZ) * NY + y) * NH + (z // NZ) % NH


def permute(value, target):
    pairs = []
    for x in range(NX):
        for c in range(NC):
            for z in range(NZ * NH):
                for y in range(NY):
                    pairs.append((index_of(x, c, z, y), index_of(*target(x, c, z, y))))
    return lax.ppermute(value, AXES, pairs)


def from_half(value):
    return permute(value, lambda x, c, z, y: (x, c, z + 8, y))


def from_core(value):
    return permute(value, lambda x, c, z, y: (x, 1 - c, z, y))


def from_x(value, r):
    return permute(value, lambda x, c, z, y: ((x - r) % NX, c, z, y))


def from_y(value, r):
    return permute(value, lambda x, c, z, y: (x, c, z, (y - r) % NY))


def from_shift(value, n):
    return permute(value, lambda x, c, z, y: (x, c, z - int(SHIFT[y, c, n]), y))


def to_shift(value, n):
    return permute(value, lambda x, c, z, y: (x, c, z + int(SHIFT[y, c, n]), y))


def here():
    return tuple(lax.axis_index(name) for name in AXES)


def shift_of(tab, y, c, n):
    return tab[SHIFTS, (y * NC + c) * 2 + n]


def slot_of(x, c, z):
    return (x * NC + c) * NZ + lax.rem(z + 2 * NZ, NZ)


def limits(tab, a, b):
    allowed = jnp.abs(tab[LEFT_QN, a] - tab[RIGHT_QN, b]) <= SPREAD
    return jnp.where(allowed, tab[LEFT_DIMS, a], 0), tab[RIGHT_DIMS, b]


def masked(block, tab, a, b):
    rows, cols = limits(tab, a, b)
    row = lax.broadcasted_iota(jnp.int32, (M, M), 0)
    col = lax.broadcasted_iota(jnp.int32, (M, M), 1)
    return jnp.where((row < rows) & (col < cols), block.astype(jnp.float32), 0.0)


def right_sector(tab, x, c, z, j):
    return tab[RIGHT_ORDER, slot_of(lax.rem(x + j % NX, NX), c if j < NX else 1 - c, z)]


def terms_kernel(*refs):
    x, c, z, y, h = here()
    left, right = refs[-2:]
    for r in range(NY):
        for half in range(2):
            source = refs[2 * r + half]
            place = lax.rem(y + r, NY) * 4 + 2 * (h if half == 0 else 1 - h)
            for k in range(2):
                left[place + k] = source[k]
                right[place + k] = source[2 + k]


def sent_kernel(keep, got, out):
    x = lax.axis_index("x")
    for r in range(NX):
        to_x = lax.rem(x + r, NX)
        for to_y in range(NY):
            for n in range(2):
                out[to_x * NY + to_y, n] = keep[r, n]
                out[to_x * NY + to_y, 2 + n] = got[r, n]


def psi_kernel(tab, psi, out0, out1):
    x, c, z, y, h = here()
    a = tab[LEFT_ORDER, slot_of(x, c, z)]
    for n, out in enumerate((out0, out1)):
        to_z = z - shift_of(tab, y, c, n)
        for j in range(2 * NX):
            b = right_sector(tab, x, c, to_z, j)
            out[j] = masked(psi[b], tab, a, b).astype(jnp.bfloat16)


def product(state_of, left, right, inner):
    for j in range(2 * NX):
        for group in range(NK // 4):
            terms = right[j][4 * group : 4 * group + 4].reshape(4 * M, M)
            value = lax.dot_general(
                state_of(j), terms, (((1,), (1,)), ((), ())), preferred_element_type=jnp.float32
            ).astype(jnp.bfloat16)
            for n in range(2):
                for part in range(4):
                    k = 4 * group + part
                    inner[n, k * M : (k + 1) * M, j * M : (j + 1) * M] = value[
                        n * M : (n + 1) * M, part * M : (part + 1) * M
                    ]
    for n in range(2):
        row = jnp.concatenate([left[n][k] for k in range(NK)], axis=1)
        yield jnp.dot(row, inner[n], preferred_element_type=jnp.float32)


def first_product_kernel(tab, *refs):
    left, right, starts, (keep, give, inner) = refs[:2], refs[2:10], refs[10:12], refs[12:]
    x, c, z, y, h = here()

    def state_of(j):
        return jnp.concatenate([starts[0][j], starts[1][j]], axis=0)

    for n, value in enumerate(product(state_of, left, right, inner)):
        a = tab[LEFT_ORDER, slot_of(x, c, z + shift_of(tab, y, c, n))]
        for j in range(2 * NX):
            b = right_sector(tab, x, c, z, j)
            block = masked(value[:, j * M : (j + 1) * M], tab, a, b).astype(jnp.bfloat16)
            (keep if j < NX else give)[j % NX, n] = block


def second_product_kernel(*refs):
    left, right, (keep, give, out0, out1, inner) = refs[:2], refs[2:10], refs[10:]

    def state_of(j):
        return (keep if j < NX else give)[j % NX].reshape(2 * M, M)

    for out, value in zip((out0, out1), product(state_of, left, right, inner)):
        for j in range(2 * NX):
            out[j] = value[:, j * M : (j + 1) * M].astype(jnp.bfloat16)


def first_order_kernel(tab, came, out):
    x, c, z, y, h = here()
    for x_from in range(NX):
        for y_from in range(NY):
            for i in range(4):
                core = c if i < 2 else 1 - c
                slot = slot_of(x_from, core, z + shift_of(tab, y_from, core, i % 2))
                out[tab[LEFT_ORDER, slot]] = came[(x_from * NY + y_from) * 4 + i]


def second_pack_kernel(tab, back0, back1, out0, out1, out2, out3, packed):
    x, c, z, y, h = here()
    packed[...] = jnp.zeros(packed.shape, packed.dtype)
    for n, back in enumerate((back0, back1)):
        z_from = z - shift_of(tab, y, c, n)
        for j in range(2 * NX):
            b = right_sector(tab, x, c, z_from, j)
            group = b // 8

            @pl.when(lax.rem(group, NH) == h)
            def _(j=j, b=b, back=back, group=group):
                packed[lax.rem(group // NH - y + NY, NY), lax.rem(b, 8)] = back[j]

    for r, out in enumerate((out0, out1, out2, out3)):
        out[...] = packed[r]


def second_pick_kernel(tab, part0, part1, part2, part3, out):
    x, c, z, y, h = here()
    a = tab[LEFT_ORDER, slot_of(x, c, z)]
    for q in range(8):
        value = part0[q].astype(jnp.float32)
        for part in (part1, part2, part3):
            value = value + part[q].astype(jnp.float32)
        out[q] = masked(value, tab, a, (y * NH + h) * 8 + q).astype(jnp.bfloat16)


VMEM = pl.BlockSpec(memory_space=pltpu.VMEM)
SMEM = pl.BlockSpec(memory_space=pltpu.SMEM)


def blocks(*shape):
    return jax.ShapeDtypeStruct(shape + (M, M), jnp.bfloat16)


def call(kernel, name, inputs, outputs, scratch=(), flops=0, size=0, vmem=16 << 20):
    return pl.pallas_call(
        kernel,
        name=name,
        out_shape=outputs,
        in_specs=[SMEM if v.dtype == jnp.int32 else VMEM for v in inputs],
        out_specs=jax.tree.map(lambda _: VMEM, outputs),
        scratch_shapes=list(scratch),
        cost_estimate=pl.CostEstimate(flops=flops, bytes_accessed=size, transcendentals=0),
        compiler_params=pltpu.CompilerParams(vmem_limit_bytes=vmem),
    )(*inputs)


def on_device(
    psi, left_ops, right_ops, left_order, right_order, left_qn, right_qn, left_dims, right_dims
):
    h = lax.axis_index("h")
    with jax.named_scope("half_exchange"):
        own = jnp.concatenate([left_ops[:, 0], right_ops[:, 0]], 0)
        other = from_half(own)
    with jax.named_scope("own_over_y"):
        pieces = [[own]] + [[from_y(own, r)] for r in range(1, NY)]
    with jax.named_scope("psi_pack"):
        tab = jnp.concatenate(
            [
                jnp.stack([left_order, right_order, left_qn, right_qn, left_dims, right_dims]),
                jnp.asarray(CONSTANT_ROWS),
            ]
        )
        packed = call(psi_kernel, "psi_pack", (tab, psi[0]), [blocks(8)] * 2, size=3 << 20)
        other, *packed = lax.optimization_barrier((other, *packed))
    with jax.named_scope("other_over_y"):
        pieces[0].append(other)
        for r in range(1, NY):
            pieces[r].append(from_y(other, r))
    with jax.named_scope("psi_shift"):
        starts = [from_shift(packed[n], n) for n in range(2)]
    with jax.named_scope("terms"):
        if PSI_FIRST:
            pieces, starts = lax.optimization_barrier((pieces, starts))
        left16, right16 = call(
            terms_kernel, "terms", sum(pieces, []), [blocks(NK)] * 2, size=2 << 20
        )
    with jax.named_scope("left_shift"):
        left = [from_shift(left16, n) for n in range(2)]
    with jax.named_scope("right_over_x"):
        right = [right16] + [from_x(right16, r) for r in range(1, NX)]
    with jax.named_scope("right_core"):
        right = right + [from_core(value) for value in right]

    inner = [pltpu.VMEM((2, NK * M, 8 * M), jnp.bfloat16)]
    flops = 2 * 16 * NK * 2 * M**3
    with jax.named_scope("first_product"):
        keep, give = call(
            first_product_kernel, "first_product", (tab, *left, *right, *starts),
            [blocks(NX, 2)] * 2, inner, flops, 6 << 20, 32 << 20,
        )
    with jax.named_scope("first_core"):
        got = from_core(give)
    with jax.named_scope("second_product"):
        seconds = call(
            second_product_kernel, "second_product", (*left, *right, keep, give),
            [blocks(8)] * 2, inner, flops, 6 << 20, 32 << 20,
        )
    with jax.named_scope("first_out"):
        got, *seconds = lax.optimization_barrier((got, *seconds))
        sent = call(sent_kernel, "first_sent", (keep, got), blocks(NX * NY, 4), size=2 << 20)
        came = lax.all_to_all(sent, ("x", "y"), 0, 0, tiled=True).reshape(64, M, M)
    with jax.named_scope("second_shift"):
        back = [to_shift(seconds[n], n) for n in range(2)]
    with jax.named_scope("second_over_y"):
        parts = call(
            second_pack_kernel, "second_pack", (tab, *back), [blocks(8)] * NY,
            [pltpu.VMEM((NY, 8, M, M), jnp.bfloat16)], size=2 << 20,
        )
        if OUT_FIRST:
            came, *parts = lax.optimization_barrier((came, *parts))
        parts = [parts[0]] + [from_y(parts[r], -r) for r in range(1, NY)]
    with jax.named_scope("first_order"):
        first_out = call(first_order_kernel, "first_order", (tab, came), blocks(64), size=4 << 20)
    with jax.named_scope("second_pick"):
        second_out = call(
            second_pick_kernel, "second_pick", (tab, *parts), blocks(8), size=2 << 20
        )
    return first_out[None], second_out[None]


def solution(mesh):
    fine = Mesh(mesh.devices.reshape(NX, NC, NZ, NY, NH), AXES)
    slots, ops = P(SLOT), P(("y", "h"), SLOT)
    return jax.shard_map(
        on_device,
        mesh=fine,
        in_specs=(slots, ops, ops, P(), P(), P(), P(), P(), P()),
        out_specs=(slots, P(SLOT, ("y", "h"))),
        check_vma=False,
    )
```

time: 966 us -> 162 us (0.17)
  waiting for transfers between devices: 874 us -> 43.7 us
  starting transfers between devices: 25.5 us -> 95.9 us
  between operations: 18.2 us -> 1.01 us
  local copies, waits for them, and re-layouts: 19.5 us -> 3.7 us
  Pallas kernels: 0 us -> 14.7 us
  other arithmetic: 14.9 us -> 0.89 us
  matrix products: 13.3 us -> 0 us
    psum x1 -> x0, waiting for transfers between devices: 363 us -> none  [on_device(): lax.psum(partial_value.astype(jnp.bfloat16), 'ops').astype(jnp.float32)]
    all_to_all x2 -> x1, waiting for transfers between devices: 372 us -> 12.8 us  [on_device(): came = lax.all_to_all(sent, ('x', 'y'), 0, 0, tiled=True).reshape(64, M, M)]
    reduce_scatter x1 -> x0, waiting for transfers between devices: 139 us -> none  [on_device(): lax.psum_scatter(second_partial.astype(jnp.bfloat16), 'ops', scatter_dime...]
    ppermute x0 -> x24, starting transfers between devices: none -> 89.5 us  [permute(): return lax.ppermute(value, AXES, pairs)]
    ppermute x0 -> x24, waiting for transfers between devices: none -> 30.9 us  [permute(): return lax.ppermute(value, AXES, pairs)]
    all_to_all x2 -> x1, starting transfers between devices: 25.4 us -> 6.39 us  [on_device(): came = lax.all_to_all(sent, ('x', 'y'), 0, 0, tiled=True).reshape(64, M, M)]
    pallas_call x0 -> x8, Pallas kernels: none -> 14.7 us  [call(): pl.pallas_call(kernel, name=name, out_shape=outputs, in_specs=[SMEM if v....]
    dot_general x4 -> x0, matrix products: 13.3 us -> none  [the longest x1 3.43 us: on_device(): jnp.einsum('kixy,kzy->ixz', arrived, right_here, preferred_element_type=j...]
  transfers between devices with their start and end apart: 4 -> 25, of which waited for: 4 -> 8; matrix products, arithmetic and copies ran while one was open for 1% -> 0% of each run, Pallas kernels for 0% -> 5%
where the time goes in v3:
time: 162 us; the launch traced here: 160 us
  starting transfers between devices  95.9 us (59%)
  waiting for transfers between devices  43.7 us (27%)
  Pallas kernels  14.7 us (9%)
  local copies, waits for them, and re-layouts  3.7 us (2%)
    ppermute x24, starting transfers between devices, permute(): return lax.ppermute(value, AXES, pairs)  89.5 us
    ppermute x24, waiting for transfers between devices, permute(): return lax.ppermute(value, AXES, pairs)  30.9 us
    pallas_call x8, Pallas kernels, call(): pl.pallas_call(kernel, name=name, out_shape=outputs, in_specs=[SMEM if v....  14.7 us
    all_to_all x1, waiting for transfers between devices, on_device(): came = lax.all_to_all(sent, ('x', 'y'), 0, 0, tiled=True).reshape(64, M, M)  12.8 us
    all_to_all x1, starting transfers between devices, on_device(): came = lax.all_to_all(sent, ('x', 'y'), 0, 0, tiled=True).reshape(64, M, M)  6.39 us
  transfers between devices with their start and end apart: 25, of which 8 were waited for; matrix products, arithmetic and copies ran while one was open for 0% of the time, Pallas kernels for 5%

profile of v3, /device:TPU:1, one launch (start us, length us, event | category | flops | bytes accessed | tf_op | source)
XLA Modules:
  0.0 159.9 jit_solution(11121646551404644401)
XLA Ops:
  0.6 0.9 pad_maximum_fusion.refs_0_
  1.5 16.3 %collective-permute-start = (bf16[4,128,128]{2,1,0:T(8,128)(2,1)S(1)}, bf16[4,128,128]{2,1,0:T(8,128)(2,1)S(1)}, u32[]{:S(2)}, u32[]{:S(2)}) collective-permute-start(bf16[4,128,128]{2,1,0:T(8,128)(2,1)S(1)} %pad_maximum_fusion.refs_0_), channel_id=1, source_target_pairs={{0,1},{2,3},{4,5},{6,7},{8,9},{10,11},{12,13},{14,15},{16,17},{18,... | collective-permute-start | bytes 393224 | tf_op jit(solution)/shard_map/half_exchange/ppermute | solution.py:51
  17.8 3.2 %collective-permute-start.5 = (bf16[4,128,128]{2,1,0:T(8,128)(2,1)S(1)}, bf16[4,128,128]{2,1,0:T(8,128)(2,1)S(1)}, u32[]{:S(2)}, u32[]{:S(2)}) collective-permute-start(bf16[4,128,128]{2,1,0:T(8,128)(2,1)S(1)} %pad_maximum_fusion.refs_0_), channel_id=1, source_target_pairs={{0,2},{2,4},{4,6},{6,0},{8,10},{10,12},{12,14},{14,8},{16,18},{18,... | collective-permute-start | bytes 393224 | tf_op jit(solution)/shard_map/own_over_y/ppermute | solution.py:51
  21.0 4.5 %collective-permute-start.3 = (bf16[4,128,128]{2,1,0:T(8,128)(2,1)S(1)}, bf16[4,128,128]{2,1,0:T(8,128)(2,1)S(1)}, u32[]{:S(2)}, u32[]{:S(2)}) collective-permute-start(bf16[4,128,128]{2,1,0:T(8,128)(2,1)S(1)} %pad_maximum_fusion.refs_0_), channel_id=1, source_target_pairs={{0,4},{2,6},{4,0},{6,2},{8,12},{10,14},{12,8},{14,10},{16,20},{18,... | collective-permute-start | bytes 393224 | tf_op jit(solution)/shard_map/own_over_y/ppermute | solution.py:51
  25.5 3.0 %collective-permute-start.1 = (bf16[4,128,128]{2,1,0:T(8,128)(2,1)S(1)}, bf16[4,128,128]{2,1,0:T(8,128)(2,1)S(1)}, u32[]{:S(2)}, u32[]{:S(2)}) collective-permute-start(bf16[4,128,128]{2,1,0:T(8,128)(2,1)S(1)} %pad_maximum_fusion.refs_0_), channel_id=1, source_target_pairs={{0,6},{2,0},{4,2},{6,4},{8,14},{10,8},{12,10},{14,12},{16,22},{18,... | collective-permute-start | bytes 393224 | tf_op jit(solution)/shard_map/own_over_y/ppermute | solution.py:51
  28.5 0.8 concatenate.6.tab
  29.3 1.6 copy-done.1
  30.9 0.8 psi_pack.1
  31.7 0.0 collective-permute-done.refs_1_
  31.7 0.7 collective-permute-start.7
  32.4 4.0 %collective-permute-start.8 = (bf16[8,128,128]{2,1,0:T(8,128)(2,1)S(1)}, bf16[8,128,128]{2,1,0:T(8,128)(2,1)S(1)}, u32[]{:S(2)}, u32[]{:S(2)}) collective-permute-start(bf16[8,128,128]{2,1,0:T(8,128)(2,1)S(1)} %get-tuple-element.39), channel_id=1, source_target_pairs={{0,33},{2,26},{4,45},{6,22},{8,41},{10,34},{12,53},{14,30},{16,49}... | collective-permute-start | bytes 786440 | tf_op jit(solution)/shard_map/psi_shift/ppermute | solution.py:51
  36.4 0.0 collective-permute-done.5.refs_6_
  36.5 7.3 %collective-permute-start.6 = (bf16[4,128,128]{2,1,0:T(8,128)(2,1)S(1)}, bf16[4,128,128]{2,1,0:T(8,128)(2,1)S(1)}, u32[]{:S(2)}, u32[]{:S(2)}) collective-permute-start(bf16[4,128,128]{2,1,0:T(8,128)(2,1)S(1)} %collective-permute-done.refs_1_), channel_id=1, source_target_pairs={{0,2},{2,4},{4,6},{6,0},{8,10},{10,12},{12,14},{14,8},{16,18},{18,... | collective-permute-start | bytes 393224 | tf_op jit(solution)/shard_map/other_over_y/ppermute | solution.py:51
  43.8 3.4 %collective-permute-start.4 = (bf16[4,128,128]{2,1,0:T(8,128)(2,1)S(1)}, bf16[4,128,128]{2,1,0:T(8,128)(2,1)S(1)}, u32[]{:S(2)}, u32[]{:S(2)}) collective-permute-start(bf16[4,128,128]{2,1,0:T(8,128)(2,1)S(1)} %collective-permute-done.refs_1_), channel_id=1, source_target_pairs={{0,4},{2,6},{4,0},{6,2},{8,12},{10,14},{12,8},{14,10},{16,20},{18,... | collective-permute-start | bytes 393224 | tf_op jit(solution)/shard_map/other_over_y/ppermute | solution.py:51
  47.2 2.9 %collective-permute-start.2 = (bf16[4,128,128]{2,1,0:T(8,128)(2,1)S(1)}, bf16[4,128,128]{2,1,0:T(8,128)(2,1)S(1)}, u32[]{:S(2)}, u32[]{:S(2)}) collective-permute-start(bf16[4,128,128]{2,1,0:T(8,128)(2,1)S(1)} %collective-permute-done.refs_1_), channel_id=1, source_target_pairs={{0,6},{2,0},{4,2},{6,4},{8,14},{10,8},{12,10},{14,12},{16,22},{18,... | collective-permute-start | bytes 393224 | tf_op jit(solution)/shard_map/other_over_y/ppermute | solution.py:51
  50.0 2.4 %collective-permute-done.4.refs_5_ = bf16[4,128,128]{2,1,0:T(8,128)(2,1)S(1)} collective-permute-done((bf16[4,128,128]{2,1,0:T(8,128)(2,1)S(1)}, bf16[4,128,128]{2,1,0:T(8,128)(2,1)S(1)}, u32[]{:S(2)}, u32[]{:S(2)}) %collective-permute-start.4) | collective-permute-done | bytes 131104 | tf_op jit(solution)/shard_map/other_over_y/ppermute | solution.py:51
  52.5 1.0 collective-permute-done.2.refs_3_
  53.5 0.1 terms.1
  53.5 2.8 %collective-permute-start.10 = (bf16[16,128,128]{2,1,0:T(8,128)(2,1)S(1)}, bf16[16,128,128]{2,1,0:T(8,128)(2,1)S(1)}, u32[]{:S(2)}, u32[]{:S(2)}) collective-permute-start(bf16[16,128,128]{2,1,0:T(8,128)(2,1)S(1)} %get-tuple-element.48), channel_id=1, source_target_pairs={{0,33},{2,26},{4,45},{6,22},{8,41},{10,34},{12,53},{14,30},{16,49}... | collective-permute-start | bytes 1572872 | tf_op jit(solution)/shard_map/left_shift/ppermute | solution.py:51
  56.4 3.1 %collective-permute-start.13 = (bf16[16,128,128]{2,1,0:T(8,128)(2,1)S(1)}, bf16[16,128,128]{2,1,0:T(8,128)(2,1)S(1)}, u32[]{:S(2)}, u32[]{:S(2)}) collective-permute-start(bf16[16,128,128]{2,1,0:T(8,128)(2,1)S(1)} %get-tuple-element.49.refs_2_), channel_id=1, source_target_pairs={{0,128},{2,130},{4,132},{6,134},{8,136},{10,138},{12,140},{14,142}... | collective-permute-start | bytes 1572872 | tf_op jit(solution)/shard_map/right_over_x/ppermute | solution.py:51
  59.5 4.4 %collective-permute-start.12 = (bf16[16,128,128]{2,1,0:T(8,128)(2,1)S(1)}, bf16[16,128,128]{2,1,0:T(8,128)(2,1)S(1)}, u32[]{:S(2)}, u32[]{:S(2)}) collective-permute-start(bf16[16,128,128]{2,1,0:T(8,128)(2,1)S(1)} %get-tuple-element.49.refs_2_), channel_id=1, source_target_pairs={{0,256},{2,258},{4,260},{6,262},{8,264},{10,266},{12,268},{14,270}... | collective-permute-start | bytes 1572872 | tf_op jit(solution)/shard_map/right_over_x/ppermute | solution.py:51
  63.9 3.1 %collective-permute-start.11 = (bf16[16,128,128]{2,1,0:T(8,128)(2,1)S(1)}, bf16[16,128,128]{2,1,0:T(8,128)(2,1)S(1)}, u32[]{:S(2)}, u32[]{:S(2)}) collective-permute-start(bf16[16,128,128]{2,1,0:T(8,128)(2,1)S(1)} %get-tuple-element.49.refs_2_), channel_id=1, source_target_pairs={{0,384},{2,386},{4,388},{6,390},{8,392},{10,394},{12,396},{14,398}... | collective-permute-start | bytes 1572872 | tf_op jit(solution)/shard_map/right_over_x/ppermute | solution.py:51
  67.0 0.7 collective-permute-start.9
  67.7 9.3 %collective-permute-done.10.refs_1_ = bf16[16,128,128]{2,1,0:T(8,128)(2,1)S(1)} collective-permute-done((bf16[16,128,128]{2,1,0:T(8,128)(2,1)S(1)}, bf16[16,128,128]{2,1,0:T(8,128)(2,1)S(1)}, u32[]{:S(2)}, u32[]{:S(2)}) %collective-permute-start.10) | collective-permute-done | bytes 524320 | tf_op jit(solution)/shard_map/left_shift/ppermute | solution.py:51
  77.0 8.6 %collective-permute-start.14 = (bf16[16,128,128]{2,1,0:T(8,128)(2,1)S(1)}, bf16[16,128,128]{2,1,0:T(8,128)(2,1)S(1)}, u32[]{:S(2)}, u32[]{:S(2)}) collective-permute-start(bf16[16,128,128]{2,1,0:T(8,128)(2,1)S(1)} %get-tuple-element.49.refs_2_), channel_id=1, source_target_pairs={{0,64},{2,66},{4,68},{6,70},{8,72},{10,74},{12,76},{14,78},{16,80}... | collective-permute-start | bytes 1572872 | tf_op jit(solution)/shard_map/right_core/ppermute | solution.py:51
  85.6 1.9 %collective-permute-start.17 = (bf16[16,128,128]{2,1,0:T(8,128)(2,1)S(1)}, bf16[16,128,128]{2,1,0:T(8,128)(2,1)S(1)}, u32[]{:S(2)}, u32[]{:S(2)}) collective-permute-start(bf16[16,128,128]{2,1,0:T(8,128)(2,1)S(1)} %collective-permute-done.13.refs_5_), channel_id=1, source_target_pairs={{0,64},{2,66},{4,68},{6,70},{8,72},{10,74},{12,76},{14,78},{16,80}... | collective-permute-start | bytes 1572872 | tf_op jit(solution)/shard_map/right_core/ppermute | solution.py:51
  87.6 2.4 %collective-permute-start.16 = (bf16[16,128,128]{2,1,0:T(8,128)(2,1)S(1)}, bf16[16,128,128]{2,1,0:T(8,128)(2,1)S(1)}, u32[]{:S(2)}, u32[]{:S(2)}) collective-permute-start(bf16[16,128,128]{2,1,0:T(8,128)(2,1)S(1)} %collective-permute-done.12.refs_4_), channel_id=1, source_target_pairs={{0,64},{2,66},{4,68},{6,70},{8,72},{10,74},{12,76},{14,78},{16,80}... | collective-permute-start | bytes 1572872 | tf_op jit(solution)/shard_map/right_core/ppermute | solution.py:51
  90.0 1.9 %collective-permute-start.15 = (bf16[16,128,128]{2,1,0:T(8,128)(2,1)S(1)}, bf16[16,128,128]{2,1,0:T(8,128)(2,1)S(1)}, u32[]{:S(2)}, u32[]{:S(2)}) collective-permute-start(bf16[16,128,128]{2,1,0:T(8,128)(2,1)S(1)} %collective-permute-done.11.refs_3_), channel_id=1, source_target_pairs={{0,64},{2,66},{4,68},{6,70},{8,72},{10,74},{12,76},{14,78},{16,80}... | collective-permute-start | bytes 1572872 | tf_op jit(solution)/shard_map/right_core/ppermute | solution.py:51
  92.0 1.8 %collective-permute-done.15.refs_7_ = bf16[16,128,128]{2,1,0:T(8,128)(2,1)S(1)} collective-permute-done((bf16[16,128,128]{2,1,0:T(8,128)(2,1)S(1)}, bf16[16,128,128]{2,1,0:T(8,128)(2,1)S(1)}, u32[]{:S(2)}, u32[]{:S(2)}) %collective-permute-start.15) | collective-permute-done | bytes 524320 | tf_op jit(solution)/shard_map/right_core/ppermute | solution.py:51
  93.8 4.6 %first_product.1 = (bf16[4,2,128,128]{3,2,1,0:T(8,128)(2,1)S(1)}, bf16[4,2,128,128]{3,2,1,0:T(8,128)(2,1)S(1)}) custom-call(s32[8,64]{1,0:T(8,128)S(1)} %concatenate.6.tab, bf16[16,128,128]{2,1,0:T(8,128)(2,1)S(1)} %collective-permute-done.9.refs_0_, bf16[16,128,128]{2,1,0:T(8,128)(2,1)S(1)} %collective-permute-done.10.refs_1_, ...), custom_call_target="tpu_custom_call" | custom-call | flops 2147483648 | bytes 6291456 | tf_op jit(solution)/shard_map/first_product/first_product/pallas_call | solution.py:228
  98.4 2.0 %collective-permute-start.18 = (bf16[4,2,128,128]{3,2,1,0:T(8,128)(2,1)S(1)}, bf16[4,2,128,128]{3,2,1,0:T(8,128)(2,1)S(1)}, u32[]{:S(2)}, u32[]{:S(2)}) collective-permute-start(bf16[4,2,128,128]{3,2,1,0:T(8,128)(2,1)S(1)} %get-tuple-element.53.refs_11_), channel_id=1, source_target_pairs={{0,64},{2,66},{4,68},{6,70},{8,72},{10,74},{12,76},{14,78},{16,80}... | collective-permute-start | bytes 786440 | tf_op jit(solution)/shard_map/first_core/ppermute | solution.py:51
  100.5 4.0 %second_product.1 = (bf16[8,128,128]{2,1,0:T(8,128)(2,1)S(1)}, bf16[8,128,128]{2,1,0:T(8,128)(2,1)S(1)}) custom-call(bf16[16,128,128]{2,1,0:T(8,128)(2,1)S(1)} %collective-permute-done.9.refs_0_, bf16[16,128,128]{2,1,0:T(8,128)(2,1)S(1)} %collective-permute-done.10.refs_1_, bf16[16,128,128]{2,1,0:T(8,128)(2,1)S(1)} %get-tuple-element.49.refs_2_, ...), custom_call_target="tpu_custom_call" | custom-call | flops 2147483648 | bytes 6291456 | tf_op jit(solution)/shard_map/second_product/second_product/pallas_call | solution.py:228
  104.5 0.3 first_sent.1
  104.8 0.0 copy-start
  104.8 1.3 copy-done
  106.1 6.4 %all-to-all-start = ((bf16[16,4,128,128]{3,2,1,0:T(8,128)(2,1)}), bf16[16,4,128,128]{3,2,1,0:T(8,128)(2,1)S(1)}, u32[]{:S(2)}, u32[]{:S(2)}) async-start(bf16[16,4,128,128]{3,2,1,0:T(8,128)(2,1)} %copy-done), calls=%async_computation | async-start | bytes 4194304 | tf_op jit(solution)/shard_map/first_out/all_to_all | solution.py:294
  112.5 0.7 collective-permute-start.19
  113.2 4.2 %collective-permute-start.20 = (bf16[8,128,128]{2,1,0:T(8,128)(2,1)S(1)}, bf16[8,128,128]{2,1,0:T(8,128)(2,1)S(1)}, u32[]{:S(2)}, u32[]{:S(2)}) collective-permute-start(bf16[8,128,128]{2,1,0:T(8,128)(2,1)S(1)} %get-tuple-element.58), channel_id=1, source_target_pairs={{0,32},{2,43},{4,28},{6,55},{8,40},{10,51},{12,36},{14,63},{16,48}... | collective-permute-start | bytes 786440 | tf_op jit(solution)/shard_map/second_shift/ppermute | solution.py:51
  117.4 10.3 %collective-permute-done.20.back1 = bf16[8,128,128]{2,1,0:T(8,128)(2,1)S(1)} collective-permute-done((bf16[8,128,128]{2,1,0:T(8,128)(2,1)S(1)}, bf16[8,128,128]{2,1,0:T(8,128)(2,1)S(1)}, u32[]{:S(2)}, u32[]{:S(2)}) %collective-permute-start.20) | collective-permute-done | bytes 262176 | tf_op jit(solution)/shard_map/second_shift/ppermute | solution.py:51
  127.7 1.2 second_pack.1
  128.9 12.8 %all-to-all-done = bf16[16,4,128,128]{3,2,1,0:T(8,128)(2,1)S(1)} async-done(((bf16[16,4,128,128]{3,2,1,0:T(8,128)(2,1)}), bf16[16,4,128,128]{3,2,1,0:T(8,128)(2,1)S(1)}, u32[]{:S(2)}, u32[]{:S(2)}) %all-to-all-start) | async-done | bytes 2097184 | tf_op jit(solution)/shard_map/first_out/all_to_all | solution.py:294
  141.7 2.2 %collective-permute-start.21 = (bf16[8,128,128]{2,1,0:T(8,128)(2,1)S(1)}, bf16[8,128,128]{2,1,0:T(8,128)(2,1)S(1)}, u32[]{:S(2)}, u32[]{:S(2)}) collective-permute-start(bf16[8,128,128]{2,1,0:T(8,128)(2,1)S(1)} %get-tuple-element.65), channel_id=1, source_target_pairs={{0,2},{2,4},{4,6},{6,0},{8,10},{10,12},{12,14},{14,8},{16,18},{18,... | collective-permute-start | bytes 786440 | tf_op jit(solution)/shard_map/second_over_y/ppermute | solution.py:51
  143.9 2.9 %collective-permute-start.22 = (bf16[8,128,128]{2,1,0:T(8,128)(2,1)S(1)}, bf16[8,128,128]{2,1,0:T(8,128)(2,1)S(1)}, u32[]{:S(2)}, u32[]{:S(2)}) collective-permute-start(bf16[8,128,128]{2,1,0:T(8,128)(2,1)S(1)} %get-tuple-element.66), channel_id=1, source_target_pairs={{0,4},{2,6},{4,0},{6,2},{8,12},{10,14},{12,8},{14,10},{16,20},{18,... | collective-permute-start | bytes 786440 | tf_op jit(solution)/shard_map/second_over_y/ppermute | solution.py:51
  146.8 3.3 %collective-permute-start.23 = (bf16[8,128,128]{2,1,0:T(8,128)(2,1)S(1)}, bf16[8,128,128]{2,1,0:T(8,128)(2,1)S(1)}, u32[]{:S(2)}, u32[]{:S(2)}) collective-permute-start(bf16[8,128,128]{2,1,0:T(8,128)(2,1)S(1)} %get-tuple-element.67), channel_id=1, source_target_pairs={{0,6},{2,0},{4,2},{6,4},{8,14},{10,8},{12,10},{14,12},{16,22},{18,... | collective-permute-start | bytes 786440 | tf_op jit(solution)/shard_map/second_over_y/ppermute | solution.py:51
  150.1 2.3 %first_order.1 = bf16[64,128,128]{2,1,0:T(8,128)(2,1)} custom-call(s32[8,64]{1,0:T(8,128)S(1)} %concatenate.6.tab, bf16[64,128,128]{2,1,0:T(8,128)(2,1)S(1)} %bitcast.12), custom_call_target="tpu_custom_call" | custom-call | bytes 4194304 | tf_op jit(solution)/shard_map/first_order/first_order/pallas_call | solution.py:228
  152.5 3.1 %collective-permute-done.22.part2 = bf16[8,128,128]{2,1,0:T(8,128)(2,1)S(1)} collective-permute-done((bf16[8,128,128]{2,1,0:T(8,128)(2,1)S(1)}, bf16[8,128,128]{2,1,0:T(8,128)(2,1)S(1)}, u32[]{:S(2)}, u32[]{:S(2)}) %collective-permute-start.22) | collective-permute-done | bytes 262176 | tf_op jit(solution)/shard_map/second_over_y/ppermute | solution.py:51
  155.6 2.9 %collective-permute-done.23.part3 = bf16[8,128,128]{2,1,0:T(8,128)(2,1)S(1)} collective-permute-done((bf16[8,128,128]{2,1,0:T(8,128)(2,1)S(1)}, bf16[8,128,128]{2,1,0:T(8,128)(2,1)S(1)}, u32[]{:S(2)}, u32[]{:S(2)}) %collective-permute-start.23) | collective-permute-done | bytes 262176 | tf_op jit(solution)/shard_map/second_over_y/ppermute | solution.py:51
  158.4 1.5 second_pick.1
  (16 shorter events, 0.0 us)
Async XLA Ops:
  1.5 30.2 %collective-permute-start = (bf16[4,128,128]{2,1,0:T(8,128)(2,1)S(1)}, bf16[4,128,128]{2,1,0:T(8,128)(2,1)S(1)}, u32[]{:S(2)}, u32[]{:S(2)}) collective-permute-start(bf16[4,128,128]{2,1,0:T(8,128)(2,1)S(1)} %pad_maximum_fusion.refs_0_), channel_id=1, source_target_pairs={{0,1},{2,3},{4,5},{6,7},{8,9},{10,11},{12,13},{14,15},{16,17},{18,... | collective-permute-start | bytes 393224 | tf_op jit(solution)/shard_map/half_exchange/ppermute | solution.py:51
  17.8 18.6 %collective-permute-start.5 = (bf16[4,128,128]{2,1,0:T(8,128)(2,1)S(1)}, bf16[4,128,128]{2,1,0:T(8,128)(2,1)S(1)}, u32[]{:S(2)}, u32[]{:S(2)}) collective-permute-start(bf16[4,128,128]{2,1,0:T(8,128)(2,1)S(1)} %pad_maximum_fusion.refs_0_), channel_id=1, source_target_pairs={{0,2},{2,4},{4,6},{6,0},{8,10},{10,12},{12,14},{14,8},{16,18},{18,... | collective-permute-start | bytes 393224 | tf_op jit(solution)/shard_map/own_over_y/ppermute | solution.py:51
  21.0 22.8 %collective-permute-start.3 = (bf16[4,128,128]{2,1,0:T(8,128)(2,1)S(1)}, bf16[4,128,128]{2,1,0:T(8,128)(2,1)S(1)}, u32[]{:S(2)}, u32[]{:S(2)}) collective-permute-start(bf16[4,128,128]{2,1,0:T(8,128)(2,1)S(1)} %pad_maximum_fusion.refs_0_), channel_id=1, source_target_pairs={{0,4},{2,6},{4,0},{6,2},{8,12},{10,14},{12,8},{14,10},{16,20},{18,... | collective-permute-start | bytes 393224 | tf_op jit(solution)/shard_map/own_over_y/ppermute | solution.py:51
  25.5 21.6 %collective-permute-start.1 = (bf16[4,128,128]{2,1,0:T(8,128)(2,1)S(1)}, bf16[4,128,128]{2,1,0:T(8,128)(2,1)S(1)}, u32[]{:S(2)}, u32[]{:S(2)}) collective-permute-start(bf16[4,128,128]{2,1,0:T(8,128)(2,1)S(1)} %pad_maximum_fusion.refs_0_), channel_id=1, source_target_pairs={{0,6},{2,0},{4,2},{6,4},{8,14},{10,8},{12,10},{14,12},{16,22},{18,... | collective-permute-start | bytes 393224 | tf_op jit(solution)/shard_map/own_over_y/ppermute | solution.py:51
  29.3 1.6 copy-start.1
  31.7 21.7 %collective-permute-start.7 = (bf16[8,128,128]{2,1,0:T(8,128)(2,1)S(1)}, bf16[8,128,128]{2,1,0:T(8,128)(2,1)S(1)}, u32[]{:S(2)}, u32[]{:S(2)}) collective-permute-start(bf16[8,128,128]{2,1,0:T(8,128)(2,1)S(1)} %get-tuple-element.38), channel_id=1, source_target_pairs={{0,0},{2,59},{4,12},{6,55},{8,8},{10,2},{12,20},{14,63},{16,16},{1... | collective-permute-start | bytes 786440 | tf_op jit(solution)/shard_map/psi_shift/ppermute | solution.py:51
  32.4 21.0 %collective-permute-start.8 = (bf16[8,128,128]{2,1,0:T(8,128)(2,1)S(1)}, bf16[8,128,128]{2,1,0:T(8,128)(2,1)S(1)}, u32[]{:S(2)}, u32[]{:S(2)}) collective-permute-start(bf16[8,128,128]{2,1,0:T(8,128)(2,1)S(1)} %get-tuple-element.39), channel_id=1, source_target_pairs={{0,33},{2,26},{4,45},{6,22},{8,41},{10,34},{12,53},{14,30},{16,49}... | collective-permute-start | bytes 786440 | tf_op jit(solution)/shard_map/psi_shift/ppermute | solution.py:51
  36.5 13.6 %collective-permute-start.6 = (bf16[4,128,128]{2,1,0:T(8,128)(2,1)S(1)}, bf16[4,128,128]{2,1,0:T(8,128)(2,1)S(1)}, u32[]{:S(2)}, u32[]{:S(2)}) collective-permute-start(bf16[4,128,128]{2,1,0:T(8,128)(2,1)S(1)} %collective-permute-done.refs_1_), channel_id=1, source_target_pairs={{0,2},{2,4},{4,6},{6,0},{8,10},{10,12},{12,14},{14,8},{16,18},{18,... | collective-permute-start | bytes 393224 | tf_op jit(solution)/shard_map/other_over_y/ppermute | solution.py:51
  43.8 8.7 %collective-permute-start.4 = (bf16[4,128,128]{2,1,0:T(8,128)(2,1)S(1)}, bf16[4,128,128]{2,1,0:T(8,128)(2,1)S(1)}, u32[]{:S(2)}, u32[]{:S(2)}) collective-permute-start(bf16[4,128,128]{2,1,0:T(8,128)(2,1)S(1)} %collective-permute-done.refs_1_), channel_id=1, source_target_pairs={{0,4},{2,6},{4,0},{6,2},{8,12},{10,14},{12,8},{14,10},{16,20},{18,... | collective-permute-start | bytes 393224 | tf_op jit(solution)/shard_map/other_over_y/ppermute | solution.py:51
  47.2 6.3 %collective-permute-start.2 = (bf16[4,128,128]{2,1,0:T(8,128)(2,1)S(1)}, bf16[4,128,128]{2,1,0:T(8,128)(2,1)S(1)}, u32[]{:S(2)}, u32[]{:S(2)}) collective-permute-start(bf16[4,128,128]{2,1,0:T(8,128)(2,1)S(1)} %collective-permute-done.refs_1_), channel_id=1, source_target_pairs={{0,6},{2,0},{4,2},{6,4},{8,14},{10,8},{12,10},{14,12},{16,22},{18,... | collective-permute-start | bytes 393224 | tf_op jit(solution)/shard_map/other_over_y/ppermute | solution.py:51
  53.5 23.5 %collective-permute-start.10 = (bf16[16,128,128]{2,1,0:T(8,128)(2,1)S(1)}, bf16[16,128,128]{2,1,0:T(8,128)(2,1)S(1)}, u32[]{:S(2)}, u32[]{:S(2)}) collective-permute-start(bf16[16,128,128]{2,1,0:T(8,128)(2,1)S(1)} %get-tuple-element.48), channel_id=1, source_target_pairs={{0,33},{2,26},{4,45},{6,22},{8,41},{10,34},{12,53},{14,30},{16,49}... | collective-permute-start | bytes 1572872 | tf_op jit(solution)/shard_map/left_shift/ppermute | solution.py:51
  56.4 29.2 %collective-permute-start.13 = (bf16[16,128,128]{2,1,0:T(8,128)(2,1)S(1)}, bf16[16,128,128]{2,1,0:T(8,128)(2,1)S(1)}, u32[]{:S(2)}, u32[]{:S(2)}) collective-permute-start(bf16[16,128,128]{2,1,0:T(8,128)(2,1)S(1)} %get-tuple-element.49.refs_2_), channel_id=1, source_target_pairs={{0,128},{2,130},{4,132},{6,134},{8,136},{10,138},{12,140},{14,142}... | collective-permute-start | bytes 1572872 | tf_op jit(solution)/shard_map/right_over_x/ppermute | solution.py:51
  59.5 28.1 %collective-permute-start.12 = (bf16[16,128,128]{2,1,0:T(8,128)(2,1)S(1)}, bf16[16,128,128]{2,1,0:T(8,128)(2,1)S(1)}, u32[]{:S(2)}, u32[]{:S(2)}) collective-permute-start(bf16[16,128,128]{2,1,0:T(8,128)(2,1)S(1)} %get-tuple-element.49.refs_2_), channel_id=1, source_target_pairs={{0,256},{2,258},{4,260},{6,262},{8,264},{10,266},{12,268},{14,270}... | collective-permute-start | bytes 1572872 | tf_op jit(solution)/shard_map/right_over_x/ppermute | solution.py:51
  63.9 26.1 %collective-permute-start.11 = (bf16[16,128,128]{2,1,0:T(8,128)(2,1)S(1)}, bf16[16,128,128]{2,1,0:T(8,128)(2,1)S(1)}, u32[]{:S(2)}, u32[]{:S(2)}) collective-permute-start(bf16[16,128,128]{2,1,0:T(8,128)(2,1)S(1)} %get-tuple-element.49.refs_2_), channel_id=1, source_target_pairs={{0,384},{2,386},{4,388},{6,390},{8,392},{10,394},{12,396},{14,398}... | collective-permute-start | bytes 1572872 | tf_op jit(solution)/shard_map/right_over_x/ppermute | solution.py:51
  67.0 25.0 %collective-permute-start.9 = (bf16[16,128,128]{2,1,0:T(8,128)(2,1)S(1)}, bf16[16,128,128]{2,1,0:T(8,128)(2,1)S(1)}, u32[]{:S(2)}, u32[]{:S(2)}) collective-permute-start(bf16[16,128,128]{2,1,0:T(8,128)(2,1)S(1)} %get-tuple-element.48), channel_id=1, source_target_pairs={{0,0},{2,59},{4,12},{6,55},{8,8},{10,2},{12,20},{14,63},{16,16},{1... | collective-permute-start | bytes 1572872 | tf_op jit(solution)/shard_map/left_shift/ppermute | solution.py:51
  77.0 14.9 %collective-permute-start.14 = (bf16[16,128,128]{2,1,0:T(8,128)(2,1)S(1)}, bf16[16,128,128]{2,1,0:T(8,128)(2,1)S(1)}, u32[]{:S(2)}, u32[]{:S(2)}) collective-permute-start(bf16[16,128,128]{2,1,0:T(8,128)(2,1)S(1)} %get-tuple-element.49.refs_2_), channel_id=1, source_target_pairs={{0,64},{2,66},{4,68},{6,70},{8,72},{10,74},{12,76},{14,78},{16,80}... | collective-permute-start | bytes 1572872 | tf_op jit(solution)/shard_map/right_core/ppermute | solution.py:51
  85.6 6.3 %collective-permute-start.17 = (bf16[16,128,128]{2,1,0:T(8,128)(2,1)S(1)}, bf16[16,128,128]{2,1,0:T(8,128)(2,1)S(1)}, u32[]{:S(2)}, u32[]{:S(2)}) collective-permute-start(bf16[16,128,128]{2,1,0:T(8,128)(2,1)S(1)} %collective-permute-done.13.refs_5_), channel_id=1, source_target_pairs={{0,64},{2,66},{4,68},{6,70},{8,72},{10,74},{12,76},{14,78},{16,80}... | collective-permute-start | bytes 1572872 | tf_op jit(solution)/shard_map/right_core/ppermute | solution.py:51
  87.6 4.4 %collective-permute-start.16 = (bf16[16,128,128]{2,1,0:T(8,128)(2,1)S(1)}, bf16[16,128,128]{2,1,0:T(8,128)(2,1)S(1)}, u32[]{:S(2)}, u32[]{:S(2)}) collective-permute-start(bf16[16,128,128]{2,1,0:T(8,128)(2,1)S(1)} %collective-permute-done.12.refs_4_), channel_id=1, source_target_pairs={{0,64},{2,66},{4,68},{6,70},{8,72},{10,74},{12,76},{14,78},{16,80}... | collective-permute-start | bytes 1572872 | tf_op jit(solution)/shard_map/right_core/ppermute | solution.py:51
  90.0 3.8 %collective-permute-start.15 = (bf16[16,128,128]{2,1,0:T(8,128)(2,1)S(1)}, bf16[16,128,128]{2,1,0:T(8,128)(2,1)S(1)}, u32[]{:S(2)}, u32[]{:S(2)}) collective-permute-start(bf16[16,128,128]{2,1,0:T(8,128)(2,1)S(1)} %collective-permute-done.11.refs_3_), channel_id=1, source_target_pairs={{0,64},{2,66},{4,68},{6,70},{8,72},{10,74},{12,76},{14,78},{16,80}... | collective-permute-start | bytes 1572872 | tf_op jit(solution)/shard_map/right_core/ppermute | solution.py:51
  98.4 6.0 %collective-permute-start.18 = (bf16[4,2,128,128]{3,2,1,0:T(8,128)(2,1)S(1)}, bf16[4,2,128,128]{3,2,1,0:T(8,128)(2,1)S(1)}, u32[]{:S(2)}, u32[]{:S(2)}) collective-permute-start(bf16[4,2,128,128]{3,2,1,0:T(8,128)(2,1)S(1)} %get-tuple-element.53.refs_11_), channel_id=1, source_target_pairs={{0,64},{2,66},{4,68},{6,70},{8,72},{10,74},{12,76},{14,78},{16,80}... | collective-permute-start | bytes 786440 | tf_op jit(solution)/shard_map/first_core/ppermute | solution.py:51
  104.8 1.3 copy-start
  106.1 35.6 %all-to-all-start = ((bf16[16,4,128,128]{3,2,1,0:T(8,128)(2,1)}), bf16[16,4,128,128]{3,2,1,0:T(8,128)(2,1)S(1)}, u32[]{:S(2)}, u32[]{:S(2)}) async-start(bf16[16,4,128,128]{3,2,1,0:T(8,128)(2,1)} %copy-done), calls=%async_computation | async-start | bytes 4194304 | tf_op jit(solution)/shard_map/first_out/all_to_all | solution.py:294
  112.5 4.9 %collective-permute-start.19 = (bf16[8,128,128]{2,1,0:T(8,128)(2,1)S(1)}, bf16[8,128,128]{2,1,0:T(8,128)(2,1)S(1)}, u32[]{:S(2)}, u32[]{:S(2)}) collective-permute-start(bf16[8,128,128]{2,1,0:T(8,128)(2,1)S(1)} %get-tuple-element.57), channel_id=1, source_target_pairs={{0,0},{2,10},{4,61},{6,22},{8,8},{10,18},{12,4},{14,30},{16,16},{1... | collective-permute-start | bytes 786440 | tf_op jit(solution)/shard_map/second_shift/ppermute | solution.py:51
  113.2 14.5 %collective-permute-start.20 = (bf16[8,128,128]{2,1,0:T(8,128)(2,1)S(1)}, bf16[8,128,128]{2,1,0:T(8,128)(2,1)S(1)}, u32[]{:S(2)}, u32[]{:S(2)}) collective-permute-start(bf16[8,128,128]{2,1,0:T(8,128)(2,1)S(1)} %get-tuple-element.58), channel_id=1, source_target_pairs={{0,32},{2,43},{4,28},{6,55},{8,40},{10,51},{12,36},{14,63},{16,48}... | collective-permute-start | bytes 786440 | tf_op jit(solution)/shard_map/second_shift/ppermute | solution.py:51
  141.7 10.8 %collective-permute-start.21 = (bf16[8,128,128]{2,1,0:T(8,128)(2,1)S(1)}, bf16[8,128,128]{2,1,0:T(8,128)(2,1)S(1)}, u32[]{:S(2)}, u32[]{:S(2)}) collective-permute-start(bf16[8,128,128]{2,1,0:T(8,128)(2,1)S(1)} %get-tuple-element.65), channel_id=1, source_target_pairs={{0,2},{2,4},{4,6},{6,0},{8,10},{10,12},{12,14},{14,8},{16,18},{18,... | collective-permute-start | bytes 786440 | tf_op jit(solution)/shard_map/second_over_y/ppermute | solution.py:51
  143.9 11.7 %collective-permute-start.22 = (bf16[8,128,128]{2,1,0:T(8,128)(2,1)S(1)}, bf16[8,128,128]{2,1,0:T(8,128)(2,1)S(1)}, u32[]{:S(2)}, u32[]{:S(2)}) collective-permute-start(bf16[8,128,128]{2,1,0:T(8,128)(2,1)S(1)} %get-tuple-element.66), channel_id=1, source_target_pairs={{0,4},{2,6},{4,0},{6,2},{8,12},{10,14},{12,8},{14,10},{16,20},{18,... | collective-permute-start | bytes 786440 | tf_op jit(solution)/shard_map/second_over_y/ppermute | solution.py:51
  146.8 11.6 %collective-permute-start.23 = (bf16[8,128,128]{2,1,0:T(8,128)(2,1)S(1)}, bf16[8,128,128]{2,1,0:T(8,128)(2,1)S(1)}, u32[]{:S(2)}, u32[]{:S(2)}) collective-permute-start(bf16[8,128,128]{2,1,0:T(8,128)(2,1)S(1)} %get-tuple-element.67), channel_id=1, source_target_pairs={{0,6},{2,0},{4,2},{6,4},{8,14},{10,8},{12,10},{14,12},{16,22},{18,... | collective-permute-start | bytes 786440 | tf_op jit(solution)/shard_map/second_over_y/ppermute | solution.py:51

commit v4 on v3

--- a/solution.py
+++ b/solution.py
@@ -10,8 +10,6 @@
 from jax.sharding import PartitionSpec as P
 
 SPREAD = 1
-PSI_FIRST = True
-OUT_FIRST = True
 M = 128
 NX, NC, NZ, NY, NH = 4, 2, 8, 4, 2
 NK = 16
@@ -19,9 +17,9 @@
 SLOT = ("x", "c", "z")
 SHIFT = np.array(
     [
-        [[0, 4], [0, -4]],
-        [[1, -3], [-1, 3]],
-        [[-1, 3], [1, -3]],
+        [[4, 0], [-4, 0]],
+        [[-3, 1], [3, -1]],
+        [[3, -1], [-3, 1]],
         [[2, -2], [-2, 2]],
     ],
     np.int32,
@@ -108,11 +106,10 @@
     left, right = refs[-2:]
     for r in range(NY):
         for half in range(2):
-            source = refs[2 * r + half]
             place = lax.rem(y + r, NY) * 4 + 2 * (h if half == 0 else 1 - h)
             for k in range(2):
-                left[place + k] = source[k]
-                right[place + k] = source[2 + k]
+                left[place + k] = refs[r][4 * half + k]
+                right[place + k] = refs[r][4 * half + 2 + k]
 
 
 def sent_kernel(keep, got, out):
@@ -224,7 +221,7 @@
     return jax.ShapeDtypeStruct(shape + (M, M), jnp.bfloat16)
 
 
-def call(kernel, name, inputs, outputs, scratch=(), flops=0, size=0, vmem=16 << 20):
+def call(kernel, name, inputs, outputs, scratch=(), flops=0, size=0, vmem=8 << 20):
     return pl.pallas_call(
         kernel,
         name=name,
@@ -244,8 +241,6 @@
     with jax.named_scope("half_exchange"):
         own = jnp.concatenate([left_ops[:, 0], right_ops[:, 0]], 0)
         other = from_half(own)
-    with jax.named_scope("own_over_y"):
-        pieces = [[own]] + [[from_y(own, r)] for r in range(1, NY)]
     with jax.named_scope("psi_pack"):
         tab = jnp.concatenate(
             [
@@ -254,56 +249,54 @@
             ]
         )
         packed = call(psi_kernel, "psi_pack", (tab, psi[0]), [blocks(8)] * 2, size=3 << 20)
-        other, *packed = lax.optimization_barrier((other, *packed))
-    with jax.named_scope("other_over_y"):
-        pieces[0].append(other)
-        for r in range(1, NY):
-            pieces[r].append(from_y(other, r))
+    with jax.named_scope("over_y"):
+        pieces = [jnp.concatenate([own, other], 0)]
+        pieces += [from_y(pieces[0], r) for r in range(1, NY)]
     with jax.named_scope("psi_shift"):
         starts = [from_shift(packed[n], n) for n in range(2)]
     with jax.named_scope("terms"):
-        if PSI_FIRST:
-            pieces, starts = lax.optimization_barrier((pieces, starts))
+        pieces, starts = lax.optimization_barrier((pieces, starts))
         left16, right16 = call(
-            terms_kernel, "terms", sum(pieces, []), [blocks(NK)] * 2, size=2 << 20
-        )
+            terms_kernel, "terms", pieces, [blocks(NK)] * 2, size=2 << 20
+        )
+    with jax.named_scope("right_core"):
+        right_swapped = from_core(right16)
     with jax.named_scope("left_shift"):
         left = [from_shift(left16, n) for n in range(2)]
     with jax.named_scope("right_over_x"):
         right = [right16] + [from_x(right16, r) for r in range(1, NX)]
     with jax.named_scope("right_core"):
-        right = right + [from_core(value) for value in right]
+        right = right + [right_swapped] + [from_core(value) for value in right[1:]]
 
     inner = [pltpu.VMEM((2, NK * M, 8 * M), jnp.bfloat16)]
     flops = 2 * 16 * NK * 2 * M**3
     with jax.named_scope("first_product"):
         keep, give = call(
             first_product_kernel, "first_product", (tab, *left, *right, *starts),
-            [blocks(NX, 2)] * 2, inner, flops, 6 << 20, 32 << 20,
+            [blocks(NX, 2)] * 2, inner, flops, 6 << 20, 20 << 20,
         )
     with jax.named_scope("first_core"):
         got = from_core(give)
     with jax.named_scope("second_product"):
         seconds = call(
             second_product_kernel, "second_product", (*left, *right, keep, give),
-            [blocks(8)] * 2, inner, flops, 6 << 20, 32 << 20,
-        )
+            [blocks(8)] * 2, inner, flops, 6 << 20, 20 << 20,
+        )
+    with jax.named_scope("second_shift"):
+        back = [to_shift(seconds[n], n) for n in range(2)]
     with jax.named_scope("first_out"):
         got, *seconds = lax.optimization_barrier((got, *seconds))
         sent = call(sent_kernel, "first_sent", (keep, got), blocks(NX * NY, 4), size=2 << 20)
         came = lax.all_to_all(sent, ("x", "y"), 0, 0, tiled=True).reshape(64, M, M)
-    with jax.named_scope("second_shift"):
-        back = [to_shift(seconds[n], n) for n in range(2)]
     with jax.named_scope("second_over_y"):
         parts = call(
             second_pack_kernel, "second_pack", (tab, *back), [blocks(8)] * NY,
             [pltpu.VMEM((NY, 8, M, M), jnp.bfloat16)], size=2 << 20,
         )
-        if OUT_FIRST:
-            came, *parts = lax.optimization_barrier((came, *parts))
         parts = [parts[0]] + [from_y(parts[r], -r) for r in range(1, NY)]
     with jax.named_scope("first_order"):
         first_out = call(first_order_kernel, "first_order", (tab, came), blocks(64), size=4 << 20)
+    first_out, *parts = lax.optimization_barrier((first_out, *parts))
     with jax.named_scope("second_pick"):
         second_out = call(
             second_pick_kernel, "second_pick", (tab, *parts), blocks(8), size=2 << 20

time: 162 us -> 152 us (0.938)
  starting transfers between devices: 95.9 us -> 88.1 us
    all_to_all x1, waiting for transfers between devices: 12.8 us -> 0.01 us  [on_device(): came = lax.all_to_all(sent, ('x', 'y'), 0, 0, tiled=True).reshape(64, M, M)]
    ppermute x24 -> x21, waiting for transfers between devices: 30.9 us -> 42.3 us  [permute(): return lax.ppermute(value, AXES, pairs)]
    ppermute x24 -> x21, starting transfers between devices: 89.5 us -> 82.8 us  [permute(): return lax.ppermute(value, AXES, pairs)]
  transfers between devices with their start and end apart: 25 -> 22, of which waited for: 8 -> 7; matrix products, arithmetic and copies ran while one was open for 0% -> 1% of each run, Pallas kernels for 5% -> 6%
where the time goes in v4:
time: 152 us
  starting transfers between devices  88.1 us (58%)
  waiting for transfers between devices  42.3 us (28%)
  Pallas kernels  15.5 us (10%)
  local copies, waits for them, and re-layouts  3.7 us (2%)
    ppermute x21, starting transfers between devices, permute(): return lax.ppermute(value, AXES, pairs)  82.8 us
    ppermute x21, waiting for transfers between devices, permute(): return lax.ppermute(value, AXES, pairs)  42.3 us
    pallas_call x8, Pallas kernels, call(): pl.pallas_call(kernel, name=name, out_shape=outputs, in_specs=[SMEM if v....  15.5 us
    all_to_all x1, starting transfers between devices, on_device(): came = lax.all_to_all(sent, ('x', 'y'), 0, 0, tiled=True).reshape(64, M, M)  5.34 us
  transfers between devices with their start and end apart: 22, of which 7 were waited for; matrix products, arithmetic and copies ran while one was open for 1% of the time, Pallas kernels for 6%

profile of v4, /device:TPU:1, one launch (start us, length us, event | category | flops | bytes accessed | tf_op | source)
XLA Modules:
  0.0 151.5 jit_solution(17146464382306989929)
XLA Ops:
  0.6 0.9 pad_maximum_fusion.1
  1.6 16.3 %collective-permute-start = (bf16[4,128,128]{2,1,0:T(8,128)(2,1)S(1)}, bf16[4,128,128]{2,1,0:T(8,128)(2,1)S(1)}, u32[]{:S(2)}, u32[]{:S(2)}) collective-permute-start(bf16[4,128,128]{2,1,0:T(8,128)(2,1)S(1)} %pad_maximum_fusion.1), channel_id=1, source_target_pairs={{0,1},{2,3},{4,5},{6,7},{8,9},{10,11},{12,13},{14,15},{16,17},{18,... | collective-permute-start | bytes 393224 | tf_op jit(solution)/shard_map/half_exchange/ppermute | solution.py:49
  17.9 0.8 concatenate.10.tab
  18.7 1.6 %copy-done.1 = bf16[1,64,128,128]{3,2,1,0:T(8,128)(2,1)S(1)} copy-done((bf16[1,64,128,128]{3,2,1,0:T(8,128)(2,1)S(1)}, bf16[1,64,128,128]{3,2,1,0:T(8,128)(2,1)}, u32[]{:S(2)}) %copy-start.1) | copy-done | bytes 2097176
  20.2 0.8 psi_pack.1
  21.0 4.0 %collective-permute-start.4 = (bf16[8,128,128]{2,1,0:T(8,128)(2,1)S(1)}, bf16[8,128,128]{2,1,0:T(8,128)(2,1)S(1)}, u32[]{:S(2)}, u32[]{:S(2)}) collective-permute-start(bf16[8,128,128]{2,1,0:T(8,128)(2,1)S(1)} %get-tuple-element.26), channel_id=1, source_target_pairs={{0,33},{2,26},{4,45},{6,55},{8,41},{10,34},{12,53},{14,63},{16,49}... | collective-permute-start | bytes 786440 | tf_op jit(solution)/shard_map/psi_shift/ppermute | solution.py:49
  25.1 0.7 collective-permute-start.5
  25.8 3.1 %collective-permute-start.3 = (bf16[8,128,128]{2,1,0:T(8,128)(2,1)S(1)}, bf16[8,128,128]{2,1,0:T(8,128)(2,1)S(1)}, u32[]{:S(2)}, u32[]{:S(2)}) collective-permute-start(bf16[8,128,128]{2,1,0:T(8,128)(2,1)S(1)} %pad_maximum_fusion.refs_0_), channel_id=1, source_target_pairs={{0,2},{2,4},{4,6},{6,0},{8,10},{10,12},{12,14},{14,8},{16,18},{18,... | collective-permute-start | bytes 786440 | tf_op jit(solution)/shard_map/over_y/ppermute | solution.py:49
  28.9 7.4 %collective-permute-start.2 = (bf16[8,128,128]{2,1,0:T(8,128)(2,1)S(1)}, bf16[8,128,128]{2,1,0:T(8,128)(2,1)S(1)}, u32[]{:S(2)}, u32[]{:S(2)}) collective-permute-start(bf16[8,128,128]{2,1,0:T(8,128)(2,1)S(1)} %pad_maximum_fusion.refs_0_), channel_id=1, source_target_pairs={{0,4},{2,6},{4,0},{6,2},{8,12},{10,14},{12,8},{14,10},{16,20},{18,... | collective-permute-start | bytes 786440 | tf_op jit(solution)/shard_map/over_y/ppermute | solution.py:49
  36.3 3.0 %collective-permute-start.1 = (bf16[8,128,128]{2,1,0:T(8,128)(2,1)S(1)}, bf16[8,128,128]{2,1,0:T(8,128)(2,1)S(1)}, u32[]{:S(2)}, u32[]{:S(2)}) collective-permute-start(bf16[8,128,128]{2,1,0:T(8,128)(2,1)S(1)} %pad_maximum_fusion.refs_0_), channel_id=1, source_target_pairs={{0,6},{2,0},{4,2},{6,4},{8,14},{10,8},{12,10},{14,12},{16,22},{18,... | collective-permute-start | bytes 786440 | tf_op jit(solution)/shard_map/over_y/ppermute | solution.py:49
  39.3 0.0 collective-permute-done.5.refs_11_
  39.3 0.3 collective-permute-done.3.refs_3_
  39.6 6.5 %collective-permute-done.2.refs_2_ = bf16[8,128,128]{2,1,0:T(8,128)(2,1)S(1)} collective-permute-done((bf16[8,128,128]{2,1,0:T(8,128)(2,1)S(1)}, bf16[8,128,128]{2,1,0:T(8,128)(2,1)S(1)}, u32[]{:S(2)}, u32[]{:S(2)}) %collective-permute-start.2) | collective-permute-done | bytes 262176 | tf_op jit(solution)/shard_map/over_y/ppermute | solution.py:49
  46.1 1.3 collective-permute-done.1.refs_1_
  47.4 0.1 terms.1
  47.5 0.7 collective-permute-start.7
  48.2 3.1 %collective-permute-start.10 = (bf16[16,128,128]{2,1,0:T(8,128)(2,1)S(1)}, bf16[16,128,128]{2,1,0:T(8,128)(2,1)S(1)}, u32[]{:S(2)}, u32[]{:S(2)}) collective-permute-start(bf16[16,128,128]{2,1,0:T(8,128)(2,1)S(1)} %get-tuple-element.33.refs_2_), channel_id=1, source_target_pairs={{0,128},{2,130},{4,132},{6,134},{8,136},{10,138},{12,140},{14,142}... | collective-permute-start | bytes 1572872 | tf_op jit(solution)/shard_map/right_over_x/ppermute | solution.py:49
  51.3 4.4 %collective-permute-start.9 = (bf16[16,128,128]{2,1,0:T(8,128)(2,1)S(1)}, bf16[16,128,128]{2,1,0:T(8,128)(2,1)S(1)}, u32[]{:S(2)}, u32[]{:S(2)}) collective-permute-start(bf16[16,128,128]{2,1,0:T(8,128)(2,1)S(1)} %get-tuple-element.33.refs_2_), channel_id=1, source_target_pairs={{0,256},{2,258},{4,260},{6,262},{8,264},{10,266},{12,268},{14,270}... | collective-permute-start | bytes 1572872 | tf_op jit(solution)/shard_map/right_over_x/ppermute | solution.py:49
  55.7 3.1 %collective-permute-start.8 = (bf16[16,128,128]{2,1,0:T(8,128)(2,1)S(1)}, bf16[16,128,128]{2,1,0:T(8,128)(2,1)S(1)}, u32[]{:S(2)}, u32[]{:S(2)}) collective-permute-start(bf16[16,128,128]{2,1,0:T(8,128)(2,1)S(1)} %get-tuple-element.33.refs_2_), channel_id=1, source_target_pairs={{0,384},{2,386},{4,388},{6,390},{8,392},{10,394},{12,396},{14,398}... | collective-permute-start | bytes 1572872 | tf_op jit(solution)/shard_map/right_over_x/ppermute | solution.py:49
  58.8 3.0 %collective-permute-start.6 = (bf16[16,128,128]{2,1,0:T(8,128)(2,1)S(1)}, bf16[16,128,128]{2,1,0:T(8,128)(2,1)S(1)}, u32[]{:S(2)}, u32[]{:S(2)}) collective-permute-start(bf16[16,128,128]{2,1,0:T(8,128)(2,1)S(1)} %get-tuple-element.32), channel_id=1, source_target_pairs={{0,33},{2,26},{4,45},{6,55},{8,41},{10,34},{12,53},{14,63},{16,49}... | collective-permute-start | bytes 1572872 | tf_op jit(solution)/shard_map/left_shift/ppermute | solution.py:49
  61.8 7.7 %collective-permute-start.11 = (bf16[16,128,128]{2,1,0:T(8,128)(2,1)S(1)}, bf16[16,128,128]{2,1,0:T(8,128)(2,1)S(1)}, u32[]{:S(2)}, u32[]{:S(2)}) collective-permute-start(bf16[16,128,128]{2,1,0:T(8,128)(2,1)S(1)} %get-tuple-element.33.refs_2_), channel_id=1, source_target_pairs={{0,64},{2,66},{4,68},{6,70},{8,72},{10,74},{12,76},{14,78},{16,80}... | collective-permute-start | bytes 1572872 | tf_op jit(solution)/shard_map/right_core/ppermute | solution.py:49
  69.6 1.9 %collective-permute-start.14 = (bf16[16,128,128]{2,1,0:T(8,128)(2,1)S(1)}, bf16[16,128,128]{2,1,0:T(8,128)(2,1)S(1)}, u32[]{:S(2)}, u32[]{:S(2)}) collective-permute-start(bf16[16,128,128]{2,1,0:T(8,128)(2,1)S(1)} %collective-permute-done.10.refs_5_), channel_id=1, source_target_pairs={{0,64},{2,66},{4,68},{6,70},{8,72},{10,74},{12,76},{14,78},{16,80}... | collective-permute-start | bytes 1572872 | tf_op jit(solution)/shard_map/right_core/ppermute | solution.py:49
  71.5 4.3 %collective-permute-done.9.refs_4_ = bf16[16,128,128]{2,1,0:T(8,128)(2,1)S(1)} collective-permute-done((bf16[16,128,128]{2,1,0:T(8,128)(2,1)S(1)}, bf16[16,128,128]{2,1,0:T(8,128)(2,1)S(1)}, u32[]{:S(2)}, u32[]{:S(2)}) %collective-permute-start.9) | collective-permute-done | bytes 524320 | tf_op jit(solution)/shard_map/right_over_x/ppermute | solution.py:49
  75.8 3.9 %collective-permute-start.13 = (bf16[16,128,128]{2,1,0:T(8,128)(2,1)S(1)}, bf16[16,128,128]{2,1,0:T(8,128)(2,1)S(1)}, u32[]{:S(2)}, u32[]{:S(2)}) collective-permute-start(bf16[16,128,128]{2,1,0:T(8,128)(2,1)S(1)} %collective-permute-done.9.refs_4_), channel_id=1, source_target_pairs={{0,64},{2,66},{4,68},{6,70},{8,72},{10,74},{12,76},{14,78},{16,80}... | collective-permute-start | bytes 1572872 | tf_op jit(solution)/shard_map/right_core/ppermute | solution.py:49
  79.8 1.9 %collective-permute-start.12 = (bf16[16,128,128]{2,1,0:T(8,128)(2,1)S(1)}, bf16[16,128,128]{2,1,0:T(8,128)(2,1)S(1)}, u32[]{:S(2)}, u32[]{:S(2)}) collective-permute-start(bf16[16,128,128]{2,1,0:T(8,128)(2,1)S(1)} %collective-permute-done.8.refs_3_), channel_id=1, source_target_pairs={{0,64},{2,66},{4,68},{6,70},{8,72},{10,74},{12,76},{14,78},{16,80}... | collective-permute-start | bytes 1572872 | tf_op jit(solution)/shard_map/right_core/ppermute | solution.py:49
  81.7 7.9 %collective-permute-done.6.refs_0_ = bf16[16,128,128]{2,1,0:T(8,128)(2,1)S(1)} collective-permute-done((bf16[16,128,128]{2,1,0:T(8,128)(2,1)S(1)}, bf16[16,128,128]{2,1,0:T(8,128)(2,1)S(1)}, u32[]{:S(2)}, u32[]{:S(2)}) %collective-permute-start.6) | collective-permute-done | bytes 524320 | tf_op jit(solution)/shard_map/left_shift/ppermute | solution.py:49
  89.6 0.0 collective-permute-done.14.refs_9_
  89.6 0.0 collective-permute-done.13.refs_8_
  89.6 0.0 collective-permute-done.12.refs_7_
  89.6 4.6 %first_product.1 = (bf16[4,2,128,128]{3,2,1,0:T(8,128)(2,1)S(1)}, bf16[4,2,128,128]{3,2,1,0:T(8,128)(2,1)S(1)}) custom-call(s32[8,64]{1,0:T(8,128)S(1)} %concatenate.10.tab, bf16[16,128,128]{2,1,0:T(8,128)(2,1)S(1)} %collective-permute-done.6.refs_0_, bf16[16,128,128]{2,1,0:T(8,128)(2,1)S(1)} %collective-permute-done.7.refs_1_, ...), custom_call_target="tpu_custom_call" | custom-call | flops 2147483648 | bytes 6291456 | tf_op jit(solution)/shard_map/first_product/first_product/pallas_call | solution.py:225
  94.2 1.9 %collective-permute-start.15 = (bf16[4,2,128,128]{3,2,1,0:T(8,128)(2,1)S(1)}, bf16[4,2,128,128]{3,2,1,0:T(8,128)(2,1)S(1)}, u32[]{:S(2)}, u32[]{:S(2)}) collective-permute-start(bf16[4,2,128,128]{3,2,1,0:T(8,128)(2,1)S(1)} %get-tuple-element.37.refs_11_), channel_id=1, source_target_pairs={{0,64},{2,66},{4,68},{6,70},{8,72},{10,74},{12,76},{14,78},{16,80}... | collective-permute-start | bytes 786440 | tf_op jit(solution)/shard_map/first_core/ppermute | solution.py:49
  96.2 4.0 %second_product.1 = (bf16[8,128,128]{2,1,0:T(8,128)(2,1)S(1)}, bf16[8,128,128]{2,1,0:T(8,128)(2,1)S(1)}) custom-call(bf16[16,128,128]{2,1,0:T(8,128)(2,1)S(1)} %collective-permute-done.6.refs_0_, bf16[16,128,128]{2,1,0:T(8,128)(2,1)S(1)} %collective-permute-done.7.refs_1_, bf16[16,128,128]{2,1,0:T(8,128)(2,1)S(1)} %get-tuple-element.33.refs_2_, ...), custom_call_target="tpu_custom_call" | custom-call | flops 2147483648 | bytes 6291456 | tf_op jit(solution)/shard_map/second_product/second_product/pallas_call | solution.py:225
  100.2 0.3 first_sent.1
  100.5 0.0 copy-start
  100.5 1.3 copy-done
  101.8 5.3 %all-to-all-start = ((bf16[16,4,128,128]{3,2,1,0:T(8,128)(2,1)}), bf16[16,4,128,128]{3,2,1,0:T(8,128)(2,1)S(1)}, u32[]{:S(2)}, u32[]{:S(2)}) async-start(bf16[16,4,128,128]{3,2,1,0:T(8,128)(2,1)} %copy-done), calls=%async_computation | async-start | bytes 4194304 | tf_op jit(solution)/shard_map/first_out/all_to_all | solution.py:290
  107.1 4.3 %collective-permute-start.16 = (bf16[8,128,128]{2,1,0:T(8,128)(2,1)S(1)}, bf16[8,128,128]{2,1,0:T(8,128)(2,1)S(1)}, u32[]{:S(2)}, u32[]{:S(2)}) collective-permute-start(bf16[8,128,128]{2,1,0:T(8,128)(2,1)S(1)} %get-tuple-element.38), channel_id=1, source_target_pairs={{0,32},{2,43},{4,28},{6,22},{8,40},{10,51},{12,36},{14,30},{16,48}... | collective-permute-start | bytes 786440 | tf_op jit(solution)/shard_map/second_shift/ppermute | solution.py:49
  111.4 0.7 collective-permute-start.17
  112.1 13.9 %collective-permute-done.16.back0 = bf16[8,128,128]{2,1,0:T(8,128)(2,1)S(1)} collective-permute-done((bf16[8,128,128]{2,1,0:T(8,128)(2,1)S(1)}, bf16[8,128,128]{2,1,0:T(8,128)(2,1)S(1)}, u32[]{:S(2)}, u32[]{:S(2)}) %collective-permute-start.16) | collective-permute-done | bytes 262176 | tf_op jit(solution)/shard_map/second_shift/ppermute | solution.py:49
  126.0 0.0 collective-permute-done.17.back1
  126.0 2.0 %second_pack.1 = (bf16[8,128,128]{2,1,0:T(8,128)(2,1)S(1)}, bf16[8,128,128]{2,1,0:T(8,128)(2,1)}, bf16[8,128,128]{2,1,0:T(8,128)(2,1)}, bf16[8,128,128]{2,1,0:T(8,128)(2,1)S(1)}) custom-call(s32[8,64]{1,0:T(8,128)S(1)} %concatenate.10.tab, bf16[8,128,128]{2,1,0:T(8,128)(2,1)S(1)} %collective-permute-done.16.back0, ...), custom_call_target="tpu_custom_call" | custom-call | bytes 2097152 | tf_op jit(solution)/shard_map/second_over_y/second_pack/pallas_call | solution.py:225
  128.0 4.1 %collective-permute-start.18 = (bf16[8,128,128]{2,1,0:T(8,128)(2,1)}, bf16[8,128,128]{2,1,0:T(8,128)(2,1)S(1)}, u32[]{:S(2)}, u32[]{:S(2)}) collective-permute-start(bf16[8,128,128]{2,1,0:T(8,128)(2,1)} %get-tuple-element.42), channel_id=1, source_target_pairs={{0,2},{2,4},{4,6},{6,0},{8,10},{10,12},{12,14},{14,8},{16,18},{18,... | collective-permute-start | bytes 786440 | tf_op jit(solution)/shard_map/second_over_y/ppermute | solution.py:49
  132.1 4.4 %collective-permute-start.19 = (bf16[8,128,128]{2,1,0:T(8,128)(2,1)}, bf16[8,128,128]{2,1,0:T(8,128)(2,1)S(1)}, u32[]{:S(2)}, u32[]{:S(2)}) collective-permute-start(bf16[8,128,128]{2,1,0:T(8,128)(2,1)} %get-tuple-element.43), channel_id=1, source_target_pairs={{0,4},{2,6},{4,0},{6,2},{8,12},{10,14},{12,8},{14,10},{16,20},{18,... | collective-permute-start | bytes 786440 | tf_op jit(solution)/shard_map/second_over_y/ppermute | solution.py:49
  136.6 3.2 %collective-permute-start.20 = (bf16[8,128,128]{2,1,0:T(8,128)(2,1)S(1)}, bf16[8,128,128]{2,1,0:T(8,128)(2,1)S(1)}, u32[]{:S(2)}, u32[]{:S(2)}) collective-permute-start(bf16[8,128,128]{2,1,0:T(8,128)(2,1)S(1)} %get-tuple-element.44), channel_id=1, source_target_pairs={{0,6},{2,0},{4,2},{6,4},{8,14},{10,8},{12,10},{14,12},{16,22},{18,... | collective-permute-start | bytes 786440 | tf_op jit(solution)/shard_map/second_over_y/ppermute | solution.py:49
  139.7 0.0 all-to-all-done
  139.7 2.3 %first_order.1 = bf16[64,128,128]{2,1,0:T(8,128)(2,1)} custom-call(s32[8,64]{1,0:T(8,128)S(1)} %concatenate.10.tab, bf16[64,128,128]{2,1,0:T(8,128)(2,1)S(1)} %bitcast.12), custom_call_target="tpu_custom_call" | custom-call | bytes 4194304 | tf_op jit(solution)/shard_map/first_order/first_order/pallas_call | solution.py:225
  142.0 8.0 %collective-permute-done.19.part2 = bf16[8,128,128]{2,1,0:T(8,128)(2,1)S(1)} collective-permute-done((bf16[8,128,128]{2,1,0:T(8,128)(2,1)}, bf16[8,128,128]{2,1,0:T(8,128)(2,1)S(1)}, u32[]{:S(2)}, u32[]{:S(2)}) %collective-permute-start.19) | collective-permute-done | bytes 262176 | tf_op jit(solution)/shard_map/second_over_y/ppermute | solution.py:49
  150.0 1.5 second_pick.1
  (15 shorter events, 0.1 us)
Async XLA Ops:
  0.6 25.1 %copy-start.2 = (bf16[2,1,128,128]{3,2,1,0:T(8,128)(2,1)S(1)}, bf16[2,1,128,128]{3,2,1,0:T(8,128)(2,1)}, u32[]{:S(2)}) copy-start(bf16[2,1,128,128]{3,2,1,0:T(8,128)(2,1)} %param.12) | copy-start | bytes 196612
  0.6 25.1 %copy-start.3 = (bf16[2,1,128,128]{3,2,1,0:T(8,128)(2,1)S(1)}, bf16[2,1,128,128]{3,2,1,0:T(8,128)(2,1)}, u32[]{:S(2)}) copy-start(bf16[2,1,128,128]{3,2,1,0:T(8,128)(2,1)} %param.11) | copy-start | bytes 196612
  1.6 24.2 %collective-permute-start = (bf16[4,128,128]{2,1,0:T(8,128)(2,1)S(1)}, bf16[4,128,128]{2,1,0:T(8,128)(2,1)S(1)}, u32[]{:S(2)}, u32[]{:S(2)}) collective-permute-start(bf16[4,128,128]{2,1,0:T(8,128)(2,1)S(1)} %pad_maximum_fusion.1), channel_id=1, source_target_pairs={{0,1},{2,3},{4,5},{6,7},{8,9},{10,11},{12,13},{14,15},{16,17},{18,... | collective-permute-start | bytes 393224 | tf_op jit(solution)/shard_map/half_exchange/ppermute | solution.py:49
  18.6 1.6 %copy-start.1 = (bf16[1,64,128,128]{3,2,1,0:T(8,128)(2,1)S(1)}, bf16[1,64,128,128]{3,2,1,0:T(8,128)(2,1)}, u32[]{:S(2)}) copy-start(bf16[1,64,128,128]{3,2,1,0:T(8,128)(2,1)} %param.10) | copy-start | bytes 6291460
  21.0 18.2 %collective-permute-start.4 = (bf16[8,128,128]{2,1,0:T(8,128)(2,1)S(1)}, bf16[8,128,128]{2,1,0:T(8,128)(2,1)S(1)}, u32[]{:S(2)}, u32[]{:S(2)}) collective-permute-start(bf16[8,128,128]{2,1,0:T(8,128)(2,1)S(1)} %get-tuple-element.26), channel_id=1, source_target_pairs={{0,33},{2,26},{4,45},{6,55},{8,41},{10,34},{12,53},{14,63},{16,49}... | collective-permute-start | bytes 786440 | tf_op jit(solution)/shard_map/psi_shift/ppermute | solution.py:49
  25.1 14.2 %collective-permute-start.5 = (bf16[8,128,128]{2,1,0:T(8,128)(2,1)S(1)}, bf16[8,128,128]{2,1,0:T(8,128)(2,1)S(1)}, u32[]{:S(2)}, u32[]{:S(2)}) collective-permute-start(bf16[8,128,128]{2,1,0:T(8,128)(2,1)S(1)} %get-tuple-element.27), channel_id=1, source_target_pairs={{0,0},{2,59},{4,12},{6,22},{8,8},{10,2},{12,20},{14,30},{16,16},{1... | collective-permute-start | bytes 786440 | tf_op jit(solution)/shard_map/psi_shift/ppermute | solution.py:49
  25.8 13.8 %collective-permute-start.3 = (bf16[8,128,128]{2,1,0:T(8,128)(2,1)S(1)}, bf16[8,128,128]{2,1,0:T(8,128)(2,1)S(1)}, u32[]{:S(2)}, u32[]{:S(2)}) collective-permute-start(bf16[8,128,128]{2,1,0:T(8,128)(2,1)S(1)} %pad_maximum_fusion.refs_0_), channel_id=1, source_target_pairs={{0,2},{2,4},{4,6},{6,0},{8,10},{10,12},{12,14},{14,8},{16,18},{18,... | collective-permute-start | bytes 786440 | tf_op jit(solution)/shard_map/over_y/ppermute | solution.py:49
  28.9 17.2 %collective-permute-start.2 = (bf16[8,128,128]{2,1,0:T(8,128)(2,1)S(1)}, bf16[8,128,128]{2,1,0:T(8,128)(2,1)S(1)}, u32[]{:S(2)}, u32[]{:S(2)}) collective-permute-start(bf16[8,128,128]{2,1,0:T(8,128)(2,1)S(1)} %pad_maximum_fusion.refs_0_), channel_id=1, source_target_pairs={{0,4},{2,6},{4,0},{6,2},{8,12},{10,14},{12,8},{14,10},{16,20},{18,... | collective-permute-start | bytes 786440 | tf_op jit(solution)/shard_map/over_y/ppermute | solution.py:49
  36.3 11.1 %collective-permute-start.1 = (bf16[8,128,128]{2,1,0:T(8,128)(2,1)S(1)}, bf16[8,128,128]{2,1,0:T(8,128)(2,1)S(1)}, u32[]{:S(2)}, u32[]{:S(2)}) collective-permute-start(bf16[8,128,128]{2,1,0:T(8,128)(2,1)S(1)} %pad_maximum_fusion.refs_0_), channel_id=1, source_target_pairs={{0,6},{2,0},{4,2},{6,4},{8,14},{10,8},{12,10},{14,12},{16,22},{18,... | collective-permute-start | bytes 786440 | tf_op jit(solution)/shard_map/over_y/ppermute | solution.py:49
  47.5 14.3 %collective-permute-start.7 = (bf16[16,128,128]{2,1,0:T(8,128)(2,1)S(1)}, bf16[16,128,128]{2,1,0:T(8,128)(2,1)S(1)}, u32[]{:S(2)}, u32[]{:S(2)}) collective-permute-start(bf16[16,128,128]{2,1,0:T(8,128)(2,1)S(1)} %get-tuple-element.32), channel_id=1, source_target_pairs={{0,0},{2,59},{4,12},{6,22},{8,8},{10,2},{12,20},{14,30},{16,16},{1... | collective-permute-start | bytes 1572872 | tf_op jit(solution)/shard_map/left_shift/ppermute | solution.py:49
  48.2 21.4 %collective-permute-start.10 = (bf16[16,128,128]{2,1,0:T(8,128)(2,1)S(1)}, bf16[16,128,128]{2,1,0:T(8,128)(2,1)S(1)}, u32[]{:S(2)}, u32[]{:S(2)}) collective-permute-start(bf16[16,128,128]{2,1,0:T(8,128)(2,1)S(1)} %get-tuple-element.33.refs_2_), channel_id=1, source_target_pairs={{0,128},{2,130},{4,132},{6,134},{8,136},{10,138},{12,140},{14,142}... | collective-permute-start | bytes 1572872 | tf_op jit(solution)/shard_map/right_over_x/ppermute | solution.py:49
  51.3 24.5 %collective-permute-start.9 = (bf16[16,128,128]{2,1,0:T(8,128)(2,1)S(1)}, bf16[16,128,128]{2,1,0:T(8,128)(2,1)S(1)}, u32[]{:S(2)}, u32[]{:S(2)}) collective-permute-start(bf16[16,128,128]{2,1,0:T(8,128)(2,1)S(1)} %get-tuple-element.33.refs_2_), channel_id=1, source_target_pairs={{0,256},{2,258},{4,260},{6,262},{8,264},{10,266},{12,268},{14,270}... | collective-permute-start | bytes 1572872 | tf_op jit(solution)/shard_map/right_over_x/ppermute | solution.py:49
  55.7 24.1 %collective-permute-start.8 = (bf16[16,128,128]{2,1,0:T(8,128)(2,1)S(1)}, bf16[16,128,128]{2,1,0:T(8,128)(2,1)S(1)}, u32[]{:S(2)}, u32[]{:S(2)}) collective-permute-start(bf16[16,128,128]{2,1,0:T(8,128)(2,1)S(1)} %get-tuple-element.33.refs_2_), channel_id=1, source_target_pairs={{0,384},{2,386},{4,388},{6,390},{8,392},{10,394},{12,396},{14,398}... | collective-permute-start | bytes 1572872 | tf_op jit(solution)/shard_map/right_over_x/ppermute | solution.py:49
  58.8 30.9 %collective-permute-start.6 = (bf16[16,128,128]{2,1,0:T(8,128)(2,1)S(1)}, bf16[16,128,128]{2,1,0:T(8,128)(2,1)S(1)}, u32[]{:S(2)}, u32[]{:S(2)}) collective-permute-start(bf16[16,128,128]{2,1,0:T(8,128)(2,1)S(1)} %get-tuple-element.32), channel_id=1, source_target_pairs={{0,33},{2,26},{4,45},{6,55},{8,41},{10,34},{12,53},{14,63},{16,49}... | collective-permute-start | bytes 1572872 | tf_op jit(solution)/shard_map/left_shift/ppermute | solution.py:49
  61.8 27.8 %collective-permute-start.11 = (bf16[16,128,128]{2,1,0:T(8,128)(2,1)S(1)}, bf16[16,128,128]{2,1,0:T(8,128)(2,1)S(1)}, u32[]{:S(2)}, u32[]{:S(2)}) collective-permute-start(bf16[16,128,128]{2,1,0:T(8,128)(2,1)S(1)} %get-tuple-element.33.refs_2_), channel_id=1, source_target_pairs={{0,64},{2,66},{4,68},{6,70},{8,72},{10,74},{12,76},{14,78},{16,80}... | collective-permute-start | bytes 1572872 | tf_op jit(solution)/shard_map/right_core/ppermute | solution.py:49
  69.6 20.1 %collective-permute-start.14 = (bf16[16,128,128]{2,1,0:T(8,128)(2,1)S(1)}, bf16[16,128,128]{2,1,0:T(8,128)(2,1)S(1)}, u32[]{:S(2)}, u32[]{:S(2)}) collective-permute-start(bf16[16,128,128]{2,1,0:T(8,128)(2,1)S(1)} %collective-permute-done.10.refs_5_), channel_id=1, source_target_pairs={{0,64},{2,66},{4,68},{6,70},{8,72},{10,74},{12,76},{14,78},{16,80}... | collective-permute-start | bytes 1572872 | tf_op jit(solution)/shard_map/right_core/ppermute | solution.py:49
  75.8 13.8 %collective-permute-start.13 = (bf16[16,128,128]{2,1,0:T(8,128)(2,1)S(1)}, bf16[16,128,128]{2,1,0:T(8,128)(2,1)S(1)}, u32[]{:S(2)}, u32[]{:S(2)}) collective-permute-start(bf16[16,128,128]{2,1,0:T(8,128)(2,1)S(1)} %collective-permute-done.9.refs_4_), channel_id=1, source_target_pairs={{0,64},{2,66},{4,68},{6,70},{8,72},{10,74},{12,76},{14,78},{16,80}... | collective-permute-start | bytes 1572872 | tf_op jit(solution)/shard_map/right_core/ppermute | solution.py:49
  79.8 9.9 %collective-permute-start.12 = (bf16[16,128,128]{2,1,0:T(8,128)(2,1)S(1)}, bf16[16,128,128]{2,1,0:T(8,128)(2,1)S(1)}, u32[]{:S(2)}, u32[]{:S(2)}) collective-permute-start(bf16[16,128,128]{2,1,0:T(8,128)(2,1)S(1)} %collective-permute-done.8.refs_3_), channel_id=1, source_target_pairs={{0,64},{2,66},{4,68},{6,70},{8,72},{10,74},{12,76},{14,78},{16,80}... | collective-permute-start | bytes 1572872 | tf_op jit(solution)/shard_map/right_core/ppermute | solution.py:49
  94.2 5.9 %collective-permute-start.15 = (bf16[4,2,128,128]{3,2,1,0:T(8,128)(2,1)S(1)}, bf16[4,2,128,128]{3,2,1,0:T(8,128)(2,1)S(1)}, u32[]{:S(2)}, u32[]{:S(2)}) collective-permute-start(bf16[4,2,128,128]{3,2,1,0:T(8,128)(2,1)S(1)} %get-tuple-element.37.refs_11_), channel_id=1, source_target_pairs={{0,64},{2,66},{4,68},{6,70},{8,72},{10,74},{12,76},{14,78},{16,80}... | collective-permute-start | bytes 786440 | tf_op jit(solution)/shard_map/first_core/ppermute | solution.py:49
  100.5 1.3 copy-start
  101.8 37.9 %all-to-all-start = ((bf16[16,4,128,128]{3,2,1,0:T(8,128)(2,1)}), bf16[16,4,128,128]{3,2,1,0:T(8,128)(2,1)S(1)}, u32[]{:S(2)}, u32[]{:S(2)}) async-start(bf16[16,4,128,128]{3,2,1,0:T(8,128)(2,1)} %copy-done), calls=%async_computation | async-start | bytes 4194304 | tf_op jit(solution)/shard_map/first_out/all_to_all | solution.py:290
  107.1 18.9 %collective-permute-start.16 = (bf16[8,128,128]{2,1,0:T(8,128)(2,1)S(1)}, bf16[8,128,128]{2,1,0:T(8,128)(2,1)S(1)}, u32[]{:S(2)}, u32[]{:S(2)}) collective-permute-start(bf16[8,128,128]{2,1,0:T(8,128)(2,1)S(1)} %get-tuple-element.38), channel_id=1, source_target_pairs={{0,32},{2,43},{4,28},{6,22},{8,40},{10,51},{12,36},{14,30},{16,48}... | collective-permute-start | bytes 786440 | tf_op jit(solution)/shard_map/second_shift/ppermute | solution.py:49
  111.4 14.6 %collective-permute-start.17 = (bf16[8,128,128]{2,1,0:T(8,128)(2,1)S(1)}, bf16[8,128,128]{2,1,0:T(8,128)(2,1)S(1)}, u32[]{:S(2)}, u32[]{:S(2)}) collective-permute-start(bf16[8,128,128]{2,1,0:T(8,128)(2,1)S(1)} %get-tuple-element.39), channel_id=1, source_target_pairs={{0,0},{2,10},{4,61},{6,55},{8,8},{10,18},{12,4},{14,63},{16,16},{1... | collective-permute-start | bytes 786440 | tf_op jit(solution)/shard_map/second_shift/ppermute | solution.py:49
  128.0 14.0 %collective-permute-start.18 = (bf16[8,128,128]{2,1,0:T(8,128)(2,1)}, bf16[8,128,128]{2,1,0:T(8,128)(2,1)S(1)}, u32[]{:S(2)}, u32[]{:S(2)}) collective-permute-start(bf16[8,128,128]{2,1,0:T(8,128)(2,1)} %get-tuple-element.42), channel_id=1, source_target_pairs={{0,2},{2,4},{4,6},{6,0},{8,10},{10,12},{12,14},{14,8},{16,18},{18,... | collective-permute-start | bytes 786440 | tf_op jit(solution)/shard_map/second_over_y/ppermute | solution.py:49
  132.1 17.9 %collective-permute-start.19 = (bf16[8,128,128]{2,1,0:T(8,128)(2,1)}, bf16[8,128,128]{2,1,0:T(8,128)(2,1)S(1)}, u32[]{:S(2)}, u32[]{:S(2)}) collective-permute-start(bf16[8,128,128]{2,1,0:T(8,128)(2,1)} %get-tuple-element.43), channel_id=1, source_target_pairs={{0,4},{2,6},{4,0},{6,2},{8,12},{10,14},{12,8},{14,10},{16,20},{18,... | collective-permute-start | bytes 786440 | tf_op jit(solution)/shard_map/second_over_y/ppermute | solution.py:49
  136.6 13.5 %collective-permute-start.20 = (bf16[8,128,128]{2,1,0:T(8,128)(2,1)S(1)}, bf16[8,128,128]{2,1,0:T(8,128)(2,1)S(1)}, u32[]{:S(2)}, u32[]{:S(2)}) collective-permute-start(bf16[8,128,128]{2,1,0:T(8,128)(2,1)S(1)} %get-tuple-element.44), channel_id=1, source_target_pairs={{0,6},{2,0},{4,2},{6,4},{8,14},{10,8},{12,10},{14,12},{16,22},{18,... | collective-permute-start | bytes 786440 | tf_op jit(solution)/shard_map/second_over_y/ppermute | solution.py:49

commit v5 on v4

--- a/solution.py
+++ b/solution.py
@@ -17,9 +17,9 @@
 SLOT = ("x", "c", "z")
 SHIFT = np.array(
     [
-        [[4, 0], [-4, 0]],
-        [[-3, 1], [3, -1]],
-        [[3, -1], [-3, 1]],
+        [[0, 4], [0, -4]],
+        [[1, -3], [-1, 3]],
+        [[-1, 3], [1, -3]],
         [[2, -2], [-2, 2]],
     ],
     np.int32,
@@ -110,16 +110,6 @@
             for k in range(2):
                 left[place + k] = refs[r][4 * half + k]
                 right[place + k] = refs[r][4 * half + 2 + k]
-
-
-def sent_kernel(keep, got, out):
-    x = lax.axis_index("x")
-    for r in range(NX):
-        to_x = lax.rem(x + r, NX)
-        for to_y in range(NY):
-            for n in range(2):
-                out[to_x * NY + to_y, n] = keep[r, n]
-                out[to_x * NY + to_y, 2 + n] = got[r, n]
 
 
 def psi_kernel(tab, psi, out0, out1):
@@ -150,28 +140,28 @@
         yield jnp.dot(row, inner[n], preferred_element_type=jnp.float32)
 
 
-def first_product_kernel(tab, *refs):
-    left, right, starts, (keep, give, inner) = refs[:2], refs[2:10], refs[10:12], refs[12:]
-    x, c, z, y, h = here()
-
-    def state_of(j):
+def products_kernel(tab, *refs):
+    left, right, starts = refs[:2], refs[2:10], refs[10:12]
+    sent, out0, out1, first, inner = refs[12:]
+    x, c, z, y, h = here()
+
+    def states(j):
         return jnp.concatenate([starts[0][j], starts[1][j]], axis=0)
 
-    for n, value in enumerate(product(state_of, left, right, inner)):
+    for n, value in enumerate(product(states, left, right, inner)):
         a = tab[LEFT_ORDER, slot_of(x, c, z + shift_of(tab, y, c, n))]
         for j in range(2 * NX):
             b = right_sector(tab, x, c, z, j)
             block = masked(value[:, j * M : (j + 1) * M], tab, a, b).astype(jnp.bfloat16)
-            (keep if j < NX else give)[j % NX, n] = block
-
-
-def second_product_kernel(*refs):
-    left, right, (keep, give, out0, out1, inner) = refs[:2], refs[2:10], refs[10:]
-
-    def state_of(j):
-        return (keep if j < NX else give)[j % NX].reshape(2 * M, M)
-
-    for out, value in zip((out0, out1), product(state_of, left, right, inner)):
+            first[j, n] = block
+            to_x, to_c = lax.rem(x + j % NX, NX), c if j < NX else 1 - c
+            for to_y in range(NY):
+                sent[(to_x * NC + to_c) * NY + to_y, n] = block
+
+    def second_states(j):
+        return first[j].reshape(2 * M, M)
+
+    for out, value in zip((out0, out1), product(second_states, left, right, inner)):
         for j in range(2 * NX):
             out[j] = value[:, j * M : (j + 1) * M].astype(jnp.bfloat16)
 
@@ -179,11 +169,12 @@
 def first_order_kernel(tab, came, out):
     x, c, z, y, h = here()
     for x_from in range(NX):
-        for y_from in range(NY):
-            for i in range(4):
-                core = c if i < 2 else 1 - c
-                slot = slot_of(x_from, core, z + shift_of(tab, y_from, core, i % 2))
-                out[tab[LEFT_ORDER, slot]] = came[(x_from * NY + y_from) * 4 + i]
+        for c_from in range(NC):
+            for y_from in range(NY):
+                for n in range(2):
+                    slot = slot_of(x_from, c_from, z + shift_of(tab, y_from, c_from, n))
+                    place = ((x_from * NC + c_from) * NY + y_from) * 2 + n
+                    out[tab[LEFT_ORDER, slot]] = came[place]
 
 
 def second_pack_kernel(tab, back0, back1, out0, out1, out2, out3, packed):
@@ -268,26 +259,20 @@
     with jax.named_scope("right_core"):
         right = right + [right_swapped] + [from_core(value) for value in right[1:]]
 
-    inner = [pltpu.VMEM((2, NK * M, 8 * M), jnp.bfloat16)]
-    flops = 2 * 16 * NK * 2 * M**3
-    with jax.named_scope("first_product"):
-        keep, give = call(
-            first_product_kernel, "first_product", (tab, *left, *right, *starts),
-            [blocks(NX, 2)] * 2, inner, flops, 6 << 20, 20 << 20,
-        )
-    with jax.named_scope("first_core"):
-        got = from_core(give)
-    with jax.named_scope("second_product"):
-        seconds = call(
-            second_product_kernel, "second_product", (*left, *right, keep, give),
-            [blocks(8)] * 2, inner, flops, 6 << 20, 20 << 20,
-        )
+    with jax.named_scope("products"):
+        sent, *seconds = call(
+            products_kernel, "products", (tab, *left, *right, *starts),
+            [blocks(NX * NC * NY, 2), blocks(8), blocks(8)],
+            [
+                pltpu.VMEM((2 * NX, 2, M, M), jnp.bfloat16),
+                pltpu.VMEM((2, NK * M, 8 * M), jnp.bfloat16),
+            ],
+            4 * 16 * NK * 2 * M**3, 8 << 20, 20 << 20,
+        )
+    with jax.named_scope("first_out"):
+        came = lax.all_to_all(sent, ("x", "c", "y"), 0, 0, tiled=True).reshape(64, M, M)
     with jax.named_scope("second_shift"):
         back = [to_shift(seconds[n], n) for n in range(2)]
-    with jax.named_scope("first_out"):
-        got, *seconds = lax.optimization_barrier((got, *seconds))
-        sent = call(sent_kernel, "first_sent", (keep, got), blocks(NX * NY, 4), size=2 << 20)
-        came = lax.all_to_all(sent, ("x", "y"), 0, 0, tiled=True).reshape(64, M, M)
     with jax.named_scope("second_over_y"):
         parts = call(
             second_pack_kernel, "second_pack", (tab, *back), [blocks(8)] * NY,

time: 152 us -> 147 us (0.967)
  the two profiles are of different devices: /device:TPU:1 before, /device:TPU:15 now
where the time goes in v5:
time: 147 us
  starting transfers between devices  81.2 us (55%)
  waiting for transfers between devices  44.8 us (30%)
  Pallas kernels  14.9 us (10%)
  local copies, waits for them, and re-layouts  3.7 us (3%)
    ppermute x20, starting transfers between devices, permute(): return lax.ppermute(value, AXES, pairs)  75.2 us
    ppermute x20, waiting for transfers between devices, permute(): return lax.ppermute(value, AXES, pairs)  44.8 us
    pallas_call x6, Pallas kernels, call(): pl.pallas_call(kernel, name=name, out_shape=outputs, in_specs=[SMEM if v....  14.9 us
    all_to_all x1, starting transfers between devices, on_device(): lax.all_to_all(sent, ('x', 'c', 'y'), 0, 0, tiled=True).reshape(64, M, M)  6.02 us
  transfers between devices with their start and end apart: 21, of which 9 were waited for; matrix products, arithmetic and copies ran while one was open for 1% of the time, Pallas kernels for 3%

profile of v5, /device:TPU:15, one launch (start us, length us, event | category | flops | bytes accessed | tf_op | source)
XLA Modules:
  0.0 146.5 jit_solution(7783107113580430116)
XLA Ops:
  0.6 0.9 pad_maximum_fusion.1
  1.6 15.4 %collective-permute-start = (bf16[4,128,128]{2,1,0:T(8,128)(2,1)S(1)}, bf16[4,128,128]{2,1,0:T(8,128)(2,1)S(1)}, u32[]{:S(2)}, u32[]{:S(2)}) collective-permute-start(bf16[4,128,128]{2,1,0:T(8,128)(2,1)S(1)} %pad_maximum_fusion.1), channel_id=1, source_target_pairs={{0,1},{2,3},{4,5},{6,7},{8,9},{10,11},{12,13},{14,15},{16,17},{18,... | collective-permute-start | bytes 393224 | tf_op jit(solution)/shard_map/half_exchange/ppermute | solution.py:49
  17.0 0.8 concatenate.10.tab
  17.8 1.6 %copy-done = bf16[1,64,128,128]{3,2,1,0:T(8,128)(2,1)S(1)} copy-done((bf16[1,64,128,128]{3,2,1,0:T(8,128)(2,1)S(1)}, bf16[1,64,128,128]{3,2,1,0:T(8,128)(2,1)}, u32[]{:S(2)}) %copy-start) | copy-done | bytes 2097176
  19.4 0.8 psi_pack.1
  20.2 2.6 %collective-permute-start.4 = (bf16[8,128,128]{2,1,0:T(8,128)(2,1)S(1)}, bf16[8,128,128]{2,1,0:T(8,128)(2,1)S(1)}, u32[]{:S(2)}, u32[]{:S(2)}) collective-permute-start(bf16[8,128,128]{2,1,0:T(8,128)(2,1)S(1)} %get-tuple-element.24), channel_id=1, source_target_pairs={{0,0},{2,59},{4,12},{6,55},{8,8},{10,2},{12,20},{14,63},{16,16},{1... | collective-permute-start | bytes 786440 | tf_op jit(solution)/shard_map/psi_shift/ppermute | solution.py:49
  22.9 1.9 %collective-permute-start.5 = (bf16[8,128,128]{2,1,0:T(8,128)(2,1)S(1)}, bf16[8,128,128]{2,1,0:T(8,128)(2,1)S(1)}, u32[]{:S(2)}, u32[]{:S(2)}) collective-permute-start(bf16[8,128,128]{2,1,0:T(8,128)(2,1)S(1)} %get-tuple-element.25), channel_id=1, source_target_pairs={{0,33},{2,26},{4,45},{6,22},{8,41},{10,34},{12,53},{14,30},{16,49}... | collective-permute-start | bytes 786440 | tf_op jit(solution)/shard_map/psi_shift/ppermute | solution.py:49
  24.9 4.8 %collective-permute-start.3 = (bf16[8,128,128]{2,1,0:T(8,128)(2,1)S(1)}, bf16[8,128,128]{2,1,0:T(8,128)(2,1)S(1)}, u32[]{:S(2)}, u32[]{:S(2)}) collective-permute-start(bf16[8,128,128]{2,1,0:T(8,128)(2,1)S(1)} %pad_maximum_fusion.refs_0_), channel_id=1, source_target_pairs={{0,2},{2,4},{4,6},{6,0},{8,10},{10,12},{12,14},{14,8},{16,18},{18,... | collective-permute-start | bytes 786440 | tf_op jit(solution)/shard_map/over_y/ppermute | solution.py:49
  29.7 3.8 %collective-permute-start.2 = (bf16[8,128,128]{2,1,0:T(8,128)(2,1)S(1)}, bf16[8,128,128]{2,1,0:T(8,128)(2,1)S(1)}, u32[]{:S(2)}, u32[]{:S(2)}) collective-permute-start(bf16[8,128,128]{2,1,0:T(8,128)(2,1)S(1)} %pad_maximum_fusion.refs_0_), channel_id=1, source_target_pairs={{0,4},{2,6},{4,0},{6,2},{8,12},{10,14},{12,8},{14,10},{16,20},{18,... | collective-permute-start | bytes 786440 | tf_op jit(solution)/shard_map/over_y/ppermute | solution.py:49
  33.6 4.0 %collective-permute-start.1 = (bf16[8,128,128]{2,1,0:T(8,128)(2,1)S(1)}, bf16[8,128,128]{2,1,0:T(8,128)(2,1)S(1)}, u32[]{:S(2)}, u32[]{:S(2)}) collective-permute-start(bf16[8,128,128]{2,1,0:T(8,128)(2,1)S(1)} %pad_maximum_fusion.refs_0_), channel_id=1, source_target_pairs={{0,6},{2,0},{4,2},{6,4},{8,14},{10,8},{12,10},{14,12},{16,22},{18,... | collective-permute-start | bytes 786440 | tf_op jit(solution)/shard_map/over_y/ppermute | solution.py:49
  37.5 3.6 %collective-permute-done.5.refs_11_ = bf16[8,128,128]{2,1,0:T(8,128)(2,1)S(1)} collective-permute-done((bf16[8,128,128]{2,1,0:T(8,128)(2,1)S(1)}, bf16[8,128,128]{2,1,0:T(8,128)(2,1)S(1)}, u32[]{:S(2)}, u32[]{:S(2)}) %collective-permute-start.5) | collective-permute-done | bytes 262176 | tf_op jit(solution)/shard_map/psi_shift/ppermute | solution.py:49
  41.1 0.0 collective-permute-done.3.refs_3_
  41.1 0.0 collective-permute-done.2.refs_2_
  41.1 5.8 %collective-permute-done.1.refs_1_ = bf16[8,128,128]{2,1,0:T(8,128)(2,1)S(1)} collective-permute-done((bf16[8,128,128]{2,1,0:T(8,128)(2,1)S(1)}, bf16[8,128,128]{2,1,0:T(8,128)(2,1)S(1)}, u32[]{:S(2)}, u32[]{:S(2)}) %collective-permute-start.1) | collective-permute-done | bytes 262176 | tf_op jit(solution)/shard_map/over_y/ppermute | solution.py:49
  46.9 0.1 terms.1
  47.0 5.5 %collective-permute-start.7 = (bf16[16,128,128]{2,1,0:T(8,128)(2,1)S(1)}, bf16[16,128,128]{2,1,0:T(8,128)(2,1)S(1)}, u32[]{:S(2)}, u32[]{:S(2)}) collective-permute-start(bf16[16,128,128]{2,1,0:T(8,128)(2,1)S(1)} %get-tuple-element.30), channel_id=1, source_target_pairs={{0,33},{2,26},{4,45},{6,22},{8,41},{10,34},{12,53},{14,30},{16,49}... | collective-permute-start | bytes 1572872 | tf_op jit(solution)/shard_map/left_shift/ppermute | solution.py:49
  52.5 2.1 %collective-permute-start.10 = (bf16[16,128,128]{2,1,0:T(8,128)(2,1)S(1)}, bf16[16,128,128]{2,1,0:T(8,128)(2,1)S(1)}, u32[]{:S(2)}, u32[]{:S(2)}) collective-permute-start(bf16[16,128,128]{2,1,0:T(8,128)(2,1)S(1)} %get-tuple-element.31.refs_2_), channel_id=1, source_target_pairs={{0,128},{2,130},{4,132},{6,134},{8,136},{10,138},{12,140},{14,142}... | collective-permute-start | bytes 1572872 | tf_op jit(solution)/shard_map/right_over_x/ppermute | solution.py:49
  54.6 4.0 %collective-permute-start.9 = (bf16[16,128,128]{2,1,0:T(8,128)(2,1)S(1)}, bf16[16,128,128]{2,1,0:T(8,128)(2,1)S(1)}, u32[]{:S(2)}, u32[]{:S(2)}) collective-permute-start(bf16[16,128,128]{2,1,0:T(8,128)(2,1)S(1)} %get-tuple-element.31.refs_2_), channel_id=1, source_target_pairs={{0,256},{2,258},{4,260},{6,262},{8,264},{10,266},{12,268},{14,270}... | collective-permute-start | bytes 1572872 | tf_op jit(solution)/shard_map/right_over_x/ppermute | solution.py:49
  58.7 1.9 %collective-permute-start.8 = (bf16[16,128,128]{2,1,0:T(8,128)(2,1)S(1)}, bf16[16,128,128]{2,1,0:T(8,128)(2,1)S(1)}, u32[]{:S(2)}, u32[]{:S(2)}) collective-permute-start(bf16[16,128,128]{2,1,0:T(8,128)(2,1)S(1)} %get-tuple-element.31.refs_2_), channel_id=1, source_target_pairs={{0,384},{2,386},{4,388},{6,390},{8,392},{10,394},{12,396},{14,398}... | collective-permute-start | bytes 1572872 | tf_op jit(solution)/shard_map/right_over_x/ppermute | solution.py:49
  60.6 6.1 %collective-permute-start.6 = (bf16[16,128,128]{2,1,0:T(8,128)(2,1)S(1)}, bf16[16,128,128]{2,1,0:T(8,128)(2,1)S(1)}, u32[]{:S(2)}, u32[]{:S(2)}) collective-permute-start(bf16[16,128,128]{2,1,0:T(8,128)(2,1)S(1)} %get-tuple-element.30), channel_id=1, source_target_pairs={{0,0},{2,59},{4,12},{6,55},{8,8},{10,2},{12,20},{14,63},{16,16},{1... | collective-permute-start | bytes 1572872 | tf_op jit(solution)/shard_map/left_shift/ppermute | solution.py:49
  66.7 0.0 collective-permute-done.7.refs_1_
  66.7 1.9 %collective-permute-start.11 = (bf16[16,128,128]{2,1,0:T(8,128)(2,1)S(1)}, bf16[16,128,128]{2,1,0:T(8,128)(2,1)S(1)}, u32[]{:S(2)}, u32[]{:S(2)}) collective-permute-start(bf16[16,128,128]{2,1,0:T(8,128)(2,1)S(1)} %get-tuple-element.31.refs_2_), channel_id=1, source_target_pairs={{0,64},{2,66},{4,68},{6,70},{8,72},{10,74},{12,76},{14,78},{16,80}... | collective-permute-start | bytes 1572872 | tf_op jit(solution)/shard_map/right_core/ppermute | solution.py:49
  68.6 0.0 collective-permute-done.10.refs_5_
  68.6 2.4 %collective-permute-start.14 = (bf16[16,128,128]{2,1,0:T(8,128)(2,1)S(1)}, bf16[16,128,128]{2,1,0:T(8,128)(2,1)S(1)}, u32[]{:S(2)}, u32[]{:S(2)}) collective-permute-start(bf16[16,128,128]{2,1,0:T(8,128)(2,1)S(1)} %collective-permute-done.10.refs_5_), channel_id=1, source_target_pairs={{0,64},{2,66},{4,68},{6,70},{8,72},{10,74},{12,76},{14,78},{16,80}... | collective-permute-start | bytes 1572872 | tf_op jit(solution)/shard_map/right_core/ppermute | solution.py:49
  71.0 0.6 collective-permute-done.9.refs_4_
  71.6 2.0 %collective-permute-start.13 = (bf16[16,128,128]{2,1,0:T(8,128)(2,1)S(1)}, bf16[16,128,128]{2,1,0:T(8,128)(2,1)S(1)}, u32[]{:S(2)}, u32[]{:S(2)}) collective-permute-start(bf16[16,128,128]{2,1,0:T(8,128)(2,1)S(1)} %collective-permute-done.9.refs_4_), channel_id=1, source_target_pairs={{0,64},{2,66},{4,68},{6,70},{8,72},{10,74},{12,76},{14,78},{16,80}... | collective-permute-start | bytes 1572872 | tf_op jit(solution)/shard_map/right_core/ppermute | solution.py:49
  73.7 9.1 %collective-permute-done.8.refs_3_ = bf16[16,128,128]{2,1,0:T(8,128)(2,1)S(1)} collective-permute-done((bf16[16,128,128]{2,1,0:T(8,128)(2,1)S(1)}, bf16[16,128,128]{2,1,0:T(8,128)(2,1)S(1)}, u32[]{:S(2)}, u32[]{:S(2)}) %collective-permute-start.8) | collective-permute-done | bytes 524320 | tf_op jit(solution)/shard_map/right_over_x/ppermute | solution.py:49
  82.8 2.3 %collective-permute-start.12 = (bf16[16,128,128]{2,1,0:T(8,128)(2,1)S(1)}, bf16[16,128,128]{2,1,0:T(8,128)(2,1)S(1)}, u32[]{:S(2)}, u32[]{:S(2)}) collective-permute-start(bf16[16,128,128]{2,1,0:T(8,128)(2,1)S(1)} %collective-permute-done.8.refs_3_), channel_id=1, source_target_pairs={{0,64},{2,66},{4,68},{6,70},{8,72},{10,74},{12,76},{14,78},{16,80}... | collective-permute-start | bytes 1572872 | tf_op jit(solution)/shard_map/right_core/ppermute | solution.py:49
  85.1 0.0 collective-permute-done.6.refs_0_
  85.1 0.0 collective-permute-done.14.refs_9_
  85.1 0.0 collective-permute-done.13.refs_8_
  85.1 1.5 %collective-permute-done.12.refs_7_ = bf16[16,128,128]{2,1,0:T(8,128)(2,1)S(1)} collective-permute-done((bf16[16,128,128]{2,1,0:T(8,128)(2,1)S(1)}, bf16[16,128,128]{2,1,0:T(8,128)(2,1)S(1)}, u32[]{:S(2)}, u32[]{:S(2)}) %collective-permute-start.12) | collective-permute-done | bytes 524320 | tf_op jit(solution)/shard_map/right_core/ppermute | solution.py:49
  86.6 8.4 %products.1 = (bf16[32,2,128,128]{3,2,1,0:T(8,128)(2,1)S(1)}, bf16[8,128,128]{2,1,0:T(8,128)(2,1)S(1)}, bf16[8,128,128]{2,1,0:T(8,128)(2,1)S(1)}) custom-call(s32[8,64]{1,0:T(8,128)S(1)} %concatenate.10.tab, bf16[16,128,128]{2,1,0:T(8,128)(2,1)S(1)} %collective-permute-done.6.refs_0_, bf16[16,128,128]{2,1,0:T(8,128)(2,1)S(1)} %collective-permute-done.7.refs_1_, ...), custom_call_target="tpu_custom_call" | custom-call | flops 4294967296 | bytes 8388608 | tf_op jit(solution)/shard_map/products/products/pallas_call | solution.py:216
  95.0 0.0 copy-start.1
  95.0 1.3 copy-done.1
  96.3 6.0 %all-to-all-start = ((bf16[32,2,128,128]{3,2,1,0:T(8,128)(2,1)}), bf16[32,2,128,128]{3,2,1,0:T(8,128)(2,1)S(1)}, u32[]{:S(2)}, u32[]{:S(2)}) async-start(bf16[32,2,128,128]{3,2,1,0:T(8,128)(2,1)} %copy-done.1), calls=%async_computation | async-start | bytes 4194304 | tf_op jit(solution)/shard_map/first_out/all_to_all | solution.py:273
  102.4 3.3 %collective-permute-start.15 = (bf16[8,128,128]{2,1,0:T(8,128)(2,1)S(1)}, bf16[8,128,128]{2,1,0:T(8,128)(2,1)S(1)}, u32[]{:S(2)}, u32[]{:S(2)}) collective-permute-start(bf16[8,128,128]{2,1,0:T(8,128)(2,1)S(1)} %get-tuple-element.35), channel_id=1, source_target_pairs={{0,0},{2,10},{4,61},{6,22},{8,8},{10,18},{12,4},{14,30},{16,16},{1... | collective-permute-start | bytes 786440 | tf_op jit(solution)/shard_map/second_shift/ppermute | solution.py:49
  105.7 3.8 %collective-permute-start.16 = (bf16[8,128,128]{2,1,0:T(8,128)(2,1)S(1)}, bf16[8,128,128]{2,1,0:T(8,128)(2,1)S(1)}, u32[]{:S(2)}, u32[]{:S(2)}) collective-permute-start(bf16[8,128,128]{2,1,0:T(8,128)(2,1)S(1)} %get-tuple-element.36), channel_id=1, source_target_pairs={{0,32},{2,43},{4,28},{6,55},{8,40},{10,51},{12,36},{14,63},{16,48}... | collective-permute-start | bytes 786440 | tf_op jit(solution)/shard_map/second_shift/ppermute | solution.py:49
  109.5 1.5 collective-permute-done.15.back0
  110.9 12.8 %collective-permute-done.16.back1 = bf16[8,128,128]{2,1,0:T(8,128)(2,1)S(1)} collective-permute-done((bf16[8,128,128]{2,1,0:T(8,128)(2,1)S(1)}, bf16[8,128,128]{2,1,0:T(8,128)(2,1)S(1)}, u32[]{:S(2)}, u32[]{:S(2)}) %collective-permute-start.16) | collective-permute-done | bytes 262176 | tf_op jit(solution)/shard_map/second_shift/ppermute | solution.py:49
  123.7 2.0 %second_pack.1 = (bf16[8,128,128]{2,1,0:T(8,128)(2,1)S(1)}, bf16[8,128,128]{2,1,0:T(8,128)(2,1)}, bf16[8,128,128]{2,1,0:T(8,128)(2,1)}, bf16[8,128,128]{2,1,0:T(8,128)(2,1)S(1)}) custom-call(s32[8,64]{1,0:T(8,128)S(1)} %concatenate.10.tab, bf16[8,128,128]{2,1,0:T(8,128)(2,1)S(1)} %collective-permute-done.15.back0, ...), custom_call_target="tpu_custom_call" | custom-call | bytes 2097152 | tf_op jit(solution)/shard_map/second_over_y/second_pack/pallas_call | solution.py:216
  125.6 1.9 %collective-permute-start.17 = (bf16[8,128,128]{2,1,0:T(8,128)(2,1)}, bf16[8,128,128]{2,1,0:T(8,128)(2,1)S(1)}, u32[]{:S(2)}, u32[]{:S(2)}) collective-permute-start(bf16[8,128,128]{2,1,0:T(8,128)(2,1)} %get-tuple-element.38), channel_id=1, source_target_pairs={{0,2},{2,4},{4,6},{6,0},{8,10},{10,12},{12,14},{14,8},{16,18},{18,... | collective-permute-start | bytes 786440 | tf_op jit(solution)/shard_map/second_over_y/ppermute | solution.py:49
  127.6 1.9 %collective-permute-start.18 = (bf16[8,128,128]{2,1,0:T(8,128)(2,1)}, bf16[8,128,128]{2,1,0:T(8,128)(2,1)S(1)}, u32[]{:S(2)}, u32[]{:S(2)}) collective-permute-start(bf16[8,128,128]{2,1,0:T(8,128)(2,1)} %get-tuple-element.39), channel_id=1, source_target_pairs={{0,4},{2,6},{4,0},{6,2},{8,12},{10,14},{12,8},{14,10},{16,20},{18,... | collective-permute-start | bytes 786440 | tf_op jit(solution)/shard_map/second_over_y/ppermute | solution.py:49
  129.5 3.4 %collective-permute-start.19 = (bf16[8,128,128]{2,1,0:T(8,128)(2,1)S(1)}, bf16[8,128,128]{2,1,0:T(8,128)(2,1)S(1)}, u32[]{:S(2)}, u32[]{:S(2)}) collective-permute-start(bf16[8,128,128]{2,1,0:T(8,128)(2,1)S(1)} %get-tuple-element.40), channel_id=1, source_target_pairs={{0,6},{2,0},{4,2},{6,4},{8,14},{10,8},{12,10},{14,12},{16,22},{18,... | collective-permute-start | bytes 786440 | tf_op jit(solution)/shard_map/second_over_y/ppermute | solution.py:49
  132.9 2.2 %first_order.1 = bf16[64,128,128]{2,1,0:T(8,128)(2,1)} custom-call(s32[8,64]{1,0:T(8,128)S(1)} %concatenate.10.tab, bf16[64,128,128]{2,1,0:T(8,128)(2,1)S(1)} %bitcast.12), custom_call_target="tpu_custom_call" | custom-call | bytes 4194304 | tf_op jit(solution)/shard_map/first_order/first_order/pallas_call | solution.py:216
  135.0 1.5 %collective-permute-done.18.part2 = bf16[8,128,128]{2,1,0:T(8,128)(2,1)S(1)} collective-permute-done((bf16[8,128,128]{2,1,0:T(8,128)(2,1)}, bf16[8,128,128]{2,1,0:T(8,128)(2,1)S(1)}, u32[]{:S(2)}, u32[]{:S(2)}) %collective-permute-start.18) | collective-permute-done | bytes 262176 | tf_op jit(solution)/shard_map/second_over_y/ppermute | solution.py:49
  136.5 8.5 %collective-permute-done.19.part3 = bf16[8,128,128]{2,1,0:T(8,128)(2,1)S(1)} collective-permute-done((bf16[8,128,128]{2,1,0:T(8,128)(2,1)S(1)}, bf16[8,128,128]{2,1,0:T(8,128)(2,1)S(1)}, u32[]{:S(2)}, u32[]{:S(2)}) %collective-permute-start.19) | collective-permute-done | bytes 262176 | tf_op jit(solution)/shard_map/second_over_y/ppermute | solution.py:49
  145.0 1.5 %second_pick.1 = bf16[8,128,128]{2,1,0:T(8,128)(2,1)} custom-call(s32[8,64]{1,0:T(8,128)S(1)} %concatenate.10.tab, bf16[8,128,128]{2,1,0:T(8,128)(2,1)S(1)} %get-tuple-element.42.part0, bf16[8,128,128]{2,1,0:T(8,128)(2,1)S(1)} %collective-permute-done.17.part1, bf16[8,128,128]{2,1,0:T(8,128)(2,1)S(1)} %collective-permute-done.18.part2, ...), custom_call_target="tpu_custom_call" | custom-call | bytes 2097152 | tf_op jit(solution)/shard_map/second_pick/second_pick/pallas_call | solution.py:216
  (11 shorter events, 0.1 us)
Async XLA Ops:
  0.6 24.2 %copy-start.2 = (bf16[2,1,128,128]{3,2,1,0:T(8,128)(2,1)S(1)}, bf16[2,1,128,128]{3,2,1,0:T(8,128)(2,1)}, u32[]{:S(2)}) copy-start(bf16[2,1,128,128]{3,2,1,0:T(8,128)(2,1)} %param.12) | copy-start | bytes 196612
  0.6 24.2 %copy-start.3 = (bf16[2,1,128,128]{3,2,1,0:T(8,128)(2,1)S(1)}, bf16[2,1,128,128]{3,2,1,0:T(8,128)(2,1)}, u32[]{:S(2)}) copy-start(bf16[2,1,128,128]{3,2,1,0:T(8,128)(2,1)} %param.11) | copy-start | bytes 196612
  1.6 23.2 %collective-permute-start = (bf16[4,128,128]{2,1,0:T(8,128)(2,1)S(1)}, bf16[4,128,128]{2,1,0:T(8,128)(2,1)S(1)}, u32[]{:S(2)}, u32[]{:S(2)}) collective-permute-start(bf16[4,128,128]{2,1,0:T(8,128)(2,1)S(1)} %pad_maximum_fusion.1), channel_id=1, source_target_pairs={{0,1},{2,3},{4,5},{6,7},{8,9},{10,11},{12,13},{14,15},{16,17},{18,... | collective-permute-start | bytes 393224 | tf_op jit(solution)/shard_map/half_exchange/ppermute | solution.py:49
  17.8 1.6 %copy-start = (bf16[1,64,128,128]{3,2,1,0:T(8,128)(2,1)S(1)}, bf16[1,64,128,128]{3,2,1,0:T(8,128)(2,1)}, u32[]{:S(2)}) copy-start(bf16[1,64,128,128]{3,2,1,0:T(8,128)(2,1)} %param.10) | copy-start | bytes 6291460
  20.2 17.3 %collective-permute-start.4 = (bf16[8,128,128]{2,1,0:T(8,128)(2,1)S(1)}, bf16[8,128,128]{2,1,0:T(8,128)(2,1)S(1)}, u32[]{:S(2)}, u32[]{:S(2)}) collective-permute-start(bf16[8,128,128]{2,1,0:T(8,128)(2,1)S(1)} %get-tuple-element.24), channel_id=1, source_target_pairs={{0,0},{2,59},{4,12},{6,55},{8,8},{10,2},{12,20},{14,63},{16,16},{1... | collective-permute-start | bytes 786440 | tf_op jit(solution)/shard_map/psi_shift/ppermute | solution.py:49
  22.9 18.2 %collective-permute-start.5 = (bf16[8,128,128]{2,1,0:T(8,128)(2,1)S(1)}, bf16[8,128,128]{2,1,0:T(8,128)(2,1)S(1)}, u32[]{:S(2)}, u32[]{:S(2)}) collective-permute-start(bf16[8,128,128]{2,1,0:T(8,128)(2,1)S(1)} %get-tuple-element.25), channel_id=1, source_target_pairs={{0,33},{2,26},{4,45},{6,22},{8,41},{10,34},{12,53},{14,30},{16,49}... | collective-permute-start | bytes 786440 | tf_op jit(solution)/shard_map/psi_shift/ppermute | solution.py:49
  24.9 16.3 %collective-permute-start.3 = (bf16[8,128,128]{2,1,0:T(8,128)(2,1)S(1)}, bf16[8,128,128]{2,1,0:T(8,128)(2,1)S(1)}, u32[]{:S(2)}, u32[]{:S(2)}) collective-permute-start(bf16[8,128,128]{2,1,0:T(8,128)(2,1)S(1)} %pad_maximum_fusion.refs_0_), channel_id=1, source_target_pairs={{0,2},{2,4},{4,6},{6,0},{8,10},{10,12},{12,14},{14,8},{16,18},{18,... | collective-permute-start | bytes 786440 | tf_op jit(solution)/shard_map/over_y/ppermute | solution.py:49
  29.7 11.4 %collective-permute-start.2 = (bf16[8,128,128]{2,1,0:T(8,128)(2,1)S(1)}, bf16[8,128,128]{2,1,0:T(8,128)(2,1)S(1)}, u32[]{:S(2)}, u32[]{:S(2)}) collective-permute-start(bf16[8,128,128]{2,1,0:T(8,128)(2,1)S(1)} %pad_maximum_fusion.refs_0_), channel_id=1, source_target_pairs={{0,4},{2,6},{4,0},{6,2},{8,12},{10,14},{12,8},{14,10},{16,20},{18,... | collective-permute-start | bytes 786440 | tf_op jit(solution)/shard_map/over_y/ppermute | solution.py:49
  33.6 13.4 %collective-permute-start.1 = (bf16[8,128,128]{2,1,0:T(8,128)(2,1)S(1)}, bf16[8,128,128]{2,1,0:T(8,128)(2,1)S(1)}, u32[]{:S(2)}, u32[]{:S(2)}) collective-permute-start(bf16[8,128,128]{2,1,0:T(8,128)(2,1)S(1)} %pad_maximum_fusion.refs_0_), channel_id=1, source_target_pairs={{0,6},{2,0},{4,2},{6,4},{8,14},{10,8},{12,10},{14,12},{16,22},{18,... | collective-permute-start | bytes 786440 | tf_op jit(solution)/shard_map/over_y/ppermute | solution.py:49
  47.0 19.6 %collective-permute-start.7 = (bf16[16,128,128]{2,1,0:T(8,128)(2,1)S(1)}, bf16[16,128,128]{2,1,0:T(8,128)(2,1)S(1)}, u32[]{:S(2)}, u32[]{:S(2)}) collective-permute-start(bf16[16,128,128]{2,1,0:T(8,128)(2,1)S(1)} %get-tuple-element.30), channel_id=1, source_target_pairs={{0,33},{2,26},{4,45},{6,22},{8,41},{10,34},{12,53},{14,30},{16,49}... | collective-permute-start | bytes 1572872 | tf_op jit(solution)/shard_map/left_shift/ppermute | solution.py:49
  52.5 16.1 %collective-permute-start.10 = (bf16[16,128,128]{2,1,0:T(8,128)(2,1)S(1)}, bf16[16,128,128]{2,1,0:T(8,128)(2,1)S(1)}, u32[]{:S(2)}, u32[]{:S(2)}) collective-permute-start(bf16[16,128,128]{2,1,0:T(8,128)(2,1)S(1)} %get-tuple-element.31.refs_2_), channel_id=1, source_target_pairs={{0,128},{2,130},{4,132},{6,134},{8,136},{10,138},{12,140},{14,142}... | collective-permute-start | bytes 1572872 | tf_op jit(solution)/shard_map/right_over_x/ppermute | solution.py:49
  54.6 17.0 %collective-permute-start.9 = (bf16[16,128,128]{2,1,0:T(8,128)(2,1)S(1)}, bf16[16,128,128]{2,1,0:T(8,128)(2,1)S(1)}, u32[]{:S(2)}, u32[]{:S(2)}) collective-permute-start(bf16[16,128,128]{2,1,0:T(8,128)(2,1)S(1)} %get-tuple-element.31.refs_2_), channel_id=1, source_target_pairs={{0,256},{2,258},{4,260},{6,262},{8,264},{10,266},{12,268},{14,270}... | collective-permute-start | bytes 1572872 | tf_op jit(solution)/shard_map/right_over_x/ppermute | solution.py:49
  58.7 24.1 %collective-permute-start.8 = (bf16[16,128,128]{2,1,0:T(8,128)(2,1)S(1)}, bf16[16,128,128]{2,1,0:T(8,128)(2,1)S(1)}, u32[]{:S(2)}, u32[]{:S(2)}) collective-permute-start(bf16[16,128,128]{2,1,0:T(8,128)(2,1)S(1)} %get-tuple-element.31.refs_2_), channel_id=1, source_target_pairs={{0,384},{2,386},{4,388},{6,390},{8,392},{10,394},{12,396},{14,398}... | collective-permute-start | bytes 1572872 | tf_op jit(solution)/shard_map/right_over_x/ppermute | solution.py:49
  60.6 24.5 %collective-permute-start.6 = (bf16[16,128,128]{2,1,0:T(8,128)(2,1)S(1)}, bf16[16,128,128]{2,1,0:T(8,128)(2,1)S(1)}, u32[]{:S(2)}, u32[]{:S(2)}) collective-permute-start(bf16[16,128,128]{2,1,0:T(8,128)(2,1)S(1)} %get-tuple-element.30), channel_id=1, source_target_pairs={{0,0},{2,59},{4,12},{6,55},{8,8},{10,2},{12,20},{14,63},{16,16},{1... | collective-permute-start | bytes 1572872 | tf_op jit(solution)/shard_map/left_shift/ppermute | solution.py:49
  66.7 18.4 %collective-permute-start.11 = (bf16[16,128,128]{2,1,0:T(8,128)(2,1)S(1)}, bf16[16,128,128]{2,1,0:T(8,128)(2,1)S(1)}, u32[]{:S(2)}, u32[]{:S(2)}) collective-permute-start(bf16[16,128,128]{2,1,0:T(8,128)(2,1)S(1)} %get-tuple-element.31.refs_2_), channel_id=1, source_target_pairs={{0,64},{2,66},{4,68},{6,70},{8,72},{10,74},{12,76},{14,78},{16,80}... | collective-permute-start | bytes 1572872 | tf_op jit(solution)/shard_map/right_core/ppermute | solution.py:49
  68.6 16.5 %collective-permute-start.14 = (bf16[16,128,128]{2,1,0:T(8,128)(2,1)S(1)}, bf16[16,128,128]{2,1,0:T(8,128)(2,1)S(1)}, u32[]{:S(2)}, u32[]{:S(2)}) collective-permute-start(bf16[16,128,128]{2,1,0:T(8,128)(2,1)S(1)} %collective-permute-done.10.refs_5_), channel_id=1, source_target_pairs={{0,64},{2,66},{4,68},{6,70},{8,72},{10,74},{12,76},{14,78},{16,80}... | collective-permute-start | bytes 1572872 | tf_op jit(solution)/shard_map/right_core/ppermute | solution.py:49
  71.6 13.5 %collective-permute-start.13 = (bf16[16,128,128]{2,1,0:T(8,128)(2,1)S(1)}, bf16[16,128,128]{2,1,0:T(8,128)(2,1)S(1)}, u32[]{:S(2)}, u32[]{:S(2)}) collective-permute-start(bf16[16,128,128]{2,1,0:T(8,128)(2,1)S(1)} %collective-permute-done.9.refs_4_), channel_id=1, source_target_pairs={{0,64},{2,66},{4,68},{6,70},{8,72},{10,74},{12,76},{14,78},{16,80}... | collective-permute-start | bytes 1572872 | tf_op jit(solution)/shard_map/right_core/ppermute | solution.py:49
  82.8 3.8 %collective-permute-start.12 = (bf16[16,128,128]{2,1,0:T(8,128)(2,1)S(1)}, bf16[16,128,128]{2,1,0:T(8,128)(2,1)S(1)}, u32[]{:S(2)}, u32[]{:S(2)}) collective-permute-start(bf16[16,128,128]{2,1,0:T(8,128)(2,1)S(1)} %collective-permute-done.8.refs_3_), channel_id=1, source_target_pairs={{0,64},{2,66},{4,68},{6,70},{8,72},{10,74},{12,76},{14,78},{16,80}... | collective-permute-start | bytes 1572872 | tf_op jit(solution)/shard_map/right_core/ppermute | solution.py:49
  95.0 1.3 copy-start.1
  96.3 36.5 %all-to-all-start = ((bf16[32,2,128,128]{3,2,1,0:T(8,128)(2,1)}), bf16[32,2,128,128]{3,2,1,0:T(8,128)(2,1)S(1)}, u32[]{:S(2)}, u32[]{:S(2)}) async-start(bf16[32,2,128,128]{3,2,1,0:T(8,128)(2,1)} %copy-done.1), calls=%async_computation | async-start | bytes 4194304 | tf_op jit(solution)/shard_map/first_out/all_to_all | solution.py:273
  102.4 8.6 %collective-permute-start.15 = (bf16[8,128,128]{2,1,0:T(8,128)(2,1)S(1)}, bf16[8,128,128]{2,1,0:T(8,128)(2,1)S(1)}, u32[]{:S(2)}, u32[]{:S(2)}) collective-permute-start(bf16[8,128,128]{2,1,0:T(8,128)(2,1)S(1)} %get-tuple-element.35), channel_id=1, source_target_pairs={{0,0},{2,10},{4,61},{6,22},{8,8},{10,18},{12,4},{14,30},{16,16},{1... | collective-permute-start | bytes 786440 | tf_op jit(solution)/shard_map/second_shift/ppermute | solution.py:49
  105.7 18.0 %collective-permute-start.16 = (bf16[8,128,128]{2,1,0:T(8,128)(2,1)S(1)}, bf16[8,128,128]{2,1,0:T(8,128)(2,1)S(1)}, u32[]{:S(2)}, u32[]{:S(2)}) collective-permute-start(bf16[8,128,128]{2,1,0:T(8,128)(2,1)S(1)} %get-tuple-element.36), channel_id=1, source_target_pairs={{0,32},{2,43},{4,28},{6,55},{8,40},{10,51},{12,36},{14,63},{16,48}... | collective-permute-start | bytes 786440 | tf_op jit(solution)/shard_map/second_shift/ppermute | solution.py:49
  125.6 9.4 %collective-permute-start.17 = (bf16[8,128,128]{2,1,0:T(8,128)(2,1)}, bf16[8,128,128]{2,1,0:T(8,128)(2,1)S(1)}, u32[]{:S(2)}, u32[]{:S(2)}) collective-permute-start(bf16[8,128,128]{2,1,0:T(8,128)(2,1)} %get-tuple-element.38), channel_id=1, source_target_pairs={{0,2},{2,4},{4,6},{6,0},{8,10},{10,12},{12,14},{14,8},{16,18},{18,... | collective-permute-start | bytes 786440 | tf_op jit(solution)/shard_map/second_over_y/ppermute | solution.py:49
  127.6 8.9 %collective-permute-start.18 = (bf16[8,128,128]{2,1,0:T(8,128)(2,1)}, bf16[8,128,128]{2,1,0:T(8,128)(2,1)S(1)}, u32[]{:S(2)}, u32[]{:S(2)}) collective-permute-start(bf16[8,128,128]{2,1,0:T(8,128)(2,1)} %get-tuple-element.39), channel_id=1, source_target_pairs={{0,4},{2,6},{4,0},{6,2},{8,12},{10,14},{12,8},{14,10},{16,20},{18,... | collective-permute-start | bytes 786440 | tf_op jit(solution)/shard_map/second_over_y/ppermute | solution.py:49
  129.5 15.5 %collective-permute-start.19 = (bf16[8,128,128]{2,1,0:T(8,128)(2,1)S(1)}, bf16[8,128,128]{2,1,0:T(8,128)(2,1)S(1)}, u32[]{:S(2)}, u32[]{:S(2)}) collective-permute-start(bf16[8,128,128]{2,1,0:T(8,128)(2,1)S(1)} %get-tuple-element.40), channel_id=1, source_target_pairs={{0,6},{2,0},{4,2},{6,4},{8,14},{10,8},{12,10},{14,12},{16,22},{18,... | collective-permute-start | bytes 786440 | tf_op jit(solution)/shard_map/second_over_y/ppermute | solution.py:49

commit v6 on v5

--- a/solution.py
+++ b/solution.py
@@ -177,21 +177,21 @@
                     out[tab[LEFT_ORDER, slot]] = came[place]
 
 
-def second_pack_kernel(tab, back0, back1, out0, out1, out2, out3, packed):
-    x, c, z, y, h = here()
-    packed[...] = jnp.zeros(packed.shape, packed.dtype)
+def second_pack_kernel(tab, back1, back0, *outs):
+    x, c, z, y, h = here()
+    for out in outs:
+        out[...] = jnp.zeros(out.shape, out.dtype)
     for n, back in enumerate((back0, back1)):
         z_from = z - shift_of(tab, y, c, n)
         for j in range(2 * NX):
             b = right_sector(tab, x, c, z_from, j)
             group = b // 8
 
-            @pl.when(lax.rem(group, NH) == h)
-            def _(j=j, b=b, back=back, group=group):
-                packed[lax.rem(group // NH - y + NY, NY), lax.rem(b, 8)] = back[j]
-
-    for r, out in enumerate((out0, out1, out2, out3)):
-        out[...] = packed[r]
+            for r, out in enumerate(outs):
+
+                @pl.when(group == lax.rem(y + r, NY) * NH + h)
+                def _(j=j, b=b, back=back, out=out):
+                    out[lax.rem(b, 8)] = back[j]
 
 
 def second_pick_kernel(tab, part0, part1, part2, part3, out):
@@ -272,11 +272,11 @@
     with jax.named_scope("first_out"):
         came = lax.all_to_all(sent, ("x", "c", "y"), 0, 0, tiled=True).reshape(64, M, M)
     with jax.named_scope("second_shift"):
-        back = [to_shift(seconds[n], n) for n in range(2)]
+        far = to_shift(seconds[1], 1)
+        near = to_shift(seconds[0], 0)
     with jax.named_scope("second_over_y"):
         parts = call(
-            second_pack_kernel, "second_pack", (tab, *back), [blocks(8)] * NY,
-            [pltpu.VMEM((NY, 8, M, M), jnp.bfloat16)], size=2 << 20,
+            second_pack_kernel, "second_pack", (tab, far, near), [blocks(8)] * NY, size=2 << 20,
         )
         parts = [parts[0]] + [from_y(parts[r], -r) for r in range(1, NY)]
     with jax.named_scope("first_order"):

time: 147 us -> 147 us (level)
  the two profiles are of different devices: /device:TPU:15 before, /device:TPU:1 now
where the time goes in v6:
time: 147 us; the launch traced here: 145 us
  starting transfers between devices  81.8 us (56%)
  waiting for transfers between devices  42.7 us (29%)
  Pallas kernels  15 us (10%)
  local copies, waits for them, and re-layouts  3.7 us (3%)
    ppermute x20, starting transfers between devices, permute(): return lax.ppermute(value, AXES, pairs)  77 us
    ppermute x20, waiting for transfers between devices, permute(): return lax.ppermute(value, AXES, pairs)  42.7 us
    pallas_call x6, Pallas kernels, call(): pl.pallas_call(kernel, name=name, out_shape=outputs, in_specs=[SMEM if v....  15 us
    all_to_all x1, starting transfers between devices, on_device(): lax.all_to_all(sent, ('x', 'c', 'y'), 0, 0, tiled=True).reshape(64, M, M)  4.83 us
  transfers between devices with their start and end apart: 21, of which 8 were waited for; matrix products, arithmetic and copies ran while one was open for 1% of the time, Pallas kernels for 3%

profile of v6, /device:TPU:1, one launch (start us, length us, event | category | flops | bytes accessed | tf_op | source)
XLA Modules:
  0.0 145.2 jit_solution(8885425173252938786)
XLA Ops:
  0.6 0.9 pad_maximum_fusion.1
  1.6 16.3 %collective-permute-start = (bf16[4,128,128]{2,1,0:T(8,128)(2,1)S(1)}, bf16[4,128,128]{2,1,0:T(8,128)(2,1)S(1)}, u32[]{:S(2)}, u32[]{:S(2)}) collective-permute-start(bf16[4,128,128]{2,1,0:T(8,128)(2,1)S(1)} %pad_maximum_fusion.1), channel_id=1, source_target_pairs={{0,1},{2,3},{4,5},{6,7},{8,9},{10,11},{12,13},{14,15},{16,17},{18,... | collective-permute-start | bytes 393224 | tf_op jit(solution)/shard_map/half_exchange/ppermute | solution.py:49
  17.9 0.8 concatenate.10.tab
  18.7 1.6 %copy-done = bf16[1,64,128,128]{3,2,1,0:T(8,128)(2,1)S(1)} copy-done((bf16[1,64,128,128]{3,2,1,0:T(8,128)(2,1)S(1)}, bf16[1,64,128,128]{3,2,1,0:T(8,128)(2,1)}, u32[]{:S(2)}) %copy-start) | copy-done | bytes 2097176
  20.2 0.8 psi_pack.1
  21.0 0.7 collective-permute-start.4
  21.7 4.0 %collective-permute-start.5 = (bf16[8,128,128]{2,1,0:T(8,128)(2,1)S(1)}, bf16[8,128,128]{2,1,0:T(8,128)(2,1)S(1)}, u32[]{:S(2)}, u32[]{:S(2)}) collective-permute-start(bf16[8,128,128]{2,1,0:T(8,128)(2,1)S(1)} %get-tuple-element.25), channel_id=1, source_target_pairs={{0,33},{2,26},{4,45},{6,22},{8,41},{10,34},{12,53},{14,30},{16,49}... | collective-permute-start | bytes 786440 | tf_op jit(solution)/shard_map/psi_shift/ppermute | solution.py:49
  25.8 0.0 collective-permute-done
  25.8 3.1 %collective-permute-start.3 = (bf16[8,128,128]{2,1,0:T(8,128)(2,1)S(1)}, bf16[8,128,128]{2,1,0:T(8,128)(2,1)S(1)}, u32[]{:S(2)}, u32[]{:S(2)}) collective-permute-start(bf16[8,128,128]{2,1,0:T(8,128)(2,1)S(1)} %pad_maximum_fusion.refs_0_), channel_id=1, source_target_pairs={{0,2},{2,4},{4,6},{6,0},{8,10},{10,12},{12,14},{14,8},{16,18},{18,... | collective-permute-start | bytes 786440 | tf_op jit(solution)/shard_map/over_y/ppermute | solution.py:49
  28.9 7.4 %collective-permute-start.2 = (bf16[8,128,128]{2,1,0:T(8,128)(2,1)S(1)}, bf16[8,128,128]{2,1,0:T(8,128)(2,1)S(1)}, u32[]{:S(2)}, u32[]{:S(2)}) collective-permute-start(bf16[8,128,128]{2,1,0:T(8,128)(2,1)S(1)} %pad_maximum_fusion.refs_0_), channel_id=1, source_target_pairs={{0,4},{2,6},{4,0},{6,2},{8,12},{10,14},{12,8},{14,10},{16,20},{18,... | collective-permute-start | bytes 786440 | tf_op jit(solution)/shard_map/over_y/ppermute | solution.py:49
  36.3 1.9 %collective-permute-start.1 = (bf16[8,128,128]{2,1,0:T(8,128)(2,1)S(1)}, bf16[8,128,128]{2,1,0:T(8,128)(2,1)S(1)}, u32[]{:S(2)}, u32[]{:S(2)}) collective-permute-start(bf16[8,128,128]{2,1,0:T(8,128)(2,1)S(1)} %pad_maximum_fusion.refs_0_), channel_id=1, source_target_pairs={{0,6},{2,0},{4,2},{6,4},{8,14},{10,8},{12,10},{14,12},{16,22},{18,... | collective-permute-start | bytes 786440 | tf_op jit(solution)/shard_map/over_y/ppermute | solution.py:49
  38.2 0.0 collective-permute-done.4.refs_10_
  38.2 4.6 %collective-permute-done.5.refs_11_ = bf16[8,128,128]{2,1,0:T(8,128)(2,1)S(1)} collective-permute-done((bf16[8,128,128]{2,1,0:T(8,128)(2,1)S(1)}, bf16[8,128,128]{2,1,0:T(8,128)(2,1)S(1)}, u32[]{:S(2)}, u32[]{:S(2)}) %collective-permute-start.5) | collective-permute-done | bytes 262176 | tf_op jit(solution)/shard_map/psi_shift/ppermute | solution.py:49
  42.8 3.3 %collective-permute-done.2.refs_2_ = bf16[8,128,128]{2,1,0:T(8,128)(2,1)S(1)} collective-permute-done((bf16[8,128,128]{2,1,0:T(8,128)(2,1)S(1)}, bf16[8,128,128]{2,1,0:T(8,128)(2,1)S(1)}, u32[]{:S(2)}, u32[]{:S(2)}) %collective-permute-start.2) | collective-permute-done | bytes 262176 | tf_op jit(solution)/shard_map/over_y/ppermute | solution.py:49
  46.1 1.4 collective-permute-done.1.refs_1_
  47.4 0.1 terms.1
  47.5 3.0 %collective-permute-start.7 = (bf16[16,128,128]{2,1,0:T(8,128)(2,1)S(1)}, bf16[16,128,128]{2,1,0:T(8,128)(2,1)S(1)}, u32[]{:S(2)}, u32[]{:S(2)}) collective-permute-start(bf16[16,128,128]{2,1,0:T(8,128)(2,1)S(1)} %get-tuple-element.30), channel_id=1, source_target_pairs={{0,33},{2,26},{4,45},{6,22},{8,41},{10,34},{12,53},{14,30},{16,49}... | collective-permute-start | bytes 1572872 | tf_op jit(solution)/shard_map/left_shift/ppermute | solution.py:49
  50.5 3.1 %collective-permute-start.10 = (bf16[16,128,128]{2,1,0:T(8,128)(2,1)S(1)}, bf16[16,128,128]{2,1,0:T(8,128)(2,1)S(1)}, u32[]{:S(2)}, u32[]{:S(2)}) collective-permute-start(bf16[16,128,128]{2,1,0:T(8,128)(2,1)S(1)} %get-tuple-element.31.refs_2_), channel_id=1, source_target_pairs={{0,128},{2,130},{4,132},{6,134},{8,136},{10,138},{12,140},{14,142}... | collective-permute-start | bytes 1572872 | tf_op jit(solution)/shard_map/right_over_x/ppermute | solution.py:49
  53.7 4.4 %collective-permute-start.9 = (bf16[16,128,128]{2,1,0:T(8,128)(2,1)S(1)}, bf16[16,128,128]{2,1,0:T(8,128)(2,1)S(1)}, u32[]{:S(2)}, u32[]{:S(2)}) collective-permute-start(bf16[16,128,128]{2,1,0:T(8,128)(2,1)S(1)} %get-tuple-element.31.refs_2_), channel_id=1, source_target_pairs={{0,256},{2,258},{4,260},{6,262},{8,264},{10,266},{12,268},{14,270}... | collective-permute-start | bytes 1572872 | tf_op jit(solution)/shard_map/right_over_x/ppermute | solution.py:49
  58.0 3.1 %collective-permute-start.8 = (bf16[16,128,128]{2,1,0:T(8,128)(2,1)S(1)}, bf16[16,128,128]{2,1,0:T(8,128)(2,1)S(1)}, u32[]{:S(2)}, u32[]{:S(2)}) collective-permute-start(bf16[16,128,128]{2,1,0:T(8,128)(2,1)S(1)} %get-tuple-element.31.refs_2_), channel_id=1, source_target_pairs={{0,384},{2,386},{4,388},{6,390},{8,392},{10,394},{12,396},{14,398}... | collective-permute-start | bytes 1572872 | tf_op jit(solution)/shard_map/right_over_x/ppermute | solution.py:49
  61.1 0.7 collective-permute-start.6
  61.8 16.5 %collective-permute-done.7.refs_1_ = bf16[16,128,128]{2,1,0:T(8,128)(2,1)S(1)} collective-permute-done((bf16[16,128,128]{2,1,0:T(8,128)(2,1)S(1)}, bf16[16,128,128]{2,1,0:T(8,128)(2,1)S(1)}, u32[]{:S(2)}, u32[]{:S(2)}) %collective-permute-start.7) | collective-permute-done | bytes 524320 | tf_op jit(solution)/shard_map/left_shift/ppermute | solution.py:49
  78.3 1.9 %collective-permute-start.11 = (bf16[16,128,128]{2,1,0:T(8,128)(2,1)S(1)}, bf16[16,128,128]{2,1,0:T(8,128)(2,1)S(1)}, u32[]{:S(2)}, u32[]{:S(2)}) collective-permute-start(bf16[16,128,128]{2,1,0:T(8,128)(2,1)S(1)} %get-tuple-element.31.refs_2_), channel_id=1, source_target_pairs={{0,64},{2,66},{4,68},{6,70},{8,72},{10,74},{12,76},{14,78},{16,80}... | collective-permute-start | bytes 1572872 | tf_op jit(solution)/shard_map/right_core/ppermute | solution.py:49
  80.3 0.0 collective-permute-done.10.refs_5_
  80.3 2.4 %collective-permute-start.14 = (bf16[16,128,128]{2,1,0:T(8,128)(2,1)S(1)}, bf16[16,128,128]{2,1,0:T(8,128)(2,1)S(1)}, u32[]{:S(2)}, u32[]{:S(2)}) collective-permute-start(bf16[16,128,128]{2,1,0:T(8,128)(2,1)S(1)} %collective-permute-done.10.refs_5_), channel_id=1, source_target_pairs={{0,64},{2,66},{4,68},{6,70},{8,72},{10,74},{12,76},{14,78},{16,80}... | collective-permute-start | bytes 1572872 | tf_op jit(solution)/shard_map/right_core/ppermute | solution.py:49
  82.7 0.0 collective-permute-done.9.refs_4_
  82.7 1.9 %collective-permute-start.13 = (bf16[16,128,128]{2,1,0:T(8,128)(2,1)S(1)}, bf16[16,128,128]{2,1,0:T(8,128)(2,1)S(1)}, u32[]{:S(2)}, u32[]{:S(2)}) collective-permute-start(bf16[16,128,128]{2,1,0:T(8,128)(2,1)S(1)} %collective-permute-done.9.refs_4_), channel_id=1, source_target_pairs={{0,64},{2,66},{4,68},{6,70},{8,72},{10,74},{12,76},{14,78},{16,80}... | collective-permute-start | bytes 1572872 | tf_op jit(solution)/shard_map/right_core/ppermute | solution.py:49
  84.6 0.0 collective-permute-done.8.refs_3_
  84.6 2.4 %collective-permute-start.12 = (bf16[16,128,128]{2,1,0:T(8,128)(2,1)S(1)}, bf16[16,128,128]{2,1,0:T(8,128)(2,1)S(1)}, u32[]{:S(2)}, u32[]{:S(2)}) collective-permute-start(bf16[16,128,128]{2,1,0:T(8,128)(2,1)S(1)} %collective-permute-done.8.refs_3_), channel_id=1, source_target_pairs={{0,64},{2,66},{4,68},{6,70},{8,72},{10,74},{12,76},{14,78},{16,80}... | collective-permute-start | bytes 1572872 | tf_op jit(solution)/shard_map/right_core/ppermute | solution.py:49
  87.1 0.0 collective-permute-done.6.refs_0_
  87.1 0.0 collective-permute-done.11.refs_6_
  87.1 0.0 collective-permute-done.13.refs_8_
  87.1 1.5 %collective-permute-done.12.refs_7_ = bf16[16,128,128]{2,1,0:T(8,128)(2,1)S(1)} collective-permute-done((bf16[16,128,128]{2,1,0:T(8,128)(2,1)S(1)}, bf16[16,128,128]{2,1,0:T(8,128)(2,1)S(1)}, u32[]{:S(2)}, u32[]{:S(2)}) %collective-permute-start.12) | collective-permute-done | bytes 524320 | tf_op jit(solution)/shard_map/right_core/ppermute | solution.py:49
  88.6 8.4 %products.1 = (bf16[32,2,128,128]{3,2,1,0:T(8,128)(2,1)S(1)}, bf16[8,128,128]{2,1,0:T(8,128)(2,1)S(1)}, bf16[8,128,128]{2,1,0:T(8,128)(2,1)S(1)}) custom-call(s32[8,64]{1,0:T(8,128)S(1)} %concatenate.10.tab, bf16[16,128,128]{2,1,0:T(8,128)(2,1)S(1)} %collective-permute-done.6.refs_0_, bf16[16,128,128]{2,1,0:T(8,128)(2,1)S(1)} %collective-permute-done.7.refs_1_, ...), custom_call_target="tpu_custom_call" | custom-call | flops 4294967296 | bytes 8388608 | tf_op jit(solution)/shard_map/products/products/pallas_call | solution.py:216
  97.0 0.0 copy-start.1
  97.0 1.3 copy-done.1
  98.3 4.8 %all-to-all-start = ((bf16[32,2,128,128]{3,2,1,0:T(8,128)(2,1)}), bf16[32,2,128,128]{3,2,1,0:T(8,128)(2,1)S(1)}, u32[]{:S(2)}, u32[]{:S(2)}) async-start(bf16[32,2,128,128]{3,2,1,0:T(8,128)(2,1)} %copy-done.1), calls=%async_computation | async-start | bytes 4194304 | tf_op jit(solution)/shard_map/first_out/all_to_all | solution.py:273
  103.1 7.3 %collective-permute-start.15 = (bf16[8,128,128]{2,1,0:T(8,128)(2,1)S(1)}, bf16[8,128,128]{2,1,0:T(8,128)(2,1)S(1)}, u32[]{:S(2)}, u32[]{:S(2)}) collective-permute-start(bf16[8,128,128]{2,1,0:T(8,128)(2,1)S(1)} %get-tuple-element.35), channel_id=1, source_target_pairs={{0,32},{2,43},{4,28},{6,55},{8,40},{10,51},{12,36},{14,63},{16,48}... | collective-permute-start | bytes 786440 | tf_op jit(solution)/shard_map/second_shift/ppermute | solution.py:49
  110.5 0.7 collective-permute-start.16
  111.2 10.1 %collective-permute-done.15.back1 = bf16[8,128,128]{2,1,0:T(8,128)(2,1)S(1)} collective-permute-done((bf16[8,128,128]{2,1,0:T(8,128)(2,1)S(1)}, bf16[8,128,128]{2,1,0:T(8,128)(2,1)S(1)}, u32[]{:S(2)}, u32[]{:S(2)}) %collective-permute-start.15) | collective-permute-done | bytes 262176 | tf_op jit(solution)/shard_map/second_shift/ppermute | solution.py:49
  121.2 2.1 %second_pack.1 = (bf16[8,128,128]{2,1,0:T(8,128)(2,1)S(1)}, bf16[8,128,128]{2,1,0:T(8,128)(2,1)}, bf16[8,128,128]{2,1,0:T(8,128)(2,1)}, bf16[8,128,128]{2,1,0:T(8,128)(2,1)S(1)}) custom-call(s32[8,64]{1,0:T(8,128)S(1)} %concatenate.10.tab, bf16[8,128,128]{2,1,0:T(8,128)(2,1)S(1)} %collective-permute-done.15.back1, ...), custom_call_target="tpu_custom_call" | custom-call | bytes 2097152 | tf_op jit(solution)/shard_map/second_over_y/second_pack/pallas_call | solution.py:216
  123.3 4.9 %collective-permute-start.17 = (bf16[8,128,128]{2,1,0:T(8,128)(2,1)}, bf16[8,128,128]{2,1,0:T(8,128)(2,1)S(1)}, u32[]{:S(2)}, u32[]{:S(2)}) collective-permute-start(bf16[8,128,128]{2,1,0:T(8,128)(2,1)} %get-tuple-element.38), channel_id=1, source_target_pairs={{0,2},{2,4},{4,6},{6,0},{8,10},{10,12},{12,14},{14,8},{16,18},{18,... | collective-permute-start | bytes 786440 | tf_op jit(solution)/shard_map/second_over_y/ppermute | solution.py:49
  128.2 4.2 %collective-permute-start.18 = (bf16[8,128,128]{2,1,0:T(8,128)(2,1)}, bf16[8,128,128]{2,1,0:T(8,128)(2,1)S(1)}, u32[]{:S(2)}, u32[]{:S(2)}) collective-permute-start(bf16[8,128,128]{2,1,0:T(8,128)(2,1)} %get-tuple-element.39), channel_id=1, source_target_pairs={{0,4},{2,6},{4,0},{6,2},{8,12},{10,14},{12,8},{14,10},{16,20},{18,... | collective-permute-start | bytes 786440 | tf_op jit(solution)/shard_map/second_over_y/ppermute | solution.py:49
  132.4 3.7 %collective-permute-start.19 = (bf16[8,128,128]{2,1,0:T(8,128)(2,1)S(1)}, bf16[8,128,128]{2,1,0:T(8,128)(2,1)S(1)}, u32[]{:S(2)}, u32[]{:S(2)}) collective-permute-start(bf16[8,128,128]{2,1,0:T(8,128)(2,1)S(1)} %get-tuple-element.40), channel_id=1, source_target_pairs={{0,6},{2,0},{4,2},{6,4},{8,14},{10,8},{12,10},{14,12},{16,22},{18,... | collective-permute-start | bytes 786440 | tf_op jit(solution)/shard_map/second_over_y/ppermute | solution.py:49
  136.2 2.2 %first_order.1 = bf16[64,128,128]{2,1,0:T(8,128)(2,1)} custom-call(s32[8,64]{1,0:T(8,128)S(1)} %concatenate.10.tab, bf16[64,128,128]{2,1,0:T(8,128)(2,1)S(1)} %bitcast.12), custom_call_target="tpu_custom_call" | custom-call | bytes 4194304 | tf_op jit(solution)/shard_map/first_order/first_order/pallas_call | solution.py:216
  138.3 3.0 %collective-permute-done.18.part2 = bf16[8,128,128]{2,1,0:T(8,128)(2,1)S(1)} collective-permute-done((bf16[8,128,128]{2,1,0:T(8,128)(2,1)}, bf16[8,128,128]{2,1,0:T(8,128)(2,1)S(1)}, u32[]{:S(2)}, u32[]{:S(2)}) %collective-permute-start.18) | collective-permute-done | bytes 262176 | tf_op jit(solution)/shard_map/second_over_y/ppermute | solution.py:49
  141.3 2.3 %collective-permute-done.19.part3 = bf16[8,128,128]{2,1,0:T(8,128)(2,1)S(1)} collective-permute-done((bf16[8,128,128]{2,1,0:T(8,128)(2,1)S(1)}, bf16[8,128,128]{2,1,0:T(8,128)(2,1)S(1)}, u32[]{:S(2)}, u32[]{:S(2)}) %collective-permute-start.19) | collective-permute-done | bytes 262176 | tf_op jit(solution)/shard_map/second_over_y/ppermute | solution.py:49
  143.7 1.5 %second_pick.1 = bf16[8,128,128]{2,1,0:T(8,128)(2,1)} custom-call(s32[8,64]{1,0:T(8,128)S(1)} %concatenate.10.tab, bf16[8,128,128]{2,1,0:T(8,128)(2,1)S(1)} %get-tuple-element.42.part0, bf16[8,128,128]{2,1,0:T(8,128)(2,1)S(1)} %collective-permute-done.17.part1, bf16[8,128,128]{2,1,0:T(8,128)(2,1)S(1)} %collective-permute-done.18.part2, ...), custom_call_target="tpu_custom_call" | custom-call | bytes 2097152 | tf_op jit(solution)/shard_map/second_pick/second_pick/pallas_call | solution.py:216
  (11 shorter events, 0.1 us)
Async XLA Ops:
  0.6 25.1 %copy-start.2 = (bf16[2,1,128,128]{3,2,1,0:T(8,128)(2,1)S(1)}, bf16[2,1,128,128]{3,2,1,0:T(8,128)(2,1)}, u32[]{:S(2)}) copy-start(bf16[2,1,128,128]{3,2,1,0:T(8,128)(2,1)} %param.12) | copy-start | bytes 196612
  0.6 25.1 %copy-start.3 = (bf16[2,1,128,128]{3,2,1,0:T(8,128)(2,1)S(1)}, bf16[2,1,128,128]{3,2,1,0:T(8,128)(2,1)}, u32[]{:S(2)}) copy-start(bf16[2,1,128,128]{3,2,1,0:T(8,128)(2,1)} %param.11) | copy-start | bytes 196612
  1.6 24.2 %collective-permute-start = (bf16[4,128,128]{2,1,0:T(8,128)(2,1)S(1)}, bf16[4,128,128]{2,1,0:T(8,128)(2,1)S(1)}, u32[]{:S(2)}, u32[]{:S(2)}) collective-permute-start(bf16[4,128,128]{2,1,0:T(8,128)(2,1)S(1)} %pad_maximum_fusion.1), channel_id=1, source_target_pairs={{0,1},{2,3},{4,5},{6,7},{8,9},{10,11},{12,13},{14,15},{16,17},{18,... | collective-permute-start | bytes 393224 | tf_op jit(solution)/shard_map/half_exchange/ppermute | solution.py:49
  18.6 1.6 %copy-start = (bf16[1,64,128,128]{3,2,1,0:T(8,128)(2,1)S(1)}, bf16[1,64,128,128]{3,2,1,0:T(8,128)(2,1)}, u32[]{:S(2)}) copy-start(bf16[1,64,128,128]{3,2,1,0:T(8,128)(2,1)} %param.10) | copy-start | bytes 6291460
  21.0 17.2 %collective-permute-start.4 = (bf16[8,128,128]{2,1,0:T(8,128)(2,1)S(1)}, bf16[8,128,128]{2,1,0:T(8,128)(2,1)S(1)}, u32[]{:S(2)}, u32[]{:S(2)}) collective-permute-start(bf16[8,128,128]{2,1,0:T(8,128)(2,1)S(1)} %get-tuple-element.24), channel_id=1, source_target_pairs={{0,0},{2,59},{4,12},{6,55},{8,8},{10,2},{12,20},{14,63},{16,16},{1... | collective-permute-start | bytes 786440 | tf_op jit(solution)/shard_map/psi_shift/ppermute | solution.py:49
  21.7 21.0 %collective-permute-start.5 = (bf16[8,128,128]{2,1,0:T(8,128)(2,1)S(1)}, bf16[8,128,128]{2,1,0:T(8,128)(2,1)S(1)}, u32[]{:S(2)}, u32[]{:S(2)}) collective-permute-start(bf16[8,128,128]{2,1,0:T(8,128)(2,1)S(1)} %get-tuple-element.25), channel_id=1, source_target_pairs={{0,33},{2,26},{4,45},{6,22},{8,41},{10,34},{12,53},{14,30},{16,49}... | collective-permute-start | bytes 786440 | tf_op jit(solution)/shard_map/psi_shift/ppermute | solution.py:49
  25.8 17.0 %collective-permute-start.3 = (bf16[8,128,128]{2,1,0:T(8,128)(2,1)S(1)}, bf16[8,128,128]{2,1,0:T(8,128)(2,1)S(1)}, u32[]{:S(2)}, u32[]{:S(2)}) collective-permute-start(bf16[8,128,128]{2,1,0:T(8,128)(2,1)S(1)} %pad_maximum_fusion.refs_0_), channel_id=1, source_target_pairs={{0,2},{2,4},{4,6},{6,0},{8,10},{10,12},{12,14},{14,8},{16,18},{18,... | collective-permute-start | bytes 786440 | tf_op jit(solution)/shard_map/over_y/ppermute | solution.py:49
  28.9 17.2 %collective-permute-start.2 = (bf16[8,128,128]{2,1,0:T(8,128)(2,1)S(1)}, bf16[8,128,128]{2,1,0:T(8,128)(2,1)S(1)}, u32[]{:S(2)}, u32[]{:S(2)}) collective-permute-start(bf16[8,128,128]{2,1,0:T(8,128)(2,1)S(1)} %pad_maximum_fusion.refs_0_), channel_id=1, source_target_pairs={{0,4},{2,6},{4,0},{6,2},{8,12},{10,14},{12,8},{14,10},{16,20},{18,... | collective-permute-start | bytes 786440 | tf_op jit(solution)/shard_map/over_y/ppermute | solution.py:49
  36.3 11.2 %collective-permute-start.1 = (bf16[8,128,128]{2,1,0:T(8,128)(2,1)S(1)}, bf16[8,128,128]{2,1,0:T(8,128)(2,1)S(1)}, u32[]{:S(2)}, u32[]{:S(2)}) collective-permute-start(bf16[8,128,128]{2,1,0:T(8,128)(2,1)S(1)} %pad_maximum_fusion.refs_0_), channel_id=1, source_target_pairs={{0,6},{2,0},{4,2},{6,4},{8,14},{10,8},{12,10},{14,12},{16,22},{18,... | collective-permute-start | bytes 786440 | tf_op jit(solution)/shard_map/over_y/ppermute | solution.py:49
  47.5 30.8 %collective-permute-start.7 = (bf16[16,128,128]{2,1,0:T(8,128)(2,1)S(1)}, bf16[16,128,128]{2,1,0:T(8,128)(2,1)S(1)}, u32[]{:S(2)}, u32[]{:S(2)}) collective-permute-start(bf16[16,128,128]{2,1,0:T(8,128)(2,1)S(1)} %get-tuple-element.30), channel_id=1, source_target_pairs={{0,33},{2,26},{4,45},{6,22},{8,41},{10,34},{12,53},{14,30},{16,49}... | collective-permute-start | bytes 1572872 | tf_op jit(solution)/shard_map/left_shift/ppermute | solution.py:49
  50.5 29.7 %collective-permute-start.10 = (bf16[16,128,128]{2,1,0:T(8,128)(2,1)S(1)}, bf16[16,128,128]{2,1,0:T(8,128)(2,1)S(1)}, u32[]{:S(2)}, u32[]{:S(2)}) collective-permute-start(bf16[16,128,128]{2,1,0:T(8,128)(2,1)S(1)} %get-tuple-element.31.refs_2_), channel_id=1, source_target_pairs={{0,128},{2,130},{4,132},{6,134},{8,136},{10,138},{12,140},{14,142}... | collective-permute-start | bytes 1572872 | tf_op jit(solution)/shard_map/right_over_x/ppermute | solution.py:49
  53.7 29.0 %collective-permute-start.9 = (bf16[16,128,128]{2,1,0:T(8,128)(2,1)S(1)}, bf16[16,128,128]{2,1,0:T(8,128)(2,1)S(1)}, u32[]{:S(2)}, u32[]{:S(2)}) collective-permute-start(bf16[16,128,128]{2,1,0:T(8,128)(2,1)S(1)} %get-tuple-element.31.refs_2_), channel_id=1, source_target_pairs={{0,256},{2,258},{4,260},{6,262},{8,264},{10,266},{12,268},{14,270}... | collective-permute-start | bytes 1572872 | tf_op jit(solution)/shard_map/right_over_x/ppermute | solution.py:49
  58.0 26.6 %collective-permute-start.8 = (bf16[16,128,128]{2,1,0:T(8,128)(2,1)S(1)}, bf16[16,128,128]{2,1,0:T(8,128)(2,1)S(1)}, u32[]{:S(2)}, u32[]{:S(2)}) collective-permute-start(bf16[16,128,128]{2,1,0:T(8,128)(2,1)S(1)} %get-tuple-element.31.refs_2_), channel_id=1, source_target_pairs={{0,384},{2,386},{4,388},{6,390},{8,392},{10,394},{12,396},{14,398}... | collective-permute-start | bytes 1572872 | tf_op jit(solution)/shard_map/right_over_x/ppermute | solution.py:49
  61.1 26.0 %collective-permute-start.6 = (bf16[16,128,128]{2,1,0:T(8,128)(2,1)S(1)}, bf16[16,128,128]{2,1,0:T(8,128)(2,1)S(1)}, u32[]{:S(2)}, u32[]{:S(2)}) collective-permute-start(bf16[16,128,128]{2,1,0:T(8,128)(2,1)S(1)} %get-tuple-element.30), channel_id=1, source_target_pairs={{0,0},{2,59},{4,12},{6,55},{8,8},{10,2},{12,20},{14,63},{16,16},{1... | collective-permute-start | bytes 1572872 | tf_op jit(solution)/shard_map/left_shift/ppermute | solution.py:49
  78.3 8.7 %collective-permute-start.11 = (bf16[16,128,128]{2,1,0:T(8,128)(2,1)S(1)}, bf16[16,128,128]{2,1,0:T(8,128)(2,1)S(1)}, u32[]{:S(2)}, u32[]{:S(2)}) collective-permute-start(bf16[16,128,128]{2,1,0:T(8,128)(2,1)S(1)} %get-tuple-element.31.refs_2_), channel_id=1, source_target_pairs={{0,64},{2,66},{4,68},{6,70},{8,72},{10,74},{12,76},{14,78},{16,80}... | collective-permute-start | bytes 1572872 | tf_op jit(solution)/shard_map/right_core/ppermute | solution.py:49
  80.3 6.8 %collective-permute-start.14 = (bf16[16,128,128]{2,1,0:T(8,128)(2,1)S(1)}, bf16[16,128,128]{2,1,0:T(8,128)(2,1)S(1)}, u32[]{:S(2)}, u32[]{:S(2)}) collective-permute-start(bf16[16,128,128]{2,1,0:T(8,128)(2,1)S(1)} %collective-permute-done.10.refs_5_), channel_id=1, source_target_pairs={{0,64},{2,66},{4,68},{6,70},{8,72},{10,74},{12,76},{14,78},{16,80}... | collective-permute-start | bytes 1572872 | tf_op jit(solution)/shard_map/right_core/ppermute | solution.py:49
  82.7 4.4 %collective-permute-start.13 = (bf16[16,128,128]{2,1,0:T(8,128)(2,1)S(1)}, bf16[16,128,128]{2,1,0:T(8,128)(2,1)S(1)}, u32[]{:S(2)}, u32[]{:S(2)}) collective-permute-start(bf16[16,128,128]{2,1,0:T(8,128)(2,1)S(1)} %collective-permute-done.9.refs_4_), channel_id=1, source_target_pairs={{0,64},{2,66},{4,68},{6,70},{8,72},{10,74},{12,76},{14,78},{16,80}... | collective-permute-start | bytes 1572872 | tf_op jit(solution)/shard_map/right_core/ppermute | solution.py:49
  84.6 3.9 %collective-permute-start.12 = (bf16[16,128,128]{2,1,0:T(8,128)(2,1)S(1)}, bf16[16,128,128]{2,1,0:T(8,128)(2,1)S(1)}, u32[]{:S(2)}, u32[]{:S(2)}) collective-permute-start(bf16[16,128,128]{2,1,0:T(8,128)(2,1)S(1)} %collective-permute-done.8.refs_3_), channel_id=1, source_target_pairs={{0,64},{2,66},{4,68},{6,70},{8,72},{10,74},{12,76},{14,78},{16,80}... | collective-permute-start | bytes 1572872 | tf_op jit(solution)/shard_map/right_core/ppermute | solution.py:49
  97.0 1.3 copy-start.1
  98.3 37.8 %all-to-all-start = ((bf16[32,2,128,128]{3,2,1,0:T(8,128)(2,1)}), bf16[32,2,128,128]{3,2,1,0:T(8,128)(2,1)S(1)}, u32[]{:S(2)}, u32[]{:S(2)}) async-start(bf16[32,2,128,128]{3,2,1,0:T(8,128)(2,1)} %copy-done.1), calls=%async_computation | async-start | bytes 4194304 | tf_op jit(solution)/shard_map/first_out/all_to_all | solution.py:273
  103.1 18.1 %collective-permute-start.15 = (bf16[8,128,128]{2,1,0:T(8,128)(2,1)S(1)}, bf16[8,128,128]{2,1,0:T(8,128)(2,1)S(1)}, u32[]{:S(2)}, u32[]{:S(2)}) collective-permute-start(bf16[8,128,128]{2,1,0:T(8,128)(2,1)S(1)} %get-tuple-element.35), channel_id=1, source_target_pairs={{0,32},{2,43},{4,28},{6,55},{8,40},{10,51},{12,36},{14,63},{16,48}... | collective-permute-start | bytes 786440 | tf_op jit(solution)/shard_map/second_shift/ppermute | solution.py:49
  110.5 10.8 %collective-permute-start.16 = (bf16[8,128,128]{2,1,0:T(8,128)(2,1)S(1)}, bf16[8,128,128]{2,1,0:T(8,128)(2,1)S(1)}, u32[]{:S(2)}, u32[]{:S(2)}) collective-permute-start(bf16[8,128,128]{2,1,0:T(8,128)(2,1)S(1)} %get-tuple-element.36), channel_id=1, source_target_pairs={{0,0},{2,10},{4,61},{6,22},{8,8},{10,18},{12,4},{14,30},{16,16},{1... | collective-permute-start | bytes 786440 | tf_op jit(solution)/shard_map/second_shift/ppermute | solution.py:49
  123.3 15.0 %collective-permute-start.17 = (bf16[8,128,128]{2,1,0:T(8,128)(2,1)}, bf16[8,128,128]{2,1,0:T(8,128)(2,1)S(1)}, u32[]{:S(2)}, u32[]{:S(2)}) collective-permute-start(bf16[8,128,128]{2,1,0:T(8,128)(2,1)} %get-tuple-element.38), channel_id=1, source_target_pairs={{0,2},{2,4},{4,6},{6,0},{8,10},{10,12},{12,14},{14,8},{16,18},{18,... | collective-permute-start | bytes 786440 | tf_op jit(solution)/shard_map/second_over_y/ppermute | solution.py:49
  128.2 13.1 %collective-permute-start.18 = (bf16[8,128,128]{2,1,0:T(8,128)(2,1)}, bf16[8,128,128]{2,1,0:T(8,128)(2,1)S(1)}, u32[]{:S(2)}, u32[]{:S(2)}) collective-permute-start(bf16[8,128,128]{2,1,0:T(8,128)(2,1)} %get-tuple-element.39), channel_id=1, source_target_pairs={{0,4},{2,6},{4,0},{6,2},{8,12},{10,14},{12,8},{14,10},{16,20},{18,... | collective-permute-start | bytes 786440 | tf_op jit(solution)/shard_map/second_over_y/ppermute | solution.py:49
  132.4 11.3 %collective-permute-start.19 = (bf16[8,128,128]{2,1,0:T(8,128)(2,1)S(1)}, bf16[8,128,128]{2,1,0:T(8,128)(2,1)S(1)}, u32[]{:S(2)}, u32[]{:S(2)}) collective-permute-start(bf16[8,128,128]{2,1,0:T(8,128)(2,1)S(1)} %get-tuple-element.40), channel_id=1, source_target_pairs={{0,6},{2,0},{4,2},{6,4},{8,14},{10,8},{12,10},{14,12},{16,22},{18,... | collective-permute-start | bytes 786440 | tf_op jit(solution)/shard_map/second_over_y/ppermute | solution.py:49
